TPU v7x, 256 devices: a whole 4x4x8 slice. The times are simulated.
256 devices in a mesh: dp: 8 (over y, core), seq: 32 (over z, x).
Axes of the slice: x: 4, y: 4, z: 8, core: 2. Of those that a mesh axis runs over, the one named last changes fastest.
Arguments:
- glu_out: bfloat16 [8, 4096, 1536], P('dp', 'seq'), may hold values from -8 to 8
- conv_weight: float32 [32, 1536], replicated, may hold values from -1 to 1
- bn_gain: float32 [16, 1536], replicated, may hold values from 0.25 to 1.75
- bn_bias: float32 [16, 1536], replicated, may hold values from -3 to 3
- w_out: bfloat16 [1536, 1536], P(('dp', 'seq')), may hold values from -0.15625 to 0.15625
- cotangent: bfloat16 [8, 4096, 1536], P('dp', 'seq'), may hold values from -8 to 8
- language: int32 [8], P('dp'), may hold values from 0 to 15
- length: int32 [8], P('dp'), may hold values from 256 to 4096, as said below
Outputs:
- block_out: bfloat16 [8, 4096, 1536], P('dp', 'seq')
- weight_grad: float32 [1536, 1536], P(('dp', 'seq'))
- input_grad: bfloat16 [8, 4096, 1536], P('dp', 'seq')
Inputs may be any that keep to these rules, and one draw needn't show every extreme that they name: Each length is a multiple of 256; at least one utterance is valid over all 4096 frames.
All inputs are finite; a program needn't handle non-finite values.
Results may differ from a plain program's by a relative error of at most 0.0095.
Values may be sent and summed in bfloat16 or wider, within the bound.
No kernel may reach another device: no remote copies, remote signals or barrier semaphores. Data moves between devices by JAX's collectives and lax.ppermute only.
A program may use at most 64 MiB of HBM per device.

v0:
```python
import jax
import jax.numpy as jnp
from jax import lax
from jax.sharding import PartitionSpec as P

LANGS = 16


epsilon = 1e-05


def with_halo(array, sides, width):
    for axis, dim in sides:
        size, length = (lax.axis_size(axis), array.shape[dim])
        up = [(i, (i + 1) % size) for i in range(size - 1)]
        down = [(j, i) for i, j in up]
        last = lax.slice_in_dim(array, length - width, length, axis=dim)
        first = lax.slice_in_dim(array, 0, width, axis=dim)
        before = lax.ppermute(last, axis, up)
        after = lax.ppermute(first, axis, down)
        array = jnp.concatenate([before, array, after], axis=dim)
    return array


def depthwise(padded, taps, frames):
    running = jnp.zeros((padded.shape[0], frames, padded.shape[2]), jnp.float32)
    for offset in range(taps.shape[0]):
        running = running + padded[:, offset : offset + frames].astype(jnp.float32) * taps[offset]
    return running


def with_rim(values, half_width):
    return with_halo(values, (("seq", 1),), half_width)


def per_language(one_hot, values_table):
    return jnp.dot(one_hot.T, values_table, precision=lax.Precision.HIGHEST)


def per_utterance(one_hot, values_table):
    return jnp.dot(one_hot, values_table, precision=lax.Precision.HIGHEST)[:, None, :]


def on_device(glu_out, conv_weight, bn_gain, bn_bias, w_out, cotangent, language, length):
    utterances, frames, channels = glu_out.shape
    kernel = conv_weight.shape[0]
    half_width = kernel // 2
    position = lax.axis_index("seq") * frames + lax.iota(jnp.int32, frames)
    valid = (position[None, :] < length[:, None]).astype(jnp.float32)[:, :, None]
    one_hot = (language[:, None] == lax.iota(jnp.int32, LANGS)[None, :]).astype(jnp.float32)
    masked = glu_out * valid.astype(jnp.bfloat16)
    extended = with_rim(masked, half_width)
    convolved = depthwise(extended[:, : frames + kernel - 1], conv_weight, frames)
    counts = per_language(one_hot, jnp.sum(valid, axis=(1, 2)))
    local_sum = per_language(one_hot, jnp.sum(convolved * valid, axis=1))
    total_sum, total_count = lax.psum((local_sum, counts), ("dp", "seq"))
    denominator = jnp.maximum(total_count, 1.0)[:, None]
    average = total_sum / denominator
    average_utt = per_utterance(one_hot, average)
    centred = (convolved - average_utt) * valid
    local_spread = per_language(one_hot, jnp.sum(centred * centred, axis=1))
    variance = lax.psum(local_spread, ("dp", "seq")) / denominator
    inverse_utt = per_utterance(one_hot, lax.rsqrt(variance + epsilon))
    gain_utt = per_utterance(one_hot, bn_gain)
    bias_utt = per_utterance(one_hot, bn_bias)
    normed = (convolved - average_utt) * inverse_utt
    pre_act = normed * gain_utt + bias_utt
    sigmoid_act = jax.nn.sigmoid(pre_act)
    active = (pre_act * sigmoid_act * valid).astype(jnp.bfloat16)
    full_weight = lax.all_gather(w_out, ("dp", "seq"), axis=0, tiled=True)
    flat_active = active.reshape(utterances * frames, channels)
    flat_grad = cotangent.reshape(utterances * frames, channels)
    output = jnp.dot(flat_active, full_weight, preferred_element_type=jnp.float32)
    output = output.astype(jnp.bfloat16).reshape(utterances, frames, channels)
    back_proj = lax.dot_general(
        flat_grad, full_weight, (((1,), (1,)), ((), ())), preferred_element_type=jnp.float32
    )
    back_proj = back_proj.reshape(utterances, frames, channels)
    grad_pre = back_proj * valid * sigmoid_act * (1.0 + pre_act * (1.0 - sigmoid_act))
    grad_normed = grad_pre * gain_utt
    first_sum, second_sum = lax.psum(
        (
            per_language(one_hot, jnp.sum(grad_normed, axis=1)),
            per_language(one_hot, jnp.sum(grad_normed * normed, axis=1)),
        ),
        ("dp", "seq"),
    )
    shift_term = per_utterance(one_hot, first_sum / denominator)
    scale_term = per_utterance(one_hot, second_sum / denominator)
    grad_conv = (valid * inverse_utt * (grad_normed - shift_term - normed * scale_term)).astype(
        jnp.bfloat16
    )
    rim_grad = with_rim(grad_conv, half_width)
    input_grad = (depthwise(rim_grad[:, 1:], conv_weight[::-1], frames) * valid).astype(
        jnp.bfloat16
    )
    weight_grad = lax.psum_scatter(
        lax.dot_general(
            flat_active, flat_grad, (((0,), (0,)), ((), ())), preferred_element_type=jnp.float32
        ),
        ("dp", "seq"),
        scatter_dimension=0,
        tiled=True,
    )
    return (output, weight_grad, input_grad)


def solution(mesh):
    placed = (
        P("dp", "seq", None),
        P(),
        P(),
        P(),
        P(("dp", "seq"), None),
        P("dp", "seq", None),
        P("dp"),
        P("dp"),
    )
    return jax.shard_map(
        on_device,
        mesh=mesh,
        in_specs=placed,
        out_specs=(P("dp", "seq", None), P(("dp", "seq"), None), P("dp", "seq", None)),
        check_vma=False,
    )
```

profile of v0, /device:TPU:16, one launch (start us, length us, event | category | flops | bytes accessed | tf_op | source)
XLA Modules:
  0.0 2191.8 jit_solution(3120779394419196398)
XLA Ops:
  9.7 3.4 collective-permute-start
  19.1 80.1 %psum.36 = f32[16]{0:T(128)S(1)} all-reduce(f32[16]{0:T(128)S(1)} %fusion.86), channel_id=1, replica_groups=mesh['dp'=8,'seq'=32] {'dp','seq'}, use_global_device_ids=true, to_apply=%region_3.0 | all-reduce | flops 16 | bytes 128 | tf_op jit(solution)/shard_map/psum | solution.py:56
  99.1 3.8 multiply_reduce_fusion.2
  103.8 238.7 %all-reduce.7.cloned.1.call-done = f32[16,1536]{1,0:T(8,128)} async-done(((f32[16,1536]{1,0:T(8,128)}), f32[16,1536]{1,0:T(8,128)}) %all-reduce.7.cloned.1.call-update) | async-done | bytes 98320 | tf_op jit(solution)/shard_map/psum | solution.py:56
  345.7 239.7 %all-reduce.9.cloned.1.call-done = f32[16,1536]{1,0:T(8,128)} async-done(((f32[16,1536]{1,0:T(8,128)}), f32[16,1536]{1,0:T(8,128)}) %all-reduce.9.cloned.1.call-update) | async-done | bytes 98320 | tf_op jit(solution)/shard_map/psum | solution.py:62
  586.5 5.2 fusion.65
  591.7 640.5 %fusion = f32[8,1536]{1,0:T(8,128)S(1)} fusion(f32[1536,1536]{1,0:T(8,128)} %fusion.65), kind=kCustom, calls=%all-reduce-scatter | all-reduce-scatter fusion | flops 3145729 | bytes 9486336
  1232.2 1.9 collective-permute-start.66
  1234.1 78.7 %collective-permute-start.65 = (f32[8,1536]{1,0:T(8,128)S(1)}, f32[8,1536]{1,0:T(8,128)S(1)}, u32[]{:S(2)}, u32[]{:S(2)}) collective-permute-start(f32[8,1536]{1,0:T(8,128)S(1)} %fusion), channel_id=1, source_target_pairs={{0,62},{1,63},{2,64},{3,65},{4,66},{5,67},{6,68},{7,69},{8,70},{9,... | collective-permute-start | bytes 147464
  1312.8 1.9 collective-permute-start.64
  1314.8 7.6 collective-permute-start.67
  1322.4 1.9 collective-permute-start.63
  1326.5 1.9 collective-permute-start.61
  1328.4 1.9 collective-permute-start.60
  1330.3 1.9 collective-permute-start.59
  1332.3 1.9 collective-permute-start.58
  1337.0 1.9 collective-permute-start.56
  1345.5 1.9 collective-permute-start.53
  1357.1 2.8 collective-permute-done.53
  1365.2 1.9 collective-permute-start.46
  1367.2 1.9 collective-permute-start.45
  1369.1 1.9 collective-permute-start.44
  1378.3 2.4 collective-permute-done.46
  1382.7 2.8 collective-permute-done.45
  1390.9 1.9 collective-permute-start.38
  1398.6 13.7 collective-permute-start.34
  1412.4 13.1 collective-permute-start.33
  1425.5 13.1 collective-permute-start.32
  1438.7 13.1 collective-permute-start.31
  1451.8 13.1 collective-permute-start.30
  1464.9 13.1 collective-permute-start.29
  1478.1 13.1 collective-permute-start.28
  1491.2 13.1 collective-permute-start.27
  1504.4 13.1 collective-permute-start.26
  1517.5 13.1 collective-permute-start.25
  1530.6 13.1 collective-permute-start.24
  1543.8 13.1 collective-permute-start.23
  1556.9 13.1 collective-permute-start.22
  1570.1 13.1 collective-permute-start.21
  1583.2 13.1 collective-permute-start.20
  1596.4 13.1 collective-permute-start.19
  1609.5 13.1 collective-permute-start.18
  1622.7 13.1 collective-permute-start.17
  1635.8 13.1 collective-permute-start.16
  1649.0 13.1 collective-permute-start.15
  1662.1 13.1 collective-permute-start.14
  1675.3 13.1 collective-permute-start.13
  1688.4 13.1 collective-permute-start.12
  1701.6 13.1 collective-permute-start.11
  1714.7 13.1 collective-permute-start.10
  1727.9 13.1 collective-permute-start.9
  1741.0 13.1 collective-permute-start.8
  1754.2 13.1 collective-permute-start.7
  1767.3 13.1 collective-permute-start.6
  1780.5 13.1 collective-permute-start.5
  1793.6 13.3 collective-permute-start.4
  1807.2 7.8 collective-permute-done.4
  1815.0 97.0 %concatenate.76 = f32[518,1536]{1,0:T(8,128)} concatenate(f32[6,1536]{1,0:T(8,128)S(1)} %collective-permute-done.67, f32[8,1536]{1,0:T(8,128)S(1)} %collective-permute-done.66, f32[8,1536]{1,0:T(8,128)S(1)} %collective-permute-done.65, f32[8,1536]{1,0:T(8,128)S(1)} %collective-permute-done.64, f32[8,1536]{1,0:T(8,128)S(1)} %collective-permute-done.63, ...), dimensions={0} | concatenate | bytes 6365184
  1912.0 8.4 reshape.359
  1920.4 4.1 fusion.95
  1926.8 241.7 %all-reduce.11.cloned.1.call-done = (f32[16,1536]{1,0:T(8,128)}, f32[16,1536]{1,0:T(8,128)}) async-done(((f32[16,1536]{1,0:T(8,128)}, f32[16,1536]{1,0:T(8,128)}), (f32[16,1536]{1,0:T(8,128)}, f32[16,1536]{1,0:T(8,128)})) %all-reduce.11.cloned.1.call-update) | async-done | bytes 196624 | tf_op jit(solution)/shard_map/psum | solution.py:81
  2172.3 4.5 collective-permute-start.2
  2176.8 4.0 fusion.5
  2180.8 4.5 multiply_convert_fusion
  (158 shorter events, 65.2 us)
Async XLA Ops:
  7.2 335.3 %all-reduce.7.cloned.1.call-start = ((), (), s32[]{:S(2)}) async-start(), calls=%async_computation | async-start | bytes 196608 | tf_op jit(solution)/shard_map/psum | solution.py:56
  9.7 89.5 %collective-permute-start = (bf16[1,16,1536]{2,1,0:T(8,128)(2,1)S(1)}, bf16[1,16,1536]{2,1,0:T(8,128)(2,1)S(1)}, u32[]{:S(2)}, u32[]{:S(2)}) collective-permute-start(bf16[1,16,1536]{2,1,0:T(8,128)(2,1)S(1)} %get-tuple-element.45), channel_id=1, source_target_pairs={{0,1},{1,2},{2,3},{3,4},{4,5},{5,6},{6,7},{7,8},{8,9},{9,10},{10,1... | collective-permute-start | bytes 147464 | tf_op jit(solution)/shard_map/ppermute | solution.py:19
  13.1 86.1 %collective-permute-start.1 = (bf16[1,16,1536]{2,1,0:T(8,128)(2,1)S(1)}, bf16[1,16,1536]{2,1,0:T(8,128)(2,1)S(1)}, u32[]{:S(2)}, u32[]{:S(2)}) collective-permute-start(bf16[1,16,1536]{2,1,0:T(8,128)(2,1)S(1)} %get-tuple-element.46), channel_id=1, source_target_pairs={{1,0},{2,1},{3,2},{4,3},{5,4},{6,5},{7,6},{8,7},{9,8},{10,9},{11,1... | collective-permute-start | bytes 147464 | tf_op jit(solution)/shard_map/ppermute | solution.py:20
  103.7 481.6 %all-reduce.9.cloned.1.call-start = ((), (), s32[]{:S(2)}) async-start(), calls=%async_computation.1 | async-start | bytes 196608 | tf_op jit(solution)/shard_map/psum | solution.py:62
  344.5 1567.4 %all-gather.3.cloned.1.call-start = ((), (), s32[]{:S(2)}) async-start(), calls=%async_computation.2 | async-start | bytes 6316032 | tf_op jit(solution)/shard_map/all_gather | solution.py:70
  345.3 1823.2 %all-reduce.11.cloned.1.call-start = ((), (), s32[]{:S(2)}) async-start(), calls=%async_computation.3 | async-start | bytes 393216 | tf_op jit(solution)/shard_map/psum | solution.py:81
  1232.2 94.3 %collective-permute-start.66 = (f32[8,1536]{1,0:T(8,128)S(1)}, f32[8,1536]{1,0:T(8,128)S(1)}, u32[]{:S(2)}, u32[]{:S(2)}) collective-permute-start(f32[8,1536]{1,0:T(8,128)S(1)} %fusion), channel_id=1, source_target_pairs={{0,63},{1,64},{2,65},{3,66},{4,67},{5,68},{6,69},{7,70},{8,71},{9,... | collective-permute-start | bytes 147464
  1234.1 94.3 %collective-permute-start.65 = (f32[8,1536]{1,0:T(8,128)S(1)}, f32[8,1536]{1,0:T(8,128)S(1)}, u32[]{:S(2)}, u32[]{:S(2)}) collective-permute-start(f32[8,1536]{1,0:T(8,128)S(1)} %fusion), channel_id=1, source_target_pairs={{0,62},{1,63},{2,64},{3,65},{4,66},{5,67},{6,68},{7,69},{8,70},{9,... | collective-permute-start | bytes 147464
  1312.8 17.5 collective-permute-start.64
  1328.4 11.6 collective-permute-start.60
  1330.3 13.3 collective-permute-start.59
  1332.3 13.3 collective-permute-start.58
  1335.1 12.6 collective-permute-start.57
  1337.0 13.1 collective-permute-start.56
  1340.0 12.2 collective-permute-start.55
  1343.6 11.6 collective-permute-start.54
  1345.5 14.4 collective-permute-start.53
  1347.7 15.6 collective-permute-start.52
  1350.1 15.1 collective-permute-start.51
  1352.2 15.0 collective-permute-start.50
  1355.2 13.9 collective-permute-start.49
  1359.9 13.0 collective-permute-start.48
  1363.3 13.1 collective-permute-start.47
  1365.2 15.5 collective-permute-start.46
  1367.2 18.3 collective-permute-start.45
  1369.1 19.8 collective-permute-start.44
  1372.9 17.9 collective-permute-start.43
  1376.4 16.4 collective-permute-start.42
  1380.7 14.0 collective-permute-start.41
  1390.9 21.5 collective-permute-start.38
  1392.8 32.7 %collective-permute-start.37 = (f32[8,1536]{1,0:T(8,128)S(1)}, f32[8,1536]{1,0:T(8,128)S(1)}, u32[]{:S(2)}, u32[]{:S(2)}) collective-permute-start(f32[8,1536]{1,0:T(8,128)S(1)} %fusion), channel_id=1, source_target_pairs={{0,34},{1,35},{2,36},{3,37},{4,38},{5,39},{6,40},{7,41},{8,42},{9,... | collective-permute-start | bytes 147464
  1394.7 43.9 %collective-permute-start.36 = (f32[8,1536]{1,0:T(8,128)S(1)}, f32[8,1536]{1,0:T(8,128)S(1)}, u32[]{:S(2)}, u32[]{:S(2)}) collective-permute-start(f32[8,1536]{1,0:T(8,128)S(1)} %fusion), channel_id=1, source_target_pairs={{0,33},{1,34},{2,35},{3,36},{4,37},{5,38},{6,39},{7,40},{8,41},{9,... | collective-permute-start | bytes 147464
  1396.7 55.1 %collective-permute-start.35 = (f32[8,1536]{1,0:T(8,128)S(1)}, f32[8,1536]{1,0:T(8,128)S(1)}, u32[]{:S(2)}, u32[]{:S(2)}) collective-permute-start(f32[8,1536]{1,0:T(8,128)S(1)} %fusion), channel_id=1, source_target_pairs={{0,32},{1,33},{2,34},{3,35},{4,36},{5,37},{6,38},{7,39},{8,40},{9,... | collective-permute-start | bytes 147464
  1398.6 66.3 %collective-permute-start.34 = (f32[8,1536]{1,0:T(8,128)S(1)}, f32[8,1536]{1,0:T(8,128)S(1)}, u32[]{:S(2)}, u32[]{:S(2)}) collective-permute-start(f32[8,1536]{1,0:T(8,128)S(1)} %fusion), channel_id=1, source_target_pairs={{0,31},{1,32},{2,33},{3,34},{4,35},{5,36},{6,37},{7,38},{8,39},{9,... | collective-permute-start | bytes 147464
  1412.4 65.7 %collective-permute-start.33 = (f32[8,1536]{1,0:T(8,128)S(1)}, f32[8,1536]{1,0:T(8,128)S(1)}, u32[]{:S(2)}, u32[]{:S(2)}) collective-permute-start(f32[8,1536]{1,0:T(8,128)S(1)} %fusion), channel_id=1, source_target_pairs={{0,30},{1,31},{2,32},{3,33},{4,34},{5,35},{6,36},{7,37},{8,38},{9,... | collective-permute-start | bytes 147464
  1425.5 65.7 %collective-permute-start.32 = (f32[8,1536]{1,0:T(8,128)S(1)}, f32[8,1536]{1,0:T(8,128)S(1)}, u32[]{:S(2)}, u32[]{:S(2)}) collective-permute-start(f32[8,1536]{1,0:T(8,128)S(1)} %fusion), channel_id=1, source_target_pairs={{0,29},{1,30},{2,31},{3,32},{4,33},{5,34},{6,35},{7,36},{8,37},{9,... | collective-permute-start | bytes 147464
  1438.7 65.7 %collective-permute-start.31 = (f32[8,1536]{1,0:T(8,128)S(1)}, f32[8,1536]{1,0:T(8,128)S(1)}, u32[]{:S(2)}, u32[]{:S(2)}) collective-permute-start(f32[8,1536]{1,0:T(8,128)S(1)} %fusion), channel_id=1, source_target_pairs={{0,28},{1,29},{2,30},{3,31},{4,32},{5,33},{6,34},{7,35},{8,36},{9,... | collective-permute-start | bytes 147464
  1451.8 65.7 %collective-permute-start.30 = (f32[8,1536]{1,0:T(8,128)S(1)}, f32[8,1536]{1,0:T(8,128)S(1)}, u32[]{:S(2)}, u32[]{:S(2)}) collective-permute-start(f32[8,1536]{1,0:T(8,128)S(1)} %fusion), channel_id=1, source_target_pairs={{0,27},{1,28},{2,29},{3,30},{4,31},{5,32},{6,33},{7,34},{8,35},{9,... | collective-permute-start | bytes 147464
  1464.9 65.7 %collective-permute-start.29 = (f32[8,1536]{1,0:T(8,128)S(1)}, f32[8,1536]{1,0:T(8,128)S(1)}, u32[]{:S(2)}, u32[]{:S(2)}) collective-permute-start(f32[8,1536]{1,0:T(8,128)S(1)} %fusion), channel_id=1, source_target_pairs={{0,26},{1,27},{2,28},{3,29},{4,30},{5,31},{6,32},{7,33},{8,34},{9,... | collective-permute-start | bytes 147464
  1478.1 65.7 %collective-permute-start.28 = (f32[8,1536]{1,0:T(8,128)S(1)}, f32[8,1536]{1,0:T(8,128)S(1)}, u32[]{:S(2)}, u32[]{:S(2)}) collective-permute-start(f32[8,1536]{1,0:T(8,128)S(1)} %fusion), channel_id=1, source_target_pairs={{0,25},{1,26},{2,27},{3,28},{4,29},{5,30},{6,31},{7,32},{8,33},{9,... | collective-permute-start | bytes 147464
  1491.2 65.7 %collective-permute-start.27 = (f32[8,1536]{1,0:T(8,128)S(1)}, f32[8,1536]{1,0:T(8,128)S(1)}, u32[]{:S(2)}, u32[]{:S(2)}) collective-permute-start(f32[8,1536]{1,0:T(8,128)S(1)} %fusion), channel_id=1, source_target_pairs={{0,24},{1,25},{2,26},{3,27},{4,28},{5,29},{6,30},{7,31},{8,32},{9,... | collective-permute-start | bytes 147464
  1504.4 65.7 %collective-permute-start.26 = (f32[8,1536]{1,0:T(8,128)S(1)}, f32[8,1536]{1,0:T(8,128)S(1)}, u32[]{:S(2)}, u32[]{:S(2)}) collective-permute-start(f32[8,1536]{1,0:T(8,128)S(1)} %fusion), channel_id=1, source_target_pairs={{0,23},{1,24},{2,25},{3,26},{4,27},{5,28},{6,29},{7,30},{8,31},{9,... | collective-permute-start | bytes 147464
  1517.5 65.7 %collective-permute-start.25 = (f32[8,1536]{1,0:T(8,128)S(1)}, f32[8,1536]{1,0:T(8,128)S(1)}, u32[]{:S(2)}, u32[]{:S(2)}) collective-permute-start(f32[8,1536]{1,0:T(8,128)S(1)} %fusion), channel_id=1, source_target_pairs={{0,22},{1,23},{2,24},{3,25},{4,26},{5,27},{6,28},{7,29},{8,30},{9,... | collective-permute-start | bytes 147464
  1530.6 65.7 %collective-permute-start.24 = (f32[8,1536]{1,0:T(8,128)S(1)}, f32[8,1536]{1,0:T(8,128)S(1)}, u32[]{:S(2)}, u32[]{:S(2)}) collective-permute-start(f32[8,1536]{1,0:T(8,128)S(1)} %fusion), channel_id=1, source_target_pairs={{0,21},{1,22},{2,23},{3,24},{4,25},{5,26},{6,27},{7,28},{8,29},{9,... | collective-permute-start | bytes 147464
  1543.8 65.7 %collective-permute-start.23 = (f32[8,1536]{1,0:T(8,128)S(1)}, f32[8,1536]{1,0:T(8,128)S(1)}, u32[]{:S(2)}, u32[]{:S(2)}) collective-permute-start(f32[8,1536]{1,0:T(8,128)S(1)} %fusion), channel_id=1, source_target_pairs={{0,20},{1,21},{2,22},{3,23},{4,24},{5,25},{6,26},{7,27},{8,28},{9,... | collective-permute-start | bytes 147464
  1556.9 65.7 %collective-permute-start.22 = (f32[8,1536]{1,0:T(8,128)S(1)}, f32[8,1536]{1,0:T(8,128)S(1)}, u32[]{:S(2)}, u32[]{:S(2)}) collective-permute-start(f32[8,1536]{1,0:T(8,128)S(1)} %fusion), channel_id=1, source_target_pairs={{0,19},{1,20},{2,21},{3,22},{4,23},{5,24},{6,25},{7,26},{8,27},{9,... | collective-permute-start | bytes 147464
  1570.1 65.7 %collective-permute-start.21 = (f32[8,1536]{1,0:T(8,128)S(1)}, f32[8,1536]{1,0:T(8,128)S(1)}, u32[]{:S(2)}, u32[]{:S(2)}) collective-permute-start(f32[8,1536]{1,0:T(8,128)S(1)} %fusion), channel_id=1, source_target_pairs={{0,18},{1,19},{2,20},{3,21},{4,22},{5,23},{6,24},{7,25},{8,26},{9,... | collective-permute-start | bytes 147464
  1583.2 65.7 %collective-permute-start.20 = (f32[8,1536]{1,0:T(8,128)S(1)}, f32[8,1536]{1,0:T(8,128)S(1)}, u32[]{:S(2)}, u32[]{:S(2)}) collective-permute-start(f32[8,1536]{1,0:T(8,128)S(1)} %fusion), channel_id=1, source_target_pairs={{0,17},{1,18},{2,19},{3,20},{4,21},{5,22},{6,23},{7,24},{8,25},{9,... | collective-permute-start | bytes 147464
  1596.4 65.7 %collective-permute-start.19 = (f32[8,1536]{1,0:T(8,128)S(1)}, f32[8,1536]{1,0:T(8,128)S(1)}, u32[]{:S(2)}, u32[]{:S(2)}) collective-permute-start(f32[8,1536]{1,0:T(8,128)S(1)} %fusion), channel_id=1, source_target_pairs={{0,16},{1,17},{2,18},{3,19},{4,20},{5,21},{6,22},{7,23},{8,24},{9,... | collective-permute-start | bytes 147464
  1609.5 65.7 %collective-permute-start.18 = (f32[8,1536]{1,0:T(8,128)S(1)}, f32[8,1536]{1,0:T(8,128)S(1)}, u32[]{:S(2)}, u32[]{:S(2)}) collective-permute-start(f32[8,1536]{1,0:T(8,128)S(1)} %fusion), channel_id=1, source_target_pairs={{0,15},{1,16},{2,17},{3,18},{4,19},{5,20},{6,21},{7,22},{8,23},{9,... | collective-permute-start | bytes 147464
  1622.7 65.7 %collective-permute-start.17 = (f32[8,1536]{1,0:T(8,128)S(1)}, f32[8,1536]{1,0:T(8,128)S(1)}, u32[]{:S(2)}, u32[]{:S(2)}) collective-permute-start(f32[8,1536]{1,0:T(8,128)S(1)} %fusion), channel_id=1, source_target_pairs={{0,14},{1,15},{2,16},{3,17},{4,18},{5,19},{6,20},{7,21},{8,22},{9,... | collective-permute-start | bytes 147464
  1635.8 65.7 %collective-permute-start.16 = (f32[8,1536]{1,0:T(8,128)S(1)}, f32[8,1536]{1,0:T(8,128)S(1)}, u32[]{:S(2)}, u32[]{:S(2)}) collective-permute-start(f32[8,1536]{1,0:T(8,128)S(1)} %fusion), channel_id=1, source_target_pairs={{0,13},{1,14},{2,15},{3,16},{4,17},{5,18},{6,19},{7,20},{8,21},{9,... | collective-permute-start | bytes 147464
  1649.0 65.7 %collective-permute-start.15 = (f32[8,1536]{1,0:T(8,128)S(1)}, f32[8,1536]{1,0:T(8,128)S(1)}, u32[]{:S(2)}, u32[]{:S(2)}) collective-permute-start(f32[8,1536]{1,0:T(8,128)S(1)} %fusion), channel_id=1, source_target_pairs={{0,12},{1,13},{2,14},{3,15},{4,16},{5,17},{6,18},{7,19},{8,20},{9,... | collective-permute-start | bytes 147464
  1662.1 65.7 %collective-permute-start.14 = (f32[8,1536]{1,0:T(8,128)S(1)}, f32[8,1536]{1,0:T(8,128)S(1)}, u32[]{:S(2)}, u32[]{:S(2)}) collective-permute-start(f32[8,1536]{1,0:T(8,128)S(1)} %fusion), channel_id=1, source_target_pairs={{0,11},{1,12},{2,13},{3,14},{4,15},{5,16},{6,17},{7,18},{8,19},{9,... | collective-permute-start | bytes 147464
  1675.3 65.7 %collective-permute-start.13 = (f32[8,1536]{1,0:T(8,128)S(1)}, f32[8,1536]{1,0:T(8,128)S(1)}, u32[]{:S(2)}, u32[]{:S(2)}) collective-permute-start(f32[8,1536]{1,0:T(8,128)S(1)} %fusion), channel_id=1, source_target_pairs={{0,10},{1,11},{2,12},{3,13},{4,14},{5,15},{6,16},{7,17},{8,18},{9,... | collective-permute-start | bytes 147464
  1688.4 65.7 %collective-permute-start.12 = (f32[8,1536]{1,0:T(8,128)S(1)}, f32[8,1536]{1,0:T(8,128)S(1)}, u32[]{:S(2)}, u32[]{:S(2)}) collective-permute-start(f32[8,1536]{1,0:T(8,128)S(1)} %fusion), channel_id=1, source_target_pairs={{0,9},{1,10},{2,11},{3,12},{4,13},{5,14},{6,15},{7,16},{8,17},{9,1... | collective-permute-start | bytes 147464
  1701.6 65.7 %collective-permute-start.11 = (f32[8,1536]{1,0:T(8,128)S(1)}, f32[8,1536]{1,0:T(8,128)S(1)}, u32[]{:S(2)}, u32[]{:S(2)}) collective-permute-start(f32[8,1536]{1,0:T(8,128)S(1)} %fusion), channel_id=1, source_target_pairs={{0,8},{1,9},{2,10},{3,11},{4,12},{5,13},{6,14},{7,15},{8,16},{9,17... | collective-permute-start | bytes 147464
  1714.7 65.7 %collective-permute-start.10 = (f32[8,1536]{1,0:T(8,128)S(1)}, f32[8,1536]{1,0:T(8,128)S(1)}, u32[]{:S(2)}, u32[]{:S(2)}) collective-permute-start(f32[8,1536]{1,0:T(8,128)S(1)} %fusion), channel_id=1, source_target_pairs={{0,7},{1,8},{2,9},{3,10},{4,11},{5,12},{6,13},{7,14},{8,15},{9,16}... | collective-permute-start | bytes 147464
  1727.9 65.7 %collective-permute-start.9 = (f32[8,1536]{1,0:T(8,128)S(1)}, f32[8,1536]{1,0:T(8,128)S(1)}, u32[]{:S(2)}, u32[]{:S(2)}) collective-permute-start(f32[8,1536]{1,0:T(8,128)S(1)} %fusion), channel_id=1, source_target_pairs={{0,6},{1,7},{2,8},{3,9},{4,10},{5,11},{6,12},{7,13},{8,14},{9,15},... | collective-permute-start | bytes 147464
  1741.0 66.1 %collective-permute-start.8 = (f32[8,1536]{1,0:T(8,128)S(1)}, f32[8,1536]{1,0:T(8,128)}, u32[]{:S(2)}, u32[]{:S(2)}) collective-permute-start(f32[8,1536]{1,0:T(8,128)S(1)} %fusion), channel_id=1, source_target_pairs={{0,5},{1,6},{2,7},{3,8},{4,9},{5,10},{6,11},{7,12},{8,13},{9,14},{... | collective-permute-start | bytes 147464
  1754.2 53.0 %collective-permute-start.7 = (f32[8,1536]{1,0:T(8,128)S(1)}, f32[8,1536]{1,0:T(8,128)}, u32[]{:S(2)}, u32[]{:S(2)}) collective-permute-start(f32[8,1536]{1,0:T(8,128)S(1)} %fusion), channel_id=1, source_target_pairs={{0,4},{1,5},{2,6},{3,7},{4,8},{5,9},{6,10},{7,11},{8,12},{9,13},{1... | collective-permute-start | bytes 147464
  1767.3 39.8 %collective-permute-start.6 = (f32[8,1536]{1,0:T(8,128)S(1)}, f32[8,1536]{1,0:T(8,128)}, u32[]{:S(2)}, u32[]{:S(2)}) collective-permute-start(f32[8,1536]{1,0:T(8,128)S(1)} %fusion), channel_id=1, source_target_pairs={{0,3},{1,4},{2,5},{3,6},{4,7},{5,8},{6,9},{7,10},{8,11},{9,12},{10... | collective-permute-start | bytes 147464
  1780.5 26.7 %collective-permute-start.5 = (f32[8,1536]{1,0:T(8,128)S(1)}, f32[8,1536]{1,0:T(8,128)}, u32[]{:S(2)}, u32[]{:S(2)}) collective-permute-start(f32[8,1536]{1,0:T(8,128)S(1)} %fusion), channel_id=1, source_target_pairs={{0,2},{1,3},{2,4},{3,5},{4,6},{5,7},{6,8},{7,9},{8,10},{9,11},{10,... | collective-permute-start | bytes 147464
  1793.6 21.4 collective-permute-start.4
  (29 other events, 3575.9 us)
Sparse Core Ops, SparseCore 0:
  103.8 238.5 all-reduce.6
  348.5 236.7 all-reduce.8
  589.2 114.0 all-gather.2
  1925.4 243.0 all-reduce.10
where the time goes:
time: 2200 us; the launch traced here: 2190 us
  waiting for transfers between devices  749 us (34%)
  blocking collectives  721 us (33%)
  starting transfers between devices  564 us (26%)
  local copies, waits for them, and re-layouts  110 us (5%)
    unnamed x1, blocking collectives  640 us
    unnamed x64, starting transfers between devices  553 us
    psum x1, waiting for transfers between devices, on_device(): lax.psum((per_language(one_hot, jnp.sum(grad_normed, axis=1)), per_langua...  242 us
    psum x1, waiting for transfers between devices, on_device(): variance = lax.psum(local_spread, ('dp', 'seq')) / denominator  240 us
    psum x1, waiting for transfers between devices, on_device(): total_sum, total_count = lax.psum((local_sum, counts), ('dp', 'seq'))  239 us
    unnamed x46, local copies, waits for them, and re-layouts  107 us
    psum x1, blocking collectives, on_device(): total_sum, total_count = lax.psum((local_sum, counts), ('dp', 'seq'))  80.1 us
  transfers between devices with their start and end apart: 72, of which 19 were waited for; matrix products, arithmetic and copies ran while one was open for 34% of the time, Pallas kernels for 0%

commit v1 on v0

v1 whole, which is shorter than its diff:
```python
import jax
import jax.numpy as jnp
from jax import lax
from jax.sharding import Mesh, PartitionSpec as P

LANGS = 16
EPSILON = 1e-05
F32 = jnp.float32
BF16 = jnp.bfloat16
AXES = {"y": 4, "c": 2, "z": 8, "x": 4}
STATS = ("c", "z", "y")


def gather_all(block, axes):
    size = 1
    for axis in axes:
        size *= AXES[axis]
    copies = jnp.broadcast_to(block[None], (size,) + block.shape)
    return lax.all_to_all(copies, axes, 0, 0, tiled=True)


def swap_xy(block):
    pairs = [(y * 4 + x, x * 4 + y) for y in range(4) for x in range(4)]
    return lax.ppermute(block, ("y", "x"), pairs)


def along_z(block, width):
    up = [(i, i + 1) for i in range(AXES["z"] - 1)]
    down = [(i + 1, i) for i in range(AXES["z"] - 1)]
    before = lax.ppermute(block[-width:], "z", up)
    after = lax.ppermute(block[:width], "z", down)
    return before, after


def depthwise(padded, taps, frames, start):
    running = jnp.zeros((frames, padded.shape[1]), F32)
    for offset in range(taps.shape[0]):
        running = running + padded[start + offset : start + offset + frames].astype(F32) * taps[offset]
    return running


def pack(rows):
    lanes = 128
    packed = jnp.concatenate([row.reshape(-1, lanes) for row in rows], axis=0)
    return jnp.pad(packed, ((0, 8 - packed.shape[0]), (0, 0)))


def on_device(glu_out, conv_weight, bn_gain, bn_bias, w_out, cotangent, language, length):
    glu, cot = glu_out[0], cotangent[0]
    own_frames, channels = glu.shape
    kernel = conv_weight.shape[0]
    half = kernel // 2
    parts = AXES["x"]
    block = channels // parts
    frames = own_frames * parts
    column = lax.axis_index("x") * block
    z = lax.axis_index("z")
    own_language, own_length = language[0], length[0]
    taps = lax.dynamic_slice_in_dim(conv_weight, column, block, 1)
    gain = lax.dynamic_slice(bn_gain, (own_language, column), (1, block))
    bias = lax.dynamic_slice(bn_bias, (own_language, column), (1, block))

    wide = frames + 2 * half
    position = z * frames - half + lax.iota(jnp.int32, wide)
    valid = ((position >= 0) & (position < own_length)).astype(F32)[:, None]
    valid_own = valid[half : half + frames]

    mine = lax.all_to_all(glu.reshape(own_frames, parts, block).transpose(1, 0, 2), "x", 0, 0, tiled=True)
    mine = mine.reshape(frames, block) * valid_own.astype(BF16)
    before, after = along_z(mine, 2 * half)
    padded = jnp.concatenate([before, mine, after], axis=0)
    convolved = depthwise(padded, taps, wide, 0)

    cot_rows = gather_all(cot, ("x",)).reshape(frames, channels)
    weight = gather_all(swap_xy(w_out), ("z", "y")).reshape(-1, channels)
    weight = gather_all(weight, ("c",)).reshape(block, channels)
    back_own = lax.dot_general(cot_rows, weight, (((1,), (1,)), ((), ())), preferred_element_type=F32)
    back_before, back_after = along_z(back_own, half)
    back_proj = jnp.concatenate([back_before, back_own, back_after], axis=0)

    own = convolved[half : half + frames]
    own_count = jnp.clip(own_length - z * frames, 0, frames).astype(F32)
    own_sum = jnp.sum(own * valid_own, axis=0)
    own_mean = own_sum / jnp.maximum(own_count, 1.0)
    own_spread = jnp.sum(jnp.square((own - own_mean) * valid_own), axis=0)
    facts = jnp.where(
        lax.iota(jnp.int32, 128) == 0, own_language.astype(F32), own_count
    )
    gathered = gather_all(pack([own_mean, own_spread, facts]), STATS)
    gathered = gathered.reshape(-1, 8, 128)
    rows = block // 128
    means = gathered[:, :rows].reshape(-1, block)
    spreads = gathered[:, rows : 2 * rows].reshape(-1, block)
    same = (gathered[:, 2 * rows, :1] == own_language.astype(F32)).astype(F32)
    counts = gathered[:, 2 * rows, 1:2] * same
    denominator = jnp.maximum(jnp.sum(counts), 1.0)
    average = jnp.sum(means * counts, axis=0) / denominator
    variance = jnp.sum(spreads * same + counts * jnp.square(means - average), axis=0) / denominator
    inverse = lax.rsqrt(variance + EPSILON)

    normed = (convolved - average) * inverse
    pre_act = normed * gain + bias
    gate = jax.nn.sigmoid(pre_act)
    active = (pre_act * gate * valid)[half : half + frames].astype(BF16)
    grad_normed = back_proj * valid * gate * (1.0 + pre_act * (1.0 - gate)) * gain
    grad_own = grad_normed[half : half + frames]
    first = jnp.sum(grad_own, axis=0)
    second = jnp.sum(grad_own * normed[half : half + frames], axis=0)
    sums = gather_all(pack([first, second]), STATS).reshape(-1, 8, 128)
    sums = jnp.sum(sums * same[:, :, None], axis=0) / denominator
    first_sum = sums[:rows].reshape(block)
    second_sum = sums[rows : 2 * rows].reshape(block)
    grad_conv = (valid * inverse * (grad_normed - first_sum - normed * second_sum)).astype(BF16)
    input_grad = (depthwise(grad_conv, taps[::-1], frames, 1) * valid_own).astype(BF16)
    input_grad = lax.all_to_all(input_grad.reshape(parts, own_frames, block), "x", 0, 0, tiled=True)
    input_grad = input_grad.reshape(parts, own_frames, block).transpose(1, 0, 2).reshape(own_frames, channels)

    partial = jnp.dot(active, weight, preferred_element_type=F32).astype(BF16)
    partial = lax.all_to_all(partial.reshape(parts, own_frames, channels), "x", 0, 0, tiled=True)
    output = jnp.sum(partial.reshape(parts, own_frames, channels).astype(F32), axis=0).astype(BF16)

    product = lax.dot_general(active, cot_rows, (((0,), (0,)), ((), ())), preferred_element_type=F32)
    product = product.astype(BF16).reshape(2, block // 2, channels)
    product = lax.all_to_all(product, "c", 0, 0, tiled=True).astype(F32)
    product = jnp.sum(product, axis=0).astype(BF16).reshape(32, -1, channels)
    product = lax.all_to_all(product, ("z", "y"), 0, 0, tiled=True).astype(F32)
    weight_grad = swap_xy(jnp.sum(product, axis=0))
    return output[None], weight_grad, input_grad[None]


def solution(mesh):
    fine = Mesh(mesh.devices.reshape(tuple(AXES.values())), tuple(AXES))
    dp, seq = ("y", "c"), ("z", "x")
    placed = (
        P(dp, seq, None),
        P(),
        P(),
        P(),
        P(dp + seq, None),
        P(dp, seq, None),
        P(dp),
        P(dp),
    )
    return jax.shard_map(
        on_device,
        mesh=fine,
        in_specs=placed,
        out_specs=(P(dp, seq, None), P(dp + seq, None), P(dp, seq, None)),
        check_vma=False,
    )
```

time: 2200 us -> 215 us (0.10)
  blocking collectives: 721 us -> 4.81 us
  waiting for transfers between devices: 749 us -> 95 us
  starting transfers between devices: 564 us -> 75 us
  local copies, waits for them, and re-layouts: 110 us -> 13.3 us
    psum x3 -> x0, waiting for transfers between devices: 720 us -> none  [the longest x1 242 us: on_device(): lax.psum((per_language(one_hot, jnp.sum(grad_normed, axis=1)), per_langua...]
    unnamed x1 -> x0, blocking collectives: 640 us -> none
    unnamed x64 -> x0, starting transfers between devices: 553 us -> none
    unnamed x46 -> x13, local copies, waits for them, and re-layouts: 107 us -> 1.39 us
    all_to_all x0 -> x9, waiting for transfers between devices: none -> 90.4 us  [the longest x4 51.6 us: gather_all(): return lax.all_to_all(copies, axes, 0, 0, tiled=True)]
    psum x1 -> x0, blocking collectives: 80.1 us -> none  [on_device(): total_sum, total_count = lax.psum((local_sum, counts), ('dp', 'seq'))]
    all_to_all x0 -> x9, starting transfers between devices: none -> 53.4 us  [the longest x4 30.9 us: gather_all(): return lax.all_to_all(copies, axes, 0, 0, tiled=True)]
    unnamed x68 -> x0, waiting for transfers between devices: 29 us -> none
  transfers between devices with their start and end apart: 72 -> 15, of which waited for: 19 -> 11; matrix products, arithmetic and copies ran while one was open for 34% -> 12% of each run, Pallas kernels for 0% -> 0%
where the time goes in v1:
time: 215 us; the launch traced here: 213 us
  waiting for transfers between devices  95 us (44%)
  starting transfers between devices  75 us (35%)
  other arithmetic  14.3 us (7%)
  local copies, waits for them, and re-layouts  13.3 us (6%)
  matrix products  7.75 us (4%)
  blocking collectives  4.81 us (2%)
  between operations  3 us (1%)
    all_to_all x4, waiting for transfers between devices, gather_all(): return lax.all_to_all(copies, axes, 0, 0, tiled=True)  51.6 us
    all_to_all x4, starting transfers between devices, gather_all(): return lax.all_to_all(copies, axes, 0, 0, tiled=True)  30.9 us
    all_to_all x1, waiting for transfers between devices, on_device(): product = lax.all_to_all(product, ('z', 'y'), 0, 0, tiled=True).astype(F32)  20.2 us
    all_to_all x1, waiting for transfers between devices, on_device(): lax.all_to_all(partial.reshape(parts, own_frames, channels), 'x', 0, 0, t...  11.9 us
    ppermute x2, starting transfers between devices, swap_xy(): return lax.ppermute(block, ('y', 'x'), pairs)  11.7 us
    ppermute x2, starting transfers between devices, along_z(): before = lax.ppermute(block[-width:], 'z', up)  7.39 us
    all_to_all x1, starting transfers between devices, on_device(): product = lax.all_to_all(product, ('z', 'y'), 0, 0, tiled=True).astype(F32)  6.51 us
    all_to_all x1, waiting for transfers between devices, on_device(): lax.all_to_all(input_grad.reshape(parts, own_frames, block), 'x', 0, 0, t...  6.17 us
  transfers between devices with their start and end apart: 15, of which 11 were waited for; matrix products, arithmetic and copies ran while one was open for 12% of the time, Pallas kernels for 0%

profile of v1, /device:TPU:16, one launch (start us, length us, event | category | flops | bytes accessed | tf_op | source)
XLA Modules:
  0.0 213.2 jit_solution(8027545047447092116)
XLA Ops:
  0.6 1.1 reshape_squeeze.3
  1.7 0.8 copy.22
  2.5 4.3 %all-to-all-start = ((bf16[4,128,384]{2,1,0:T(8,128)(2,1)}), bf16[4,128,384]{2,1,0:T(8,128)(2,1)S(1)}, u32[]{:S(2)}, u32[]{:S(2)}) async-start(bf16[4,128,384]{2,1,0:T(8,128)(2,1)} %bitcast.33), calls=%async_computation | async-start | bytes 786432 | tf_op jit(solution)/shard_map/all_to_all | solution.py:68
  6.8 6.1 %collective-permute-start.2 = (bf16[6,1536]{1,0:T(8,128)(2,1)S(1)}, bf16[6,1536]{1,0:T(8,128)(2,1)S(1)}, u32[]{:S(2)}, u32[]{:S(2)}) collective-permute-start(bf16[6,1536]{1,0:T(8,128)(2,1)S(1)} %copy-done.5), channel_id=1, source_target_pairs={{0,0},{1,64},{2,128},{3,192},{64,1},{65,65},{66,129},{67,193},{128... | collective-permute-start | bytes 55304 | tf_op jit(solution)/shard_map/ppermute | solution.py:24
  14.3 0.6 all-to-all-done
  14.9 0.1 bitcast_multiply_fusion
  15.1 3.8 %collective-permute-start = (bf16[32,384]{1,0:T(8,128)(2,1)S(1)}, bf16[32,384]{1,0:T(8,128)(2,1)S(1)}, u32[]{:S(2)}, u32[]{:S(2)}) collective-permute-start(bf16[32,384]{1,0:T(8,128)(2,1)S(1)} %get-tuple-element.44), channel_id=1, source_target_pairs={{0,4},{4,8},{8,12},{12,16},{16,20},{20,24},{24,28},{1,5},{5,9},{9,... | collective-permute-start | bytes 73736 | tf_op jit(solution)/shard_map/ppermute | solution.py:30
  18.9 1.3 collective-permute-start.1
  20.3 1.3 dynamic-slice_reduce_fusion.30
  21.6 1.5 dynamic-slice_reduce_fusion.31
  23.1 0.9 broadcast_in_dim.27
  24.0 13.6 %all-to-all-start.2 = ((bf16[32,6,1536]{2,1,0:T(8,128)(2,1)}), bf16[32,6,1536]{2,1,0:T(8,128)(2,1)S(1)}, u32[]{:S(2)}, u32[]{:S(2)}) async-start(bf16[32,6,1536]{2,1,0:T(8,128)(2,1)} %broadcast_in_dim.27), calls=%async_computation.2 | async-start | bytes 1572864 | tf_op jit(solution)/shard_map/all_to_all | solution.py:19
  37.7 3.5 %multiply_add_fusion.1 = f32[544,384]{1,0:T(8,128)S(1)} fusion(bf16[576,384]{1,0:T(8,128)(2,1)S(1)} %pad_maximum_fusion, bf16[512,384]{1,0:T(8,128)(2,1)S(1)} %bitcast_multiply_fusion, bf16[32,384]{1,0:T(8,128)(2,1)S(1)} %collective-permute-done, f32[384]{0:T(512)S(1)} %get-tuple-element.36, f32[384]{0:T(512)S(1)} %get-tuple-element.6, ...), kind=kLoop, calls=%fused_computation.11 | loop fusion | flops 20471808 | bytes 14254080 | tf_op jit(solution)/shard_map/add | solution.py:38
  41.2 0.1 multiply_reduce_fusion.1
  41.4 0.2 multiply_reduce_fusion
  41.6 16.3 %all-to-all-done.2 = bf16[32,6,1536]{2,1,0:T(8,128)(2,1)S(1)} async-done(((bf16[32,6,1536]{2,1,0:T(8,128)(2,1)}), bf16[32,6,1536]{2,1,0:T(8,128)(2,1)S(1)}, u32[]{:S(2)}, u32[]{:S(2)}) %all-to-all-start.2) | async-done | bytes 589856 | tf_op jit(solution)/shard_map/all_to_all | solution.py:19
  57.9 0.7 broadcast_in_dim.26
  58.6 6.0 %all-to-all-start.1 = ((f32[64,8,128]{2,1,0:T(8,128)}), f32[64,8,128]{2,1,0:T(8,128)S(1)}, u32[]{:S(2)}, u32[]{:S(2)}) async-start(f32[64,8,128]{2,1,0:T(8,128)} %broadcast_in_dim.26), calls=%async_computation.1 | async-start | bytes 524288 | tf_op jit(solution)/shard_map/all_to_all | solution.py:19
  64.6 0.2 broadcast_in_dim.28
  64.8 10.8 %all-to-all-done.1 = f32[64,8,128]{2,1,0:T(8,128)S(1)} async-done(((f32[64,8,128]{2,1,0:T(8,128)}), f32[64,8,128]{2,1,0:T(8,128)S(1)}, u32[]{:S(2)}, u32[]{:S(2)}) %all-to-all-start.1) | async-done | bytes 262176 | tf_op jit(solution)/shard_map/all_to_all | solution.py:19
  75.6 0.1 broadcast_in_dim.29
  75.7 4.8 %all_to_all.50 = bf16[2,192,1536]{2,1,0:T(8,128)(2,1)S(1)} all-to-all(bf16[2,192,1536]{2,1,0:T(8,128)(2,1)S(1)} %broadcast_in_dim.29), channel_id=1, replica_groups=mesh['y'=4,'c'=2,'z'=8,'x'=4] {'c'}, dimensions={0} | all-to-all | bytes 2359296 | tf_op jit(solution)/shard_map/all_to_all | solution.py:19
  80.5 1.4 broadcast_in_dim.58
  81.8 4.3 %all-to-all-start.5 = ((bf16[4,128,1536]{2,1,0:T(8,128)(2,1)}), bf16[4,128,1536]{2,1,0:T(8,128)(2,1)}, u32[]{:S(2)}, u32[]{:S(2)}) async-start(bf16[4,128,1536]{2,1,0:T(8,128)(2,1)} %broadcast_in_dim.58), calls=%async_computation.5 | async-start | bytes 3145728 | tf_op jit(solution)/shard_map/all_to_all | solution.py:19
  86.2 0.8 dynamic-slice_reduce_fusion.32
  87.0 0.6 fusion.8
  87.6 1.0 fusion.13
  89.2 0.1 multiply_reduce_fusion.3
  89.4 0.2 fusion.7
  89.6 18.0 %all-to-all-done.5 = bf16[4,128,1536]{2,1,0:T(8,128)(2,1)} async-done(((bf16[4,128,1536]{2,1,0:T(8,128)(2,1)}), bf16[4,128,1536]{2,1,0:T(8,128)(2,1)}, u32[]{:S(2)}, u32[]{:S(2)}) %all-to-all-start.5) | async-done | bytes 1572896 | tf_op jit(solution)/shard_map/all_to_all | solution.py:19
  107.5 2.4 %fusion.16 = f32[512,384]{1,0:T(8,128)S(1)} fusion(bf16[512,1536]{1,0:T(8,128)(2,1)} %bitcast.12, bf16[384,1536]{1,0:T(8,128)(2,1)S(1)} %bitcast.40), kind=kOutput, calls=%fused_computation.87 | convolution fusion | flops 603979776 | bytes 3538944 | tf_op jit(solution)/shard_map/dot_general | solution.py:77
  110.0 3.6 %collective-permute-start.4 = (f32[16,384]{1,0:T(8,128)S(1)}, f32[16,384]{1,0:T(8,128)S(1)}, u32[]{:S(2)}, u32[]{:S(2)}) collective-permute-start(f32[16,384]{1,0:T(8,128)S(1)} %get-tuple-element.42), channel_id=1, source_target_pairs={{0,4},{4,8},{8,12},{12,16},{16,20},{20,24},{24,28},{1,5},{5,9},{9,... | collective-permute-start | bytes 73736 | tf_op jit(solution)/shard_map/ppermute | solution.py:30
  113.5 1.3 collective-permute-start.5
  114.9 0.2 collective-permute-done.4
  115.0 4.2 %collective-permute-done.5 = f32[16,384]{1,0:T(8,128)S(1)} collective-permute-done((f32[16,384]{1,0:T(8,128)S(1)}, f32[16,384]{1,0:T(8,128)S(1)}, u32[]{:S(2)}, u32[]{:S(2)}) %collective-permute-start.5) | collective-permute-done | bytes 24608 | tf_op jit(solution)/shard_map/ppermute | solution.py:31
  119.3 0.4 fusion.2
  119.7 0.1 slice_reduce_fusion
  119.9 0.7 broadcast_in_dim.59
  120.6 7.0 %all-to-all-start.8 = ((f32[64,8,128]{2,1,0:T(8,128)}), f32[64,8,128]{2,1,0:T(8,128)S(1)}, u32[]{:S(2)}, u32[]{:S(2)}) async-start(f32[64,8,128]{2,1,0:T(8,128)} %broadcast_in_dim.59), calls=%async_computation.8 | async-start | bytes 524288 | tf_op jit(solution)/shard_map/all_to_all | solution.py:19
  127.6 0.2 add_divide_fusion
  127.8 0.2 fusion.5
  128.0 0.7 copy-done.2
  128.8 3.2 %convolution_convert_fusion.1 = bf16[384,1536]{1,0:T(8,128)(2,1)} fusion(bf16[512,384]{1,0:T(8,128)(2,1)S(1)} %fusion.5, bf16[512,1536]{1,0:T(8,128)(2,1)} %bitcast.12), kind=kOutput, calls=%fused_computation.1 | convolution fusion | flops 604569600 | bytes 3145728 | tf_op jit(solution)/shard_map/dot_general | solution.py:122
  132.0 6.6 %all-to-all-done.8 = f32[64,8,128]{2,1,0:T(8,128)S(1)} async-done(((f32[64,8,128]{2,1,0:T(8,128)}), f32[64,8,128]{2,1,0:T(8,128)S(1)}, u32[]{:S(2)}, u32[]{:S(2)}) %all-to-all-start.8) | async-done | bytes 262176 | tf_op jit(solution)/shard_map/all_to_all | solution.py:19
  138.6 4.4 %all-to-all-start.6 = ((bf16[2,192,1536]{2,1,0:T(8,128)(2,1)}), bf16[2,192,1536]{2,1,0:T(8,128)(2,1)}, u32[]{:S(2)}, u32[]{:S(2)}) async-start(bf16[2,192,1536]{2,1,0:T(8,128)(2,1)} %bitcast.43), calls=%async_computation.6 | async-start | bytes 2359296 | tf_op jit(solution)/shard_map/all_to_all | solution.py:124
  143.0 0.1 multiply_reduce_fusion.2
  143.2 0.2 multiply_convert_fusion
  143.4 4.3 %multiply_convert_fusion.1 = bf16[512,384]{1,0:T(8,128)(2,1)} fusion(bf16[544,384]{1,0:T(8,128)(2,1)S(1)} %multiply_convert_fusion, f32[384]{0:T(512)S(1)} %get-tuple-element.5, f32[384]{0:T(512)S(1)} %get-tuple-element.23, f32[384]{0:T(512)S(1)} %get-tuple-element.35, f32[384]{0:T(512)S(1)} %get-tuple-element.34, f32[384]{0:T(512)S(1)} %get-tuple-element.33, ...), kind=kLoop, calls=%fused_computation.17 | loop fusion | flops 19070976 | bytes 13027328 | tf_op jit(solution)/shard_map/convert_element_type | solution.py:114
  147.6 3.6 %all-to-all-start.9 = ((bf16[4,128,384]{2,1,0:T(8,128)(2,1)}), bf16[4,128,384]{2,1,0:T(8,128)(2,1)S(1)}, u32[]{:S(2)}, u32[]{:S(2)}) async-start(bf16[4,128,384]{2,1,0:T(8,128)(2,1)} %bitcast.18), calls=%async_computation.9 | async-start | bytes 786432 | tf_op jit(solution)/shard_map/all_to_all | solution.py:115
  151.3 1.5 reduce_sum.111
  152.8 1.1 reshape.164
  153.9 6.2 %all-to-all-done.9 = bf16[4,128,384]{2,1,0:T(8,128)(2,1)S(1)} async-done(((bf16[4,128,384]{2,1,0:T(8,128)(2,1)}), bf16[4,128,384]{2,1,0:T(8,128)(2,1)S(1)}, u32[]{:S(2)}, u32[]{:S(2)}) %all-to-all-start.9) | async-done | bytes 393248 | tf_op jit(solution)/shard_map/all_to_all | solution.py:115
  160.1 6.5 %all-to-all-start.7 = ((bf16[32,6,1536]{2,1,0:T(8,128)(2,1)}), bf16[32,6,1536]{2,1,0:T(8,128)(2,1)S(1)}, u32[]{:S(2)}, u32[]{:S(2)}) async-start(bf16[32,6,1536]{2,1,0:T(8,128)(2,1)} %reshape.164), calls=%async_computation.7 | async-start | bytes 1572864 | tf_op jit(solution)/shard_map/all_to_all | solution.py:126
  166.6 2.1 convolution_convert_fusion
  168.7 20.2 %all-to-all-done.7 = bf16[32,6,1536]{2,1,0:T(8,128)(2,1)S(1)} async-done(((bf16[32,6,1536]{2,1,0:T(8,128)(2,1)}), bf16[32,6,1536]{2,1,0:T(8,128)(2,1)S(1)}, u32[]{:S(2)}, u32[]{:S(2)}) %all-to-all-start.7) | async-done | bytes 589856 | tf_op jit(solution)/shard_map/all_to_all | solution.py:126
  188.9 3.6 %all-to-all-start.4 = ((bf16[4,128,1536]{2,1,0:T(8,128)(2,1)}), bf16[4,128,1536]{2,1,0:T(8,128)(2,1)S(1)}, u32[]{:S(2)}, u32[]{:S(2)}) async-start(bf16[4,128,1536]{2,1,0:T(8,128)(2,1)} %bitcast.9), calls=%async_computation.4 | async-start | bytes 3145728 | tf_op jit(solution)/shard_map/all_to_all | solution.py:119
  192.5 0.2 convert_reduce_fusion
  192.6 5.6 %collective-permute-start.3 = (f32[6,1536]{1,0:T(8,128)S(1)}, f32[6,1536]{1,0:T(8,128)S(1)}, u32[]{:S(2)}, u32[]{:S(2)}) collective-permute-start(f32[6,1536]{1,0:T(8,128)S(1)} %convert_reduce_fusion), channel_id=1, source_target_pairs={{0,0},{1,64},{2,128},{3,192},{64,1},{65,65},{66,129},{67,193},{128... | collective-permute-start | bytes 110600 | tf_op jit(solution)/shard_map/ppermute | solution.py:24
  198.3 0.3 copy.20
  198.6 0.9 broadcast_in_dim_reshape.2
  199.5 11.9 %all-to-all-done.4 = bf16[4,128,1536]{2,1,0:T(8,128)(2,1)S(1)} async-done(((bf16[4,128,1536]{2,1,0:T(8,128)(2,1)}), bf16[4,128,1536]{2,1,0:T(8,128)(2,1)S(1)}, u32[]{:S(2)}, u32[]{:S(2)}) %all-to-all-start.4) | async-done | bytes 1572896 | tf_op jit(solution)/shard_map/all_to_all | solution.py:119
  211.4 1.1 reduce_sum.110
  212.4 0.1 collective-permute-done.3
  212.6 0.6 copy.26
  (31 shorter events, 0.3 us)
Async XLA Ops:
  0.6 6.2 %copy-start.5 = (bf16[6,1536]{1,0:T(8,128)(2,1)S(1)}, bf16[6,1536]{1,0:T(8,128)(2,1)}, u32[]{:S(2)}) copy-start(bf16[6,1536]{1,0:T(8,128)(2,1)} %param.12) | copy-start | bytes 55300
  2.5 12.4 %all-to-all-start = ((bf16[4,128,384]{2,1,0:T(8,128)(2,1)}), bf16[4,128,384]{2,1,0:T(8,128)(2,1)S(1)}, u32[]{:S(2)}, u32[]{:S(2)}) async-start(bf16[4,128,384]{2,1,0:T(8,128)(2,1)} %bitcast.33), calls=%async_computation | async-start | bytes 786432 | tf_op jit(solution)/shard_map/all_to_all | solution.py:68
  6.8 16.2 %collective-permute-start.2 = (bf16[6,1536]{1,0:T(8,128)(2,1)S(1)}, bf16[6,1536]{1,0:T(8,128)(2,1)S(1)}, u32[]{:S(2)}, u32[]{:S(2)}) collective-permute-start(bf16[6,1536]{1,0:T(8,128)(2,1)S(1)} %copy-done.5), channel_id=1, source_target_pairs={{0,0},{1,64},{2,128},{3,192},{64,1},{65,65},{66,129},{67,193},{128... | collective-permute-start | bytes 55304 | tf_op jit(solution)/shard_map/ppermute | solution.py:24
  15.1 22.6 %collective-permute-start = (bf16[32,384]{1,0:T(8,128)(2,1)S(1)}, bf16[32,384]{1,0:T(8,128)(2,1)S(1)}, u32[]{:S(2)}, u32[]{:S(2)}) collective-permute-start(bf16[32,384]{1,0:T(8,128)(2,1)S(1)} %get-tuple-element.44), channel_id=1, source_target_pairs={{0,4},{4,8},{8,12},{12,16},{16,20},{20,24},{24,28},{1,5},{5,9},{9,... | collective-permute-start | bytes 73736 | tf_op jit(solution)/shard_map/ppermute | solution.py:30
  18.9 18.7 %collective-permute-start.1 = (bf16[32,384]{1,0:T(8,128)(2,1)S(1)}, bf16[32,384]{1,0:T(8,128)(2,1)S(1)}, u32[]{:S(2)}, u32[]{:S(2)}) collective-permute-start(bf16[32,384]{1,0:T(8,128)(2,1)S(1)} %get-tuple-element.45), channel_id=1, source_target_pairs={{4,0},{8,4},{12,8},{16,12},{20,16},{24,20},{28,24},{5,1},{9,5},{13... | collective-permute-start | bytes 73736 | tf_op jit(solution)/shard_map/ppermute | solution.py:31
  24.0 33.9 %all-to-all-start.2 = ((bf16[32,6,1536]{2,1,0:T(8,128)(2,1)}), bf16[32,6,1536]{2,1,0:T(8,128)(2,1)S(1)}, u32[]{:S(2)}, u32[]{:S(2)}) async-start(bf16[32,6,1536]{2,1,0:T(8,128)(2,1)} %broadcast_in_dim.27), calls=%async_computation.2 | async-start | bytes 1572864 | tf_op jit(solution)/shard_map/all_to_all | solution.py:19
  58.6 16.9 %all-to-all-start.1 = ((f32[64,8,128]{2,1,0:T(8,128)}), f32[64,8,128]{2,1,0:T(8,128)S(1)}, u32[]{:S(2)}, u32[]{:S(2)}) async-start(f32[64,8,128]{2,1,0:T(8,128)} %broadcast_in_dim.26), calls=%async_computation.1 | async-start | bytes 524288 | tf_op jit(solution)/shard_map/all_to_all | solution.py:19
  75.7 4.8 %copy-start.4 = (bf16[1,128,1536]{2,1,0:T(8,128)(2,1)S(1)}, bf16[1,128,1536]{2,1,0:T(8,128)(2,1)}, u32[]{:S(2)}) copy-start(bf16[1,128,1536]{2,1,0:T(8,128)(2,1)} %param.13) | copy-start | bytes 1179652
  80.5 27.1 %copy-start = (bf16[2,192,1536]{2,1,0:T(8,128)(2,1)}, bf16[2,192,1536]{2,1,0:T(8,128)(2,1)S(1)}, u32[]{:S(2)}) copy-start(bf16[2,192,1536]{2,1,0:T(8,128)(2,1)S(1)} %all_to_all.50) | copy-start | bytes 3538948
  81.8 25.7 %all-to-all-start.5 = ((bf16[4,128,1536]{2,1,0:T(8,128)(2,1)}), bf16[4,128,1536]{2,1,0:T(8,128)(2,1)}, u32[]{:S(2)}, u32[]{:S(2)}) async-start(bf16[4,128,1536]{2,1,0:T(8,128)(2,1)} %broadcast_in_dim.58), calls=%async_computation.5 | async-start | bytes 3145728 | tf_op jit(solution)/shard_map/all_to_all | solution.py:19
  110.0 5.1 %collective-permute-start.4 = (f32[16,384]{1,0:T(8,128)S(1)}, f32[16,384]{1,0:T(8,128)S(1)}, u32[]{:S(2)}, u32[]{:S(2)}) collective-permute-start(f32[16,384]{1,0:T(8,128)S(1)} %get-tuple-element.42), channel_id=1, source_target_pairs={{0,4},{4,8},{8,12},{12,16},{16,20},{20,24},{24,28},{1,5},{5,9},{9,... | collective-permute-start | bytes 73736 | tf_op jit(solution)/shard_map/ppermute | solution.py:30
  113.5 5.7 %collective-permute-start.5 = (f32[16,384]{1,0:T(8,128)S(1)}, f32[16,384]{1,0:T(8,128)S(1)}, u32[]{:S(2)}, u32[]{:S(2)}) collective-permute-start(f32[16,384]{1,0:T(8,128)S(1)} %get-tuple-element.43), channel_id=1, source_target_pairs={{4,0},{8,4},{12,8},{16,12},{20,16},{24,20},{28,24},{5,1},{9,5},{13... | collective-permute-start | bytes 73736 | tf_op jit(solution)/shard_map/ppermute | solution.py:31
  120.6 18.0 %all-to-all-start.8 = ((f32[64,8,128]{2,1,0:T(8,128)}), f32[64,8,128]{2,1,0:T(8,128)S(1)}, u32[]{:S(2)}, u32[]{:S(2)}) async-start(f32[64,8,128]{2,1,0:T(8,128)} %broadcast_in_dim.59), calls=%async_computation.8 | async-start | bytes 524288 | tf_op jit(solution)/shard_map/all_to_all | solution.py:19
  128.0 0.7 copy-start.2
  138.6 9.1 %all-to-all-start.6 = ((bf16[2,192,1536]{2,1,0:T(8,128)(2,1)}), bf16[2,192,1536]{2,1,0:T(8,128)(2,1)}, u32[]{:S(2)}, u32[]{:S(2)}) async-start(bf16[2,192,1536]{2,1,0:T(8,128)(2,1)} %bitcast.43), calls=%async_computation.6 | async-start | bytes 2359296 | tf_op jit(solution)/shard_map/all_to_all | solution.py:124
  147.6 12.4 %all-to-all-start.9 = ((bf16[4,128,384]{2,1,0:T(8,128)(2,1)}), bf16[4,128,384]{2,1,0:T(8,128)(2,1)S(1)}, u32[]{:S(2)}, u32[]{:S(2)}) async-start(bf16[4,128,384]{2,1,0:T(8,128)(2,1)} %bitcast.18), calls=%async_computation.9 | async-start | bytes 786432 | tf_op jit(solution)/shard_map/all_to_all | solution.py:115
  152.8 13.8 %copy-start.1 = (bf16[2,192,1536]{2,1,0:T(8,128)(2,1)S(1)}, bf16[2,192,1536]{2,1,0:T(8,128)(2,1)}, u32[]{:S(2)}) copy-start(bf16[2,192,1536]{2,1,0:T(8,128)(2,1)} %copy-done) | copy-start | bytes 3538948
  152.8 13.8 %copy-start.3 = (bf16[512,384]{1,0:T(8,128)(2,1)S(1)}, bf16[512,384]{1,0:T(8,128)(2,1)}, u32[]{:S(2)}) copy-start(bf16[512,384]{1,0:T(8,128)(2,1)} %copy-done.2) | copy-start | bytes 1179652
  160.1 28.8 %all-to-all-start.7 = ((bf16[32,6,1536]{2,1,0:T(8,128)(2,1)}), bf16[32,6,1536]{2,1,0:T(8,128)(2,1)S(1)}, u32[]{:S(2)}, u32[]{:S(2)}) async-start(bf16[32,6,1536]{2,1,0:T(8,128)(2,1)} %reshape.164), calls=%async_computation.7 | async-start | bytes 1572864 | tf_op jit(solution)/shard_map/all_to_all | solution.py:126
  188.9 22.4 %all-to-all-start.4 = ((bf16[4,128,1536]{2,1,0:T(8,128)(2,1)}), bf16[4,128,1536]{2,1,0:T(8,128)(2,1)S(1)}, u32[]{:S(2)}, u32[]{:S(2)}) async-start(bf16[4,128,1536]{2,1,0:T(8,128)(2,1)} %bitcast.9), calls=%async_computation.4 | async-start | bytes 3145728 | tf_op jit(solution)/shard_map/all_to_all | solution.py:119
  192.6 19.9 %collective-permute-start.3 = (f32[6,1536]{1,0:T(8,128)S(1)}, f32[6,1536]{1,0:T(8,128)S(1)}, u32[]{:S(2)}, u32[]{:S(2)}) collective-permute-start(f32[6,1536]{1,0:T(8,128)S(1)} %convert_reduce_fusion), channel_id=1, source_target_pairs={{0,0},{1,64},{2,128},{3,192},{64,1},{65,65},{66,129},{67,193},{128... | collective-permute-start | bytes 110600 | tf_op jit(solution)/shard_map/ppermute | solution.py:24

commit v2 on v1

v2 whole, which is shorter than its diff:
```python
import jax
import jax.numpy as jnp
from jax import lax
from jax.experimental import pallas as pl
from jax.experimental.pallas import tpu as pltpu
from jax.sharding import Mesh, PartitionSpec as P

EPSILON = 1e-05
F32 = jnp.float32
BF16 = jnp.bfloat16
AXES = {"y": 4, "c": 2, "z": 8, "x": 4}
STATS = ("c", "z", "y")
MEMBERS = 64
LANES = 128
PARTS = 4
OWN = 128
FRAMES = 512
BLOCK = 384
TILES = BLOCK // LANES
CHANNELS = 1536
TAPS = 32
HALF = 16
WIDE = FRAMES + 2 * HALF
ROWS = 6
SLOT = 8
SHARE = 192
LIMIT = 12 * 1024 * 1024


def call(body, outs, scratch=(), scalars=1):
    def run(*operands):
        specs = [pl.BlockSpec(memory_space=pltpu.SMEM)] * scalars
        specs += [pl.BlockSpec(memory_space=pltpu.VMEM)] * (len(operands) - scalars)
        return pl.pallas_call(
            body,
            out_shape=[jax.ShapeDtypeStruct(shape, kind) for shape, kind in outs],
            in_specs=specs,
            out_specs=[pl.BlockSpec(memory_space=pltpu.VMEM)] * len(outs),
            scratch_shapes=list(scratch),
            compiler_params=pltpu.CompilerParams(vmem_limit_bytes=LIMIT),
            cost_estimate=pl.CostEstimate(flops=1000, bytes_accessed=1000, transcendentals=0),
        )(*operands)

    return run


def dot(a, b, dims):
    return lax.dot_general(a, b, (dims, ((), ())), preferred_element_type=F32)


def at(index, size):
    return pl.ds(pl.multiple_of(index * size, size), size)


def valid_rows(start, count, length):
    position = start + lax.broadcasted_iota(jnp.int32, (count, LANES), 0)
    return (position >= 0) & (position < length)


def filter_rows(source, lane, taps, row, count, offsets):
    total = jnp.zeros((count, LANES), F32)
    for phase in range(8):
        chosen = [o for o in offsets if o % 8 == phase]
        reach = max(chosen) - phase
        window = source[row + phase : row + phase + count + reach, lane]
        for o in chosen:
            total = total + window[o - phase : o - phase + count] * taps[offsets[o]][None, :]
    return total


def conv_body(facts, first, second, third, fourth, before, after, weights, convolved, payload, padded):
    x, z, length, language = facts[0], facts[1], facts[2], facts[3]
    begin = z * FRAMES - TAPS
    for t in range(TILES):
        lane = slice(t * LANES, (t + 1) * LANES)
        for k, piece in enumerate((first, second, third, fourth)):
            j = lax.rem(x - k + PARTS, PARTS)
            keep = valid_rows(z * FRAMES + j * OWN, OWN, length)
            rows = pl.ds(pl.multiple_of(TAPS + j * OWN, TAPS), OWN)
            padded[rows, lane] = jnp.where(keep, piece[:, lane].astype(F32), 0.0)
        padded[0:TAPS, lane] = jnp.where(valid_rows(begin, TAPS, length), before[:, lane].astype(F32), 0.0)
        padded[TAPS + FRAMES :, lane] = jnp.where(
            valid_rows(begin + TAPS + FRAMES, TAPS, length), after[:, lane].astype(F32), 0.0
        )
    step = WIDE // 4
    for t in range(TILES):
        lane = slice(t * LANES, (t + 1) * LANES)
        taps = weights[:, pl.ds(pl.multiple_of(x * BLOCK + t * LANES, LANES), LANES)]

        for row in range(0, WIDE, step):
            convolved[row : row + step, lane] = filter_rows(
                padded, lane, taps, row, step, {k: k for k in range(TAPS)}
            )

    count = jnp.clip(length - z * FRAMES, 0, FRAMES).astype(F32)
    keep = valid_rows(z * FRAMES, FRAMES, length)
    lines = []
    spreads = []
    for t in range(TILES):
        lane = slice(t * LANES, (t + 1) * LANES)
        values = convolved[HALF : HALF + FRAMES, lane]
        mean = jnp.sum(jnp.where(keep, values, 0.0), axis=0, keepdims=True) / jnp.maximum(count, 1.0)
        centred = jnp.where(keep, values - mean, 0.0)
        lines.append(mean)
        spreads.append(jnp.sum(centred * centred, axis=0, keepdims=True))
    ones = jnp.ones((1, LANES), F32)
    message = jnp.concatenate(lines + spreads + [ones * language.astype(F32), ones * count], axis=0)
    payload[...] = jnp.broadcast_to(message[None], (MEMBERS, 8, LANES))


def back_body(facts, first, second, third, fourth, own_half, other_half, weight, back, low, high):
    x, core = facts[0], facts[4]
    weight[at(core, SHARE), :] = own_half[...]
    weight[at(1 - core, SHARE), :] = other_half[...]
    for k, piece in enumerate((first, second, third, fourth)):
        j = lax.rem(x - k + PARTS, PARTS)
        back[at(j, OWN), :] = dot(piece[...], weight[...], ((1,), (1,)))
    low[...] = back[0:HALF, :]
    high[...] = back[FRAMES - HALF :, :]


def combine(gathered, language):
    same = gathered[:, 6, :] == language.astype(F32)
    counts = jnp.where(same, gathered[:, 7, :], 0.0)
    total = jnp.maximum(jnp.sum(counts, axis=0, keepdims=True), 1.0)
    return same, counts, total


def chosen_row(table, index):
    here = lax.broadcasted_iota(jnp.int32, table.shape, 0) == index
    return jnp.sum(jnp.where(here, table, 0.0), axis=0, keepdims=True)


def act_body(facts, gathered, convolved, back, before, after, gains, biases, active, normed, grad, inverses, payload):
    x, z, length, language = facts[0], facts[1], facts[2], facts[3]
    same, counts, total = combine(gathered, language)
    spans = ((0, HALF), (HALF, FRAMES), (HALF + FRAMES, HALF))
    sums = [None] * 8
    sums[6] = sums[7] = jnp.zeros((1, LANES), F32)
    kept = []
    for t in range(TILES):
        lane = slice(t * LANES, (t + 1) * LANES)
        wide_lane = pl.ds(pl.multiple_of(x * BLOCK + t * LANES, LANES), LANES)
        means = gathered[:, t, :]
        average = jnp.sum(means * counts, axis=0, keepdims=True) / total
        spread = jnp.where(same, gathered[:, TILES + t, :], 0.0)
        away = means - average
        variance = jnp.sum(spread + counts * (away * away), axis=0, keepdims=True) / total
        inverse = lax.rsqrt(variance + EPSILON)
        kept.append(inverse)
        gain = chosen_row(gains[:, wide_lane], language)
        bias = chosen_row(biases[:, wide_lane], language)
        for part, (row, size) in enumerate(spans):
            step = min(size, 128)
            first = second = jnp.zeros((1, LANES), F32)
            for at_row in range(0, size, step):
                here = slice(row + at_row, row + at_row + step)
                keep = valid_rows(z * FRAMES - HALF + row + at_row, step, length)
                value = (convolved[here, lane] - average) * inverse
                pre = value * gain + bias
                gate = 1.0 / (1.0 + jnp.exp(-pre))
                source = (before, back, after)[part]
                upstream = source[at_row : at_row + step, lane]
                slope = jnp.where(keep, upstream * gate * (1.0 + pre * (1.0 - gate)), 0.0) * gain
                normed[here, lane] = value
                grad[here, lane] = slope
                if part == 1:
                    active[at_row : at_row + step, lane] = jnp.where(keep, pre * gate, 0.0).astype(BF16)
                    first = first + jnp.sum(slope, axis=0, keepdims=True)
                    second = second + jnp.sum(slope * value, axis=0, keepdims=True)
            if part == 1:
                sums[t], sums[TILES + t] = first, second
    payload[...] = jnp.broadcast_to(jnp.concatenate(sums, axis=0)[None], (MEMBERS, 8, LANES))
    inverses[...] = jnp.concatenate(kept + [sums[6]] * (8 - TILES), axis=0)


def grad_body(facts, gathered, sums, normed, grad, inverses, weights, first, second, third, fourth, rounded, result):
    x, z, length, language = facts[0], facts[1], facts[2], facts[3]
    same, counts, total = combine(gathered, language)
    keep = valid_rows(z * FRAMES - HALF, WIDE, length)
    step = FRAMES // 4
    for t in range(TILES):
        lane = slice(t * LANES, (t + 1) * LANES)
        shift = jnp.sum(jnp.where(same, sums[:, t, :], 0.0), axis=0, keepdims=True) / total
        scale = jnp.sum(jnp.where(same, sums[:, TILES + t, :], 0.0), axis=0, keepdims=True) / total
        inverse = inverses[t : t + 1, :]
        value = inverse * (grad[:, lane] - shift - normed[:, lane] * scale)
        rounded[:, lane] = jnp.where(keep, value, 0.0).astype(BF16).astype(F32)
    for t in range(TILES):
        lane = slice(t * LANES, (t + 1) * LANES)
        taps = weights[:, pl.ds(pl.multiple_of(x * BLOCK + t * LANES, LANES), LANES)]

        for row in range(0, FRAMES, step):
            value = filter_rows(rounded, lane, taps, row, step, {TAPS - k: k for k in range(TAPS)})
            inside = valid_rows(z * FRAMES + row, step, length)
            result[row : row + step, lane] = jnp.where(inside, value, 0.0)

    for k, piece in enumerate((first, second, third, fourth)):
        j = lax.rem(x + k, PARTS)
        piece[...] = result[at(j, OWN), :].astype(BF16)


def lanes_body(facts, first, second, third, fourth, joined):
    x = facts[0]
    for k, piece in enumerate((first, second, third, fourth)):
        j = lax.rem(x - k + PARTS, PARTS)
        joined[:, pl.ds(pl.multiple_of(j * BLOCK, LANES), BLOCK)] = piece[...]


def out_body(facts, active, weight, kept, first, second, third):
    x = facts[0]
    kept[...] = dot(active[at(x, OWN), :], weight[...], ((1,), (0,)))
    for k, piece in enumerate((first, second, third)):
        j = lax.rem(x + k + 1, PARTS)
        piece[...] = dot(active[at(j, OWN), :], weight[...], ((1,), (0,))).astype(BF16)


def product_body(facts, active, first, second, third, fourth, kept, sent, total):
    x, core = facts[0], facts[4]
    for k, piece in enumerate((first, second, third, fourth)):
        j = lax.rem(x - k + PARTS, PARTS)
        part = dot(active[at(j, OWN), :], piece[...], ((0,), (0,)))
        total[...] = part if k == 0 else total[...] + part
    kept[...] = total[at(core, SHARE), :]
    sent[...] = total[at(1 - core, SHARE), :].astype(BF16)


def slots():
    local = lax.broadcasted_iota(jnp.int32, (SHARE, 1), 0)
    slot = local // ROWS * SLOT + lax.rem(local, ROWS)
    return (lax.broadcasted_iota(jnp.int32, (SHARE, SHARE // ROWS * SLOT), 1) == slot).astype(BF16)


def weight_body(rows, half):
    half[...] = dot(slots(), rows[...], ((1,), (0,))).astype(BF16)


def spread_body(kept, other, spread):
    both = (kept[...] + other[...].astype(F32)).astype(BF16)
    spread[...] = dot(slots(), both, ((0,), (0,))).astype(BF16)


def around_x(piece, shift):
    size = AXES["x"]
    return lax.ppermute(piece, "x", [(i, (i + shift) % size) for i in range(size)])


def other_core(block):
    return lax.ppermute(block, "c", [(0, 1), (1, 0)])


def swap_xy(block):
    pairs = [(y * 4 + x, x * 4 + y) for y in range(4) for x in range(4)]
    return lax.ppermute(block, ("y", "x"), pairs)


def wait_for(value, *others):
    return lax.optimization_barrier((value,) + others)[0]


def along_z(low, high):
    up = [(i, i + 1) for i in range(AXES["z"] - 1)]
    down = [(i + 1, i) for i in range(AXES["z"] - 1)]
    return lax.ppermute(high, "z", up), lax.ppermute(low, "z", down)


def exchange(payload, axes):
    return lax.all_to_all(payload, axes, 0, 0, tiled=True)


def on_device(glu_out, conv_weight, bn_gain, bn_bias, w_out, cotangent, language, length):
    glu, cot = glu_out[0], cotangent[0]
    x, y, z, core = (lax.axis_index(axis) for axis in ("x", "y", "z", "c"))
    facts = jnp.stack([x, z, length[0], language[0], core, y]).astype(jnp.int32)

    pieces = [lax.dynamic_slice(glu, (0, lax.rem(x + k, PARTS) * BLOCK), (OWN, BLOCK)) for k in range(PARTS)]
    pieces = [pieces[0]] + [around_x(pieces[k], k) for k in range(1, PARTS)]
    later = wait_for(cot, *pieces)
    cots = [cot] + [around_x(later, k) for k in range(1, PARTS)]
    low = jnp.stack([piece[:TAPS] for piece in pieces])
    high = jnp.stack([piece[OWN - TAPS :] for piece in pieces])
    low = lax.dynamic_index_in_dim(low, x, 0, keepdims=False)
    high = lax.dynamic_index_in_dim(high, lax.rem(x + 1, PARTS), 0, keepdims=False)
    before, after = along_z(low, high)
    convolved, payload = call(
        conv_body,
        [((WIDE, BLOCK), F32), ((MEMBERS, 8, LANES), F32)],
        [pltpu.VMEM((WIDE + 2 * HALF, BLOCK), F32)],
    )(facts, *pieces, before, after, conv_weight)

    slot = jnp.broadcast_to(swap_xy(w_out)[None], (32, ROWS, CHANNELS))
    slot = jnp.pad(slot, ((0, 0), (0, SLOT - ROWS), (0, 0))).reshape(-1, CHANNELS)
    rows = exchange(slot, ("z", "y"))
    (half,) = call(weight_body, [((SHARE, CHANNELS), BF16)], scalars=0)(wait_for(rows, payload))
    gathered = exchange(wait_for(payload, *cots), STATS)
    weight, back, low, high = call(
        back_body,
        [((BLOCK, CHANNELS), BF16), ((FRAMES, BLOCK), F32), ((HALF, BLOCK), F32), ((HALF, BLOCK), F32)],
    )(facts, *cots, half, other_core(half))
    back_before, back_after = along_z(low, high)

    active, normed, grad, inverses, payload = call(
        act_body,
        [
            ((FRAMES, BLOCK), BF16),
            ((WIDE, BLOCK), F32),
            ((WIDE, BLOCK), F32),
            ((8, LANES), F32),
            ((MEMBERS, 8, LANES), F32),
        ],
    )(facts, gathered, convolved, back, back_before, back_after, bn_gain, bn_bias)
    sums = exchange(payload, STATS)

    kept, sent = call(
        product_body,
        [((SHARE, CHANNELS), F32), ((SHARE, CHANNELS), BF16)],
        [pltpu.VMEM((BLOCK, CHANNELS), F32)],
    )(facts, active, *cots)
    (spread,) = call(spread_body, [((32 * SLOT, CHANNELS), BF16)], scalars=0)(kept, other_core(sent))
    spread = exchange(spread, ("z", "y")).reshape(32, SLOT, CHANNELS)
    weight_grad = swap_xy(jnp.sum(spread.astype(F32), axis=0)[:ROWS])

    output, *others = call(
        out_body, [((OWN, CHANNELS), F32)] + [((OWN, CHANNELS), BF16)] * (PARTS - 1)
    )(facts, active, weight)
    for k, piece in enumerate(others):
        output = output + around_x(piece, k + 1).astype(F32)
    output = output.astype(BF16)

    pieces = call(
        grad_body,
        [((OWN, BLOCK), BF16)] * PARTS,
        [pltpu.VMEM((WIDE, BLOCK), F32), pltpu.VMEM((FRAMES, BLOCK), F32)],
    )(facts, gathered, sums, normed, grad, inverses, conv_weight)
    pieces = [pieces[0]] + [around_x(pieces[k], k) for k in range(1, PARTS)]
    (input_grad,) = call(lanes_body, [((OWN, CHANNELS), BF16)])(facts, *pieces)
    return output[None], weight_grad, input_grad[None]


def solution(mesh):
    fine = Mesh(mesh.devices.reshape(tuple(AXES.values())), tuple(AXES))
    dp, seq = ("y", "c"), ("z", "x")
    placed = (
        P(dp, seq, None),
        P(),
        P(),
        P(),
        P(dp + seq, None),
        P(dp, seq, None),
        P(dp),
        P(dp),
    )
    return jax.shard_map(
        on_device,
        mesh=fine,
        in_specs=placed,
        out_specs=(P(dp, seq, None), P(dp + seq, None), P(dp, seq, None)),
        check_vma=False,
    )
```

time: 215 us -> 151 us (0.70)
  waiting for transfers between devices: 95 us -> 37.2 us
  Pallas kernels: 0 us -> 22 us
  other arithmetic: 14.3 us -> 3.38 us
  matrix products: 7.75 us -> 0 us
  blocking collectives: 4.81 us -> 0 us
  local copies, waits for them, and re-layouts: 13.3 us -> 10.3 us
    all_to_all x9 -> x4, waiting for transfers between devices: 90.4 us -> 18.2 us  [exchange(): return lax.all_to_all(payload, axes, 0, 0, tiled=True)]
    pallas_call x0 -> x9, Pallas kernels: none -> 22 us  [run(): pl.pallas_call(body, out_shape=[jax.ShapeDtypeStruct(shape, kind) for sha...]
    ppermute x4 -> x18, starting transfers between devices: 9.98 us -> 27.3 us  [the longest x12 16.5 us: around_x(): lax.ppermute(piece, 'x', [(i, (i + shift) % size) for i in range(size)])]
    all_to_all x9 -> x4, starting transfers between devices: 53.4 us -> 39.2 us  [exchange(): return lax.all_to_all(payload, axes, 0, 0, tiled=True)]
    ppermute x2, waiting for transfers between devices: 0.14 us -> 8.13 us  [swap_xy(): return lax.ppermute(block, ('y', 'x'), pairs)]
    dot_general x3 -> x0, matrix products: 7.75 us -> none  [the longest x1 3.22 us: on_device(): lax.dot_general(active, cot_rows, (((0,), (0,)), ((), ())), preferred_ele...]
    unnamed x13 -> x39, local copies, waits for them, and re-layouts: 1.39 us -> 9.01 us
    ppermute x4 -> x18, waiting for transfers between devices: 4.41 us -> 10.9 us  [the longest x12 7.75 us: around_x(): lax.ppermute(piece, 'x', [(i, (i + shift) % size) for i in range(size)])]
  transfers between devices with their start and end apart: 15 -> 24, of which waited for: 11 -> 11; matrix products, arithmetic and copies ran while one was open for 12% -> 2% of each run, Pallas kernels for 0% -> 12%
where the time goes in v2:
time: 151 us; the launch traced here: 150 us
  starting transfers between devices  74.7 us (49%)
  waiting for transfers between devices  37.2 us (25%)
  Pallas kernels  22 us (15%)
  local copies, waits for them, and re-layouts  10.3 us (7%)
  other arithmetic  3.38 us (2%)
  between operations  2.29 us (2%)
    all_to_all x4, starting transfers between devices, exchange(): return lax.all_to_all(payload, axes, 0, 0, tiled=True)  39.2 us
    pallas_call x9, Pallas kernels, run(): pl.pallas_call(body, out_shape=[jax.ShapeDtypeStruct(shape, kind) for sha...  22 us
    all_to_all x4, waiting for transfers between devices, exchange(): return lax.all_to_all(payload, axes, 0, 0, tiled=True)  18.2 us
    ppermute x12, starting transfers between devices, around_x(): lax.ppermute(piece, 'x', [(i, (i + shift) % size) for i in range(size)])  16.5 us
    ppermute x4, starting transfers between devices, along_z(): return (lax.ppermute(high, 'z', up), lax.ppermute(low, 'z', down))  10.7 us
    unnamed x39, local copies, waits for them, and re-layouts  9.01 us
    ppermute x2, starting transfers between devices, swap_xy(): return lax.ppermute(block, ('y', 'x'), pairs)  8.18 us
    ppermute x2, waiting for transfers between devices, swap_xy(): return lax.ppermute(block, ('y', 'x'), pairs)  8.13 us
  transfers between devices with their start and end apart: 24, of which 11 were waited for; matrix products, arithmetic and copies ran while one was open for 2% of the time, Pallas kernels for 12%

profile of v2, /device:TPU:16, one launch (start us, length us, event | category | flops | bytes accessed | tf_op | source)
XLA Modules:
  0.0 149.8 jit_solution(6994254224862022866)
XLA Ops:
  0.6 4.7 %collective-permute-start.8 = (bf16[6,1536]{1,0:T(8,128)(2,1)}, bf16[6,1536]{1,0:T(8,128)(2,1)S(1)}, u32[]{:S(2)}, u32[]{:S(2)}) collective-permute-start(bf16[6,1536]{1,0:T(8,128)(2,1)} %param.12), channel_id=1, source_target_pairs={{0,0},{1,64},{2,128},{3,192},{64,1},{65,65},{66,129},{67,193},{128... | collective-permute-start | bytes 55304 | tf_op jit(solution)/shard_map/ppermute | solution.py:254
  5.3 5.1 %collective-permute-done.8 = bf16[6,1536]{1,0:T(8,128)(2,1)S(1)} collective-permute-done((bf16[6,1536]{1,0:T(8,128)(2,1)}, bf16[6,1536]{1,0:T(8,128)(2,1)S(1)}, u32[]{:S(2)}, u32[]{:S(2)}) %collective-permute-start.8) | collective-permute-done | bytes 18464 | tf_op jit(solution)/shard_map/ppermute | solution.py:254
  10.5 0.1 broadcast_in_dim.12
  10.5 1.0 pad.4
  11.6 11.7 %all-to-all-start.1 = ((bf16[32,8,1536]{2,1,0:T(8,128)(2,1)}), bf16[32,8,1536]{2,1,0:T(8,128)(2,1)S(1)}, u32[]{:S(2)}, u32[]{:S(2)}) async-start(bf16[32,8,1536]{2,1,0:T(8,128)(2,1)} %pad.4), calls=%async_computation.1 | async-start | bytes 1572864 | tf_op jit(solution)/shard_map/all_to_all | solution.py:268
  23.3 0.0 copy-start.15
  23.3 0.1 dynamic-slice_bitcast_fusion
  23.4 1.2 collective-permute-start.2
  24.6 0.9 collective-permute-start
  25.5 1.4 collective-permute-start.1
  26.9 2.2 %collective-permute-done.2.fourth = bf16[128,384]{1,0:T(8,128)(2,1)S(1)} collective-permute-done((bf16[128,384]{1,0:T(8,128)(2,1)S(1)}, bf16[128,384]{1,0:T(8,128)(2,1)S(1)}, u32[]{:S(2)}, u32[]{:S(2)}) %collective-permute-start.2) | collective-permute-done | bytes 98336 | tf_op jit(solution)/shard_map/ppermute | solution.py:245
  29.0 1.4 collective-permute-done.second
  30.4 1.2 collective-permute-done.1.third
  31.6 2.8 %collective-permute-start.7 = (bf16[128,1536]{1,0:T(8,128)(2,1)S(1)}, bf16[128,1536]{1,0:T(8,128)(2,1)S(1)}, u32[]{:S(2)}, u32[]{:S(2)}) collective-permute-start(bf16[128,1536]{1,0:T(8,128)(2,1)S(1)} %bitcast.36), channel_id=1, source_target_pairs={{0,3},{1,0},{2,1},{3,2},{4,7},{5,4},{6,5},{7,6},{8,11},{9,8},{10,9... | collective-permute-start | bytes 1179656 | tf_op jit(solution)/shard_map/ppermute | solution.py:245
  34.4 0.7 collective-permute-start.6
  35.1 0.2 collective-permute-start.5
  35.4 1.3 collective-permute-start.4
  36.7 4.5 %collective-permute-start.3 = (bf16[32,384]{1,0:T(8,128)(2,1)S(1)}, bf16[32,384]{1,0:T(8,128)(2,1)S(1)}, u32[]{:S(2)}, u32[]{:S(2)}) collective-permute-start(bf16[32,384]{1,0:T(8,128)(2,1)S(1)} %fusion.8), channel_id=1, source_target_pairs={{0,4},{4,8},{8,12},{12,16},{16,20},{20,24},{24,28},{1,5},{5,9},{9,... | collective-permute-start | bytes 73736 | tf_op jit(solution)/shard_map/ppermute | solution.py:264
  42.6 0.1 stack.45.facts
  42.7 0.0 collective-permute-done.4.after
  42.7 0.1 collective-permute-done.3.before
  42.8 5.0 %shard_map.103 = (f32[544,384]{1,0:T(8,128)S(1)}, f32[64,8,128]{2,1,0:T(8,128)}) custom-call(s32[6]{0:T(128)S(1)} %stack.45.facts, bf16[128,384]{1,0:T(8,128)(2,1)S(1)} %get-tuple-element.55.first, bf16[128,384]{1,0:T(8,128)(2,1)S(1)} %collective-permute-done.second, bf16[128,384]{1,0:T(8,128)(2,1)S(1)} %collective-permute-done.1.third, ...), custom_call_target="tpu_custom_call" | custom-call | flops 1000 | bytes 1000 | tf_op jit(solution)/shard_map/pallas_call | solution.py:34
  47.8 0.9 copy-done.5
  48.7 0.3 shard_map.104.own_half
  49.0 0.1 collective-permute-start.9
  49.1 0.0 collective-permute-done.6.third
  49.1 3.0 %collective-permute-done.5.second = bf16[128,1536]{1,0:T(8,128)(2,1)S(1)} collective-permute-done((bf16[128,1536]{1,0:T(8,128)(2,1)S(1)}, bf16[128,1536]{1,0:T(8,128)(2,1)S(1)}, u32[]{:S(2)}, u32[]{:S(2)}) %collective-permute-start.5) | collective-permute-done | bytes 393248 | tf_op jit(solution)/shard_map/ppermute | solution.py:245
  52.1 10.2 %all-to-all-start = ((f32[64,8,128]{2,1,0:T(8,128)}), f32[64,8,128]{2,1,0:T(8,128)S(1)}, u32[]{:S(2)}, u32[]{:S(2)}) async-start(f32[64,8,128]{2,1,0:T(8,128)} %get-tuple-element.29), calls=%async_computation | async-start | bytes 524288 | tf_op jit(solution)/shard_map/all_to_all | solution.py:268
  62.3 0.0 copy-start.16
  62.3 0.0 copy-start.17
  62.3 0.0 collective-permute-done.9.other_half
  62.3 2.7 %shard_map.105 = (bf16[384,1536]{1,0:T(8,128)(2,1)S(1)}, f32[512,384]{1,0:T(8,128)S(1)}, f32[16,384]{1,0:T(8,128)S(1)}, f32[16,384]{1,0:T(8,128)S(1)}) custom-call(s32[6]{0:T(128)S(1)} %stack.45.facts, bf16[128,1536]{1,0:T(8,128)(2,1)S(1)} %bitcast.39, bf16[128,1536]{1,0:T(8,128)(2,1)S(1)} %collective-permute-done.5.second, ...), custom_call_target="tpu_custom_call" | custom-call | flops 1000 | bytes 1000 | tf_op jit(solution)/shard_map/pallas_call | solution.py:34
  65.1 1.1 copy-done.3
  66.1 0.9 copy-done.11
  67.0 3.5 %collective-permute-start.10 = (f32[16,384]{1,0:T(8,128)S(1)}, f32[16,384]{1,0:T(8,128)S(1)}, u32[]{:S(2)}, u32[]{:S(2)}) collective-permute-start(f32[16,384]{1,0:T(8,128)S(1)} %get-tuple-element.33), channel_id=1, source_target_pairs={{0,4},{4,8},{8,12},{12,16},{16,20},{20,24},{24,28},{1,5},{5,9},{9,... | collective-permute-start | bytes 73736 | tf_op jit(solution)/shard_map/ppermute | solution.py:264
  70.6 1.3 collective-permute-start.11
  71.9 1.4 all-to-all-done.gathered
  73.3 3.0 %collective-permute-done.11.after = f32[16,384]{1,0:T(8,128)S(1)} collective-permute-done((f32[16,384]{1,0:T(8,128)S(1)}, f32[16,384]{1,0:T(8,128)S(1)}, u32[]{:S(2)}, u32[]{:S(2)}) %collective-permute-start.11) | collective-permute-done | bytes 24608 | tf_op jit(solution)/shard_map/ppermute | solution.py:264
  76.3 1.1 copy-done.6
  77.4 1.1 copy-done.12
  78.6 2.3 %shard_map.106 = (bf16[512,384]{1,0:T(8,128)(2,1)S(1)}, f32[544,384]{1,0:T(8,128)S(1)}, f32[544,384]{1,0:T(8,128)S(1)}, f32[8,128]{1,0:T(8,128)S(1)}, f32[64,8,128]{2,1,0:T(8,128)}) custom-call(s32[6]{0:T(128)S(1)} %stack.45.facts, f32[64,8,128]{2,1,0:T(8,128)S(1)} %all-to-all-done.gathered, f32[544,384]{1,0:T(8,128)S(1)} %copy-done.6, ...), custom_call_target="tpu_custom_call" | custom-call | flops 1000 | bytes 1000 | tf_op jit(solution)/shard_map/pallas_call | solution.py:34
  80.9 0.9 copy-done.9
  81.7 2.1 %shard_map.108 = (f32[192,1536]{1,0:T(8,128)S(1)}, bf16[192,1536]{1,0:T(8,128)(2,1)S(1)}) custom-call(s32[6]{0:T(128)S(1)} %stack.45.facts, bf16[512,384]{1,0:T(8,128)(2,1)S(1)} %get-tuple-element.35.active, bf16[128,1536]{1,0:T(8,128)(2,1)S(1)} %bitcast.40, bf16[128,1536]{1,0:T(8,128)(2,1)S(1)} %collective-permute-done.5.second, ...), custom_call_target="tpu_custom_call" | custom-call | flops 1000 | bytes 1000 | tf_op jit(solution)/shard_map/pallas_call | solution.py:34
  83.8 1.0 copy-done.1
  84.9 10.6 %all-to-all-start.3 = ((f32[64,8,128]{2,1,0:T(8,128)}), f32[64,8,128]{2,1,0:T(8,128)S(1)}, u32[]{:S(2)}, u32[]{:S(2)}) async-start(f32[64,8,128]{2,1,0:T(8,128)} %get-tuple-element.43), calls=%async_computation.3 | async-start | bytes 524288 | tf_op jit(solution)/shard_map/all_to_all | solution.py:268
  95.5 1.3 copy-done.2
  96.8 1.3 shard_map.109
  98.1 8.3 %all-to-all-done.3.sums = f32[64,8,128]{2,1,0:T(8,128)S(1)} async-done(((f32[64,8,128]{2,1,0:T(8,128)}), f32[64,8,128]{2,1,0:T(8,128)S(1)}, u32[]{:S(2)}, u32[]{:S(2)}) %all-to-all-start.3) | async-done | bytes 262176 | tf_op jit(solution)/shard_map/all_to_all | solution.py:268
  106.5 6.7 %all-to-all-start.2 = ((bf16[32,8,1536]{2,1,0:T(8,128)(2,1)}), bf16[32,8,1536]{2,1,0:T(8,128)(2,1)}, u32[]{:S(2)}, u32[]{:S(2)}) async-start(bf16[32,8,1536]{2,1,0:T(8,128)(2,1)} %bitcast.19), calls=%async_computation.2 | async-start | bytes 1572864 | tf_op jit(solution)/shard_map/all_to_all | solution.py:268
  113.2 2.3 %shard_map.107 = (f32[128,1536]{1,0:T(8,128)S(1)}, bf16[128,1536]{1,0:T(8,128)(2,1)}, bf16[128,1536]{1,0:T(8,128)(2,1)}, bf16[128,1536]{1,0:T(8,128)(2,1)}) custom-call(s32[6]{0:T(128)S(1)} %stack.45.facts, bf16[512,384]{1,0:T(8,128)(2,1)S(1)} %get-tuple-element.35.active, bf16[384,1536]{1,0:T(8,128)(2,1)S(1)} %copy-done.4), custom_call_target="tpu_custom_call" | custom-call | flops 1000 | bytes 1000 | tf_op jit(solution)/shard_map/pallas_call | solution.py:34
  115.5 1.5 collective-permute-start.12
  116.9 2.2 %collective-permute-start.13 = (bf16[128,1536]{1,0:T(8,128)(2,1)}, bf16[128,1536]{1,0:T(8,128)(2,1)}, u32[]{:S(2)}, u32[]{:S(2)}) collective-permute-start(bf16[128,1536]{1,0:T(8,128)(2,1)} %get-tuple-element.39), channel_id=1, source_target_pairs={{0,2},{1,3},{2,0},{3,1},{4,6},{5,7},{6,4},{7,5},{8,10},{9,11},{10,... | collective-permute-start | bytes 1179656 | tf_op jit(solution)/shard_map/ppermute | solution.py:245
  119.1 0.6 collective-permute-start.14
  119.8 4.7 %shard_map.110 = (bf16[128,384]{1,0:T(8,128)(2,1)S(1)}, bf16[128,384]{1,0:T(8,128)(2,1)S(1)}, bf16[128,384]{1,0:T(8,128)(2,1)S(1)}, bf16[128,384]{1,0:T(8,128)(2,1)S(1)}) custom-call(s32[6]{0:T(128)S(1)} %stack.45.facts, f32[64,8,128]{2,1,0:T(8,128)S(1)} %all-to-all-done.gathered, f32[64,8,128]{2,1,0:T(8,128)S(1)} %all-to-all-done.3.sums, ...), custom_call_target="tpu_custom_call" | custom-call | flops 1000 | bytes 1000 | tf_op jit(solution)/shard_map/pallas_call | solution.py:34
  124.4 1.5 collective-permute-start.17
  125.9 1.4 collective-permute-start.18
  127.3 8.5 %all-to-all-done.2 = bf16[32,8,1536]{2,1,0:T(8,128)(2,1)} async-done(((bf16[32,8,1536]{2,1,0:T(8,128)(2,1)}), bf16[32,8,1536]{2,1,0:T(8,128)(2,1)}, u32[]{:S(2)}, u32[]{:S(2)}) %all-to-all-start.2) | async-done | bytes 786464 | tf_op jit(solution)/shard_map/all_to_all | solution.py:268
  135.8 1.3 convert_reduce_fusion
  137.0 2.3 %collective-permute-start.19 = (bf16[128,384]{1,0:T(8,128)(2,1)S(1)}, bf16[128,384]{1,0:T(8,128)(2,1)S(1)}, u32[]{:S(2)}, u32[]{:S(2)}) collective-permute-start(bf16[128,384]{1,0:T(8,128)(2,1)S(1)} %get-tuple-element.50), channel_id=1, source_target_pairs={{0,3},{1,0},{2,1},{3,2},{4,7},{5,4},{6,5},{7,6},{8,11},{9,8},{10,9... | collective-permute-start | bytes 294920 | tf_op jit(solution)/shard_map/ppermute | solution.py:245
  139.3 3.5 %collective-permute-start.16 = (f32[6,1536]{1,0:T(8,128)S(1)}, f32[6,1536]{1,0:T(8,128)S(1)}, u32[]{:S(2)}, u32[]{:S(2)}) collective-permute-start(f32[6,1536]{1,0:T(8,128)S(1)} %bitcast.42), channel_id=1, source_target_pairs={{0,0},{1,64},{2,128},{3,192},{64,1},{65,65},{66,129},{67,193},{128... | collective-permute-start | bytes 110600 | tf_op jit(solution)/shard_map/ppermute | solution.py:254
  142.8 2.0 %fusion = bf16[1,128,1536]{2,1,0:T(8,128)(2,1)} fusion(bf16[128,1536]{1,0:T(8,128)(2,1)} %collective-permute-done.14, bf16[128,1536]{1,0:T(8,128)(2,1)} %collective-permute-done.13, f32[128,1536]{1,0:T(8,128)S(1)} %copy-done.14, bf16[128,1536]{1,0:T(8,128)(2,1)S(1)} %collective-permute-done.12), kind=kLoop, calls=%fused_computation.2 | loop fusion | flops 1376256 | bytes 2359296 | tf_op jit(solution)/shard_map/broadcast_in_dim | solution.py:337
  144.8 1.3 shard_map.111
  146.2 3.0 %collective-permute-done.16 = f32[6,1536]{1,0:T(8,128)S(1)} collective-permute-done((f32[6,1536]{1,0:T(8,128)S(1)}, f32[6,1536]{1,0:T(8,128)S(1)}, u32[]{:S(2)}, u32[]{:S(2)}) %collective-permute-start.16) | collective-permute-done | bytes 36896 | tf_op jit(solution)/shard_map/ppermute | solution.py:254
  149.2 0.6 copy.14
  (44 shorter events, 0.2 us)
Async XLA Ops:
  0.6 9.8 %collective-permute-start.8 = (bf16[6,1536]{1,0:T(8,128)(2,1)}, bf16[6,1536]{1,0:T(8,128)(2,1)S(1)}, u32[]{:S(2)}, u32[]{:S(2)}) collective-permute-start(bf16[6,1536]{1,0:T(8,128)(2,1)} %param.12), channel_id=1, source_target_pairs={{0,0},{1,64},{2,128},{3,192},{64,1},{65,65},{66,129},{67,193},{128... | collective-permute-start | bytes 55304 | tf_op jit(solution)/shard_map/ppermute | solution.py:254
  11.6 11.8 %copy-start.18 = (bf16[1,128,1536]{2,1,0:T(8,128)(2,1)S(1)}, bf16[1,128,1536]{2,1,0:T(8,128)(2,1)}, u32[]{:S(2)}) copy-start(bf16[1,128,1536]{2,1,0:T(8,128)(2,1)} %param.8) | copy-start | bytes 1179652
  11.6 20.1 %copy-start = (bf16[1,128,1536]{2,1,0:T(8,128)(2,1)S(1)}, bf16[1,128,1536]{2,1,0:T(8,128)(2,1)}, u32[]{:S(2)}) copy-start(bf16[1,128,1536]{2,1,0:T(8,128)(2,1)} %param.13) | copy-start | bytes 1179652
  11.6 37.1 %all-to-all-start.1 = ((bf16[32,8,1536]{2,1,0:T(8,128)(2,1)}), bf16[32,8,1536]{2,1,0:T(8,128)(2,1)S(1)}, u32[]{:S(2)}, u32[]{:S(2)}) async-start(bf16[32,8,1536]{2,1,0:T(8,128)(2,1)} %pad.4), calls=%async_computation.1 | async-start | bytes 1572864 | tf_op jit(solution)/shard_map/all_to_all | solution.py:268
  23.3 19.5 %copy-start.15 = (f32[32,1536]{1,0:T(8,128)S(1)}, f32[32,1536]{1,0:T(8,128)}, u32[]{:S(2)}) copy-start(f32[32,1536]{1,0:T(8,128)} %weights.3) | copy-start | bytes 589828
  23.4 5.6 %collective-permute-start.2 = (bf16[128,384]{1,0:T(8,128)(2,1)S(1)}, bf16[128,384]{1,0:T(8,128)(2,1)S(1)}, u32[]{:S(2)}, u32[]{:S(2)}) collective-permute-start(bf16[128,384]{1,0:T(8,128)(2,1)S(1)} %get-tuple-element.53), channel_id=1, source_target_pairs={{0,3},{1,0},{2,1},{3,2},{4,7},{5,4},{6,5},{7,6},{8,11},{9,8},{10,9... | collective-permute-start | bytes 294920 | tf_op jit(solution)/shard_map/ppermute | solution.py:245
  24.6 5.8 %collective-permute-start = (bf16[128,384]{1,0:T(8,128)(2,1)S(1)}, bf16[128,384]{1,0:T(8,128)(2,1)S(1)}, u32[]{:S(2)}, u32[]{:S(2)}) collective-permute-start(bf16[128,384]{1,0:T(8,128)(2,1)S(1)} %get-tuple-element.54), channel_id=1, source_target_pairs={{0,1},{1,2},{2,3},{3,0},{4,5},{5,6},{6,7},{7,4},{8,9},{9,10},{10,1... | collective-permute-start | bytes 294920 | tf_op jit(solution)/shard_map/ppermute | solution.py:245
  25.5 6.1 %collective-permute-start.1 = (bf16[128,384]{1,0:T(8,128)(2,1)S(1)}, bf16[128,384]{1,0:T(8,128)(2,1)S(1)}, u32[]{:S(2)}, u32[]{:S(2)}) collective-permute-start(bf16[128,384]{1,0:T(8,128)(2,1)S(1)} %get-tuple-element.56), channel_id=1, source_target_pairs={{0,2},{1,3},{2,0},{3,1},{4,6},{5,7},{6,4},{7,5},{8,10},{9,11},{10,... | collective-permute-start | bytes 294920 | tf_op jit(solution)/shard_map/ppermute | solution.py:245
  31.6 17.5 %collective-permute-start.7 = (bf16[128,1536]{1,0:T(8,128)(2,1)S(1)}, bf16[128,1536]{1,0:T(8,128)(2,1)S(1)}, u32[]{:S(2)}, u32[]{:S(2)}) collective-permute-start(bf16[128,1536]{1,0:T(8,128)(2,1)S(1)} %bitcast.36), channel_id=1, source_target_pairs={{0,3},{1,0},{2,1},{3,2},{4,7},{5,4},{6,5},{7,6},{8,11},{9,8},{10,9... | collective-permute-start | bytes 1179656 | tf_op jit(solution)/shard_map/ppermute | solution.py:245
  34.4 14.7 %collective-permute-start.6 = (bf16[128,1536]{1,0:T(8,128)(2,1)S(1)}, bf16[128,1536]{1,0:T(8,128)(2,1)S(1)}, u32[]{:S(2)}, u32[]{:S(2)}) collective-permute-start(bf16[128,1536]{1,0:T(8,128)(2,1)S(1)} %bitcast.37), channel_id=1, source_target_pairs={{0,2},{1,3},{2,0},{3,1},{4,6},{5,7},{6,4},{7,5},{8,10},{9,11},{10,... | collective-permute-start | bytes 1179656 | tf_op jit(solution)/shard_map/ppermute | solution.py:245
  35.1 17.0 %collective-permute-start.5 = (bf16[128,1536]{1,0:T(8,128)(2,1)S(1)}, bf16[128,1536]{1,0:T(8,128)(2,1)S(1)}, u32[]{:S(2)}, u32[]{:S(2)}) collective-permute-start(bf16[128,1536]{1,0:T(8,128)(2,1)S(1)} %bitcast.38), channel_id=1, source_target_pairs={{0,1},{1,2},{2,3},{3,0},{4,5},{5,6},{6,7},{7,4},{8,9},{9,10},{10,1... | collective-permute-start | bytes 1179656 | tf_op jit(solution)/shard_map/ppermute | solution.py:245
  35.4 7.3 %collective-permute-start.4 = (bf16[32,384]{1,0:T(8,128)(2,1)S(1)}, bf16[32,384]{1,0:T(8,128)(2,1)S(1)}, u32[]{:S(2)}, u32[]{:S(2)}) collective-permute-start(bf16[32,384]{1,0:T(8,128)(2,1)S(1)} %fusion.4), channel_id=1, source_target_pairs={{4,0},{8,4},{12,8},{16,12},{20,16},{24,20},{28,24},{5,1},{9,5},{13... | collective-permute-start | bytes 73736 | tf_op jit(solution)/shard_map/ppermute | solution.py:264
  36.7 6.1 %collective-permute-start.3 = (bf16[32,384]{1,0:T(8,128)(2,1)S(1)}, bf16[32,384]{1,0:T(8,128)(2,1)S(1)}, u32[]{:S(2)}, u32[]{:S(2)}) collective-permute-start(bf16[32,384]{1,0:T(8,128)(2,1)S(1)} %fusion.8), channel_id=1, source_target_pairs={{0,4},{4,8},{8,12},{12,16},{16,20},{20,24},{24,28},{1,5},{5,9},{9,... | collective-permute-start | bytes 73736 | tf_op jit(solution)/shard_map/ppermute | solution.py:264
  47.8 0.9 copy-start.5
  49.0 13.3 %collective-permute-start.9 = (bf16[192,1536]{1,0:T(8,128)(2,1)S(1)}, bf16[192,1536]{1,0:T(8,128)(2,1)}, u32[]{:S(2)}, u32[]{:S(2)}) collective-permute-start(bf16[192,1536]{1,0:T(8,128)(2,1)S(1)} %shard_map.104.own_half), channel_id=1, source_target_pairs={{0,32},{32,0},{1,33},{33,1},{2,34},{34,2},{3,35},{35,3},{4,36},{36... | collective-permute-start | bytes 1769480 | tf_op jit(solution)/shard_map/ppermute | solution.py:249
  52.1 21.1 %all-to-all-start = ((f32[64,8,128]{2,1,0:T(8,128)}), f32[64,8,128]{2,1,0:T(8,128)S(1)}, u32[]{:S(2)}, u32[]{:S(2)}) async-start(f32[64,8,128]{2,1,0:T(8,128)} %get-tuple-element.29), calls=%async_computation | async-start | bytes 524288 | tf_op jit(solution)/shard_map/all_to_all | solution.py:268
  62.3 14.0 %copy-start.16 = (f32[16,1536]{1,0:T(8,128)S(1)}, f32[16,1536]{1,0:T(8,128)}, u32[]{:S(2)}) copy-start(f32[16,1536]{1,0:T(8,128)} %gains.1) | copy-start | bytes 294916
  62.3 14.0 %copy-start.17 = (f32[16,1536]{1,0:T(8,128)S(1)}, f32[16,1536]{1,0:T(8,128)}, u32[]{:S(2)}) copy-start(f32[16,1536]{1,0:T(8,128)} %biases.1) | copy-start | bytes 294916
  65.1 1.1 copy-start.3
  66.1 0.9 copy-start.11
  67.0 6.2 %collective-permute-start.10 = (f32[16,384]{1,0:T(8,128)S(1)}, f32[16,384]{1,0:T(8,128)S(1)}, u32[]{:S(2)}, u32[]{:S(2)}) collective-permute-start(f32[16,384]{1,0:T(8,128)S(1)} %get-tuple-element.33), channel_id=1, source_target_pairs={{0,4},{4,8},{8,12},{12,16},{16,20},{20,24},{24,28},{1,5},{5,9},{9,... | collective-permute-start | bytes 73736 | tf_op jit(solution)/shard_map/ppermute | solution.py:264
  70.6 5.7 %collective-permute-start.11 = (f32[16,384]{1,0:T(8,128)S(1)}, f32[16,384]{1,0:T(8,128)S(1)}, u32[]{:S(2)}, u32[]{:S(2)}) collective-permute-start(f32[16,384]{1,0:T(8,128)S(1)} %get-tuple-element.34), channel_id=1, source_target_pairs={{4,0},{8,4},{12,8},{16,12},{20,16},{24,20},{28,24},{5,1},{9,5},{13... | collective-permute-start | bytes 73736 | tf_op jit(solution)/shard_map/ppermute | solution.py:264
  76.3 1.2 copy-start.6
  77.4 1.1 copy-start.12
  80.8 0.9 copy-start.9
  81.7 2.1 %copy-start.7 = (f32[544,384]{1,0:T(8,128)}, f32[544,384]{1,0:T(8,128)S(1)}, u32[]{:S(2)}) copy-start(f32[544,384]{1,0:T(8,128)S(1)} %get-tuple-element.44.normed) | copy-start | bytes 2506756
  83.8 1.0 copy-start.1
  84.9 10.6 %collective-permute-start.15 = (bf16[192,1536]{1,0:T(8,128)(2,1)S(1)}, bf16[192,1536]{1,0:T(8,128)(2,1)S(1)}, u32[]{:S(2)}, u32[]{:S(2)}) collective-permute-start(bf16[192,1536]{1,0:T(8,128)(2,1)S(1)} %get-tuple-element.42), channel_id=1, source_target_pairs={{0,32},{32,0},{1,33},{33,1},{2,34},{34,2},{3,35},{35,3},{4,36},{36... | collective-permute-start | bytes 1769480 | tf_op jit(solution)/shard_map/ppermute | solution.py:249
  84.9 21.6 %all-to-all-start.3 = ((f32[64,8,128]{2,1,0:T(8,128)}), f32[64,8,128]{2,1,0:T(8,128)S(1)}, u32[]{:S(2)}, u32[]{:S(2)}) async-start(f32[64,8,128]{2,1,0:T(8,128)} %get-tuple-element.43), calls=%async_computation.3 | async-start | bytes 524288 | tf_op jit(solution)/shard_map/all_to_all | solution.py:268
  95.5 1.3 copy-start.2
  98.1 15.1 %copy-start.4 = (bf16[384,1536]{1,0:T(8,128)(2,1)S(1)}, bf16[384,1536]{1,0:T(8,128)(2,1)}, u32[]{:S(2)}) copy-start(bf16[384,1536]{1,0:T(8,128)(2,1)} %copy-done.3) | copy-start | bytes 3538948
  106.4 13.3 %copy-start.10 = (f32[544,384]{1,0:T(8,128)S(1)}, f32[544,384]{1,0:T(8,128)}, u32[]{:S(2)}) copy-start(f32[544,384]{1,0:T(8,128)} %copy-done.9) | copy-start | bytes 2506756
  106.5 29.3 %all-to-all-start.2 = ((bf16[32,8,1536]{2,1,0:T(8,128)(2,1)}), bf16[32,8,1536]{2,1,0:T(8,128)(2,1)}, u32[]{:S(2)}, u32[]{:S(2)}) async-start(bf16[32,8,1536]{2,1,0:T(8,128)(2,1)} %bitcast.19), calls=%async_computation.2 | async-start | bytes 1572864 | tf_op jit(solution)/shard_map/all_to_all | solution.py:268
  113.1 6.6 %copy-start.8 = (f32[544,384]{1,0:T(8,128)S(1)}, f32[544,384]{1,0:T(8,128)}, u32[]{:S(2)}) copy-start(f32[544,384]{1,0:T(8,128)} %copy-done.7) | copy-start | bytes 2506756
  115.5 9.0 %copy-start.13 = (f32[128,1536]{1,0:T(8,128)}, f32[128,1536]{1,0:T(8,128)S(1)}, u32[]{:S(2)}) copy-start(f32[128,1536]{1,0:T(8,128)S(1)} %get-tuple-element.37) | copy-start | bytes 2359300
  115.5 21.6 %collective-permute-start.12 = (bf16[128,1536]{1,0:T(8,128)(2,1)}, bf16[128,1536]{1,0:T(8,128)(2,1)S(1)}, u32[]{:S(2)}, u32[]{:S(2)}) collective-permute-start(bf16[128,1536]{1,0:T(8,128)(2,1)} %get-tuple-element.38), channel_id=1, source_target_pairs={{0,1},{1,2},{2,3},{3,0},{4,5},{5,6},{6,7},{7,4},{8,9},{9,10},{10,1... | collective-permute-start | bytes 1179656 | tf_op jit(solution)/shard_map/ppermute | solution.py:245
  116.9 22.4 %collective-permute-start.13 = (bf16[128,1536]{1,0:T(8,128)(2,1)}, bf16[128,1536]{1,0:T(8,128)(2,1)}, u32[]{:S(2)}, u32[]{:S(2)}) collective-permute-start(bf16[128,1536]{1,0:T(8,128)(2,1)} %get-tuple-element.39), channel_id=1, source_target_pairs={{0,2},{1,3},{2,0},{3,1},{4,6},{5,7},{6,4},{7,5},{8,10},{9,11},{10,... | collective-permute-start | bytes 1179656 | tf_op jit(solution)/shard_map/ppermute | solution.py:245
  119.1 23.7 %collective-permute-start.14 = (bf16[128,1536]{1,0:T(8,128)(2,1)}, bf16[128,1536]{1,0:T(8,128)(2,1)}, u32[]{:S(2)}, u32[]{:S(2)}) collective-permute-start(bf16[128,1536]{1,0:T(8,128)(2,1)} %get-tuple-element.40), channel_id=1, source_target_pairs={{0,3},{1,0},{2,1},{3,2},{4,7},{5,4},{6,5},{7,6},{8,11},{9,8},{10,9... | collective-permute-start | bytes 1179656 | tf_op jit(solution)/shard_map/ppermute | solution.py:245
  124.4 18.4 %copy-start.14 = (f32[128,1536]{1,0:T(8,128)S(1)}, f32[128,1536]{1,0:T(8,128)}, u32[]{:S(2)}) copy-start(f32[128,1536]{1,0:T(8,128)} %copy-done.13) | copy-start | bytes 2359300
  124.4 20.4 %collective-permute-start.17 = (bf16[128,384]{1,0:T(8,128)(2,1)S(1)}, bf16[128,384]{1,0:T(8,128)(2,1)S(1)}, u32[]{:S(2)}, u32[]{:S(2)}) collective-permute-start(bf16[128,384]{1,0:T(8,128)(2,1)S(1)} %get-tuple-element.48), channel_id=1, source_target_pairs={{0,1},{1,2},{2,3},{3,0},{4,5},{5,6},{6,7},{7,4},{8,9},{9,10},{10,1... | collective-permute-start | bytes 294920 | tf_op jit(solution)/shard_map/ppermute | solution.py:245
  125.9 18.9 %collective-permute-start.18 = (bf16[128,384]{1,0:T(8,128)(2,1)S(1)}, bf16[128,384]{1,0:T(8,128)(2,1)S(1)}, u32[]{:S(2)}, u32[]{:S(2)}) collective-permute-start(bf16[128,384]{1,0:T(8,128)(2,1)S(1)} %get-tuple-element.49), channel_id=1, source_target_pairs={{0,2},{1,3},{2,0},{3,1},{4,6},{5,7},{6,4},{7,5},{8,10},{9,11},{10,... | collective-permute-start | bytes 294920 | tf_op jit(solution)/shard_map/ppermute | solution.py:245
  137.0 7.8 %collective-permute-start.19 = (bf16[128,384]{1,0:T(8,128)(2,1)S(1)}, bf16[128,384]{1,0:T(8,128)(2,1)S(1)}, u32[]{:S(2)}, u32[]{:S(2)}) collective-permute-start(bf16[128,384]{1,0:T(8,128)(2,1)S(1)} %get-tuple-element.50), channel_id=1, source_target_pairs={{0,3},{1,0},{2,1},{3,2},{4,7},{5,4},{6,5},{7,6},{8,11},{9,8},{10,9... | collective-permute-start | bytes 294920 | tf_op jit(solution)/shard_map/ppermute | solution.py:245
  139.3 9.9 %collective-permute-start.16 = (f32[6,1536]{1,0:T(8,128)S(1)}, f32[6,1536]{1,0:T(8,128)S(1)}, u32[]{:S(2)}, u32[]{:S(2)}) collective-permute-start(f32[6,1536]{1,0:T(8,128)S(1)} %bitcast.42), channel_id=1, source_target_pairs={{0,0},{1,64},{2,128},{3,192},{64,1},{65,65},{66,129},{67,193},{128... | collective-permute-start | bytes 110600 | tf_op jit(solution)/shard_map/ppermute | solution.py:254

commit v3 on v2

--- a/solution.py
+++ b/solution.py
@@ -22,12 +22,15 @@
 HALF = 16
 WIDE = FRAMES + 2 * HALF
 ROWS = 6
-SLOT = 8
+FOLD = 4
+SLOT = FOLD * ROWS
+SENT = 32 * SLOT
 SHARE = 192
+STRIP = SHARE // 4
 LIMIT = 12 * 1024 * 1024
 
 
-def call(body, outs, scratch=(), scalars=1):
+def call(body, outs, scratch=(), scalars=1, cost=1):
     def run(*operands):
         specs = [pl.BlockSpec(memory_space=pltpu.SMEM)] * scalars
         specs += [pl.BlockSpec(memory_space=pltpu.VMEM)] * (len(operands) - scalars)
@@ -38,10 +41,14 @@
             out_specs=[pl.BlockSpec(memory_space=pltpu.VMEM)] * len(outs),
             scratch_shapes=list(scratch),
             compiler_params=pltpu.CompilerParams(vmem_limit_bytes=LIMIT),
-            cost_estimate=pl.CostEstimate(flops=1000, bytes_accessed=1000, transcendentals=0),
+            cost_estimate=pl.CostEstimate(flops=cost * 10**9, bytes_accessed=1000, transcendentals=0),
         )(*operands)
 
     return run
+
+
+def small(body, shape, kind):
+    return lambda *operands: call(body, [(shape, kind)], scalars=0)(*operands)[0]
 
 
 def dot(a, b, dims):
@@ -68,20 +75,23 @@
     return total
 
 
-def conv_body(facts, first, second, third, fourth, before, after, weights, convolved, payload, padded):
+def edge_row(j, low, high, spare):
+    return jnp.where(j == 0, low, jnp.where(j == PARTS - 1, high, spare))
+
+
+def conv_body(facts, first, second, third, fourth, weights, convolved, payload, padded):
     x, z, length, language = facts[0], facts[1], facts[2], facts[3]
     begin = z * FRAMES - TAPS
-    for t in range(TILES):
-        lane = slice(t * LANES, (t + 1) * LANES)
-        for k, piece in enumerate((first, second, third, fourth)):
-            j = lax.rem(x - k + PARTS, PARTS)
-            keep = valid_rows(z * FRAMES + j * OWN, OWN, length)
-            rows = pl.ds(pl.multiple_of(TAPS + j * OWN, TAPS), OWN)
-            padded[rows, lane] = jnp.where(keep, piece[:, lane].astype(F32), 0.0)
-        padded[0:TAPS, lane] = jnp.where(valid_rows(begin, TAPS, length), before[:, lane].astype(F32), 0.0)
-        padded[TAPS + FRAMES :, lane] = jnp.where(
-            valid_rows(begin + TAPS + FRAMES, TAPS, length), after[:, lane].astype(F32), 0.0
-        )
+    for k, piece in enumerate((first, second, third, fourth)):
+        j = lax.rem(x - k + PARTS, PARTS)
+        main = pl.multiple_of(TAPS + j * OWN, TAPS)
+        rim = pl.multiple_of(edge_row(j, 0, TAPS + FRAMES, 2 * TAPS + FRAMES), TAPS)
+        for t in range(TILES):
+            lane = slice(t * LANES, (t + 1) * LANES)
+            keep = valid_rows(begin + main, OWN, length)
+            padded[pl.ds(main, OWN), lane] = jnp.where(keep, piece[0:OWN, lane].astype(F32), 0.0)
+            keep = valid_rows(begin + rim, TAPS, length)
+            padded[pl.ds(rim, TAPS), lane] = jnp.where(keep, piece[OWN : OWN + TAPS, lane].astype(F32), 0.0)
     step = WIDE // 4
     for t in range(TILES):
         lane = slice(t * LANES, (t + 1) * LANES)
@@ -108,15 +118,16 @@
     payload[...] = jnp.broadcast_to(message[None], (MEMBERS, 8, LANES))
 
 
-def back_body(facts, first, second, third, fourth, own_half, other_half, weight, back, low, high):
+def back_body(facts, first, second, third, fourth, own_half, other_half, back, weight):
     x, core = facts[0], facts[4]
     weight[at(core, SHARE), :] = own_half[...]
     weight[at(1 - core, SHARE), :] = other_half[...]
     for k, piece in enumerate((first, second, third, fourth)):
         j = lax.rem(x - k + PARTS, PARTS)
-        back[at(j, OWN), :] = dot(piece[...], weight[...], ((1,), (1,)))
-    low[...] = back[0:HALF, :]
-    high[...] = back[FRAMES - HALF :, :]
+        result = dot(piece[...], weight[...], ((1,), (1,)))
+        back[pl.ds(pl.multiple_of(HALF + j * OWN, HALF), OWN), :] = result[0:OWN]
+        rim = pl.multiple_of(edge_row(j, 0, HALF + FRAMES, WIDE), HALF)
+        back[pl.ds(rim, HALF), :] = result[OWN : OWN + HALF]
 
 
 def combine(gathered, language):
@@ -131,13 +142,13 @@
     return jnp.sum(jnp.where(here, table, 0.0), axis=0, keepdims=True)
 
 
-def act_body(facts, gathered, convolved, back, before, after, gains, biases, active, normed, grad, inverses, payload):
+def act_body(facts, gathered, convolved, back, gains, biases, kept, sent, normed, grad, inverses, payload, active):
     x, z, length, language = facts[0], facts[1], facts[2], facts[3]
     same, counts, total = combine(gathered, language)
     spans = ((0, HALF), (HALF, FRAMES), (HALF + FRAMES, HALF))
     sums = [None] * 8
     sums[6] = sums[7] = jnp.zeros((1, LANES), F32)
-    kept = []
+    scales = []
     for t in range(TILES):
         lane = slice(t * LANES, (t + 1) * LANES)
         wide_lane = pl.ds(pl.multiple_of(x * BLOCK + t * LANES, LANES), LANES)
@@ -147,7 +158,7 @@
         away = means - average
         variance = jnp.sum(spread + counts * (away * away), axis=0, keepdims=True) / total
         inverse = lax.rsqrt(variance + EPSILON)
-        kept.append(inverse)
+        scales.append(inverse)
         gain = chosen_row(gains[:, wide_lane], language)
         bias = chosen_row(biases[:, wide_lane], language)
         for part, (row, size) in enumerate(spans):
@@ -159,8 +170,7 @@
                 value = (convolved[here, lane] - average) * inverse
                 pre = value * gain + bias
                 gate = 1.0 / (1.0 + jnp.exp(-pre))
-                source = (before, back, after)[part]
-                upstream = source[at_row : at_row + step, lane]
+                upstream = back[here, lane]
                 slope = jnp.where(keep, upstream * gate * (1.0 + pre * (1.0 - gate)), 0.0) * gain
                 normed[here, lane] = value
                 grad[here, lane] = slope
@@ -171,7 +181,10 @@
             if part == 1:
                 sums[t], sums[TILES + t] = first, second
     payload[...] = jnp.broadcast_to(jnp.concatenate(sums, axis=0)[None], (MEMBERS, 8, LANES))
-    inverses[...] = jnp.concatenate(kept + [sums[6]] * (8 - TILES), axis=0)
+    first_core = facts[4] == 0
+    kept[...] = jnp.where(first_core, active[:, :SHARE], active[:, SHARE:])
+    sent[...] = jnp.where(first_core, active[:, SHARE:], active[:, :SHARE])
+    inverses[...] = jnp.concatenate(scales + [sums[6]] * (8 - TILES), axis=0)
 
 
 def grad_body(facts, gathered, sums, normed, grad, inverses, weights, first, second, third, fourth, rounded, result):
@@ -207,37 +220,74 @@
         joined[:, pl.ds(pl.multiple_of(j * BLOCK, LANES), BLOCK)] = piece[...]
 
 
-def out_body(facts, active, weight, kept, first, second, third):
+def out_body(facts, mine, theirs, own_half, other_half, kept, first, second, third):
     x = facts[0]
-    kept[...] = dot(active[at(x, OWN), :], weight[...], ((1,), (0,)))
-    for k, piece in enumerate((first, second, third)):
-        j = lax.rem(x + k + 1, PARTS)
-        piece[...] = dot(active[at(j, OWN), :], weight[...], ((1,), (0,))).astype(BF16)
-
-
-def product_body(facts, active, first, second, third, fourth, kept, sent, total):
-    x, core = facts[0], facts[4]
-    for k, piece in enumerate((first, second, third, fourth)):
-        j = lax.rem(x - k + PARTS, PARTS)
-        part = dot(active[at(j, OWN), :], piece[...], ((0,), (0,)))
-        total[...] = part if k == 0 else total[...] + part
-    kept[...] = total[at(core, SHARE), :]
-    sent[...] = total[at(1 - core, SHARE), :].astype(BF16)
-
-
-def slots():
-    local = lax.broadcasted_iota(jnp.int32, (SHARE, 1), 0)
-    slot = local // ROWS * SLOT + lax.rem(local, ROWS)
-    return (lax.broadcasted_iota(jnp.int32, (SHARE, SHARE // ROWS * SLOT), 1) == slot).astype(BF16)
+    for k, piece in enumerate((kept, first, second, third)):
+        rows = at(lax.rem(x + k, PARTS), OWN)
+        total = dot(mine[rows, :], own_half[...], ((1,), (0,))) + dot(theirs[rows, :], other_half[...], ((1,), (0,)))
+        piece[...] = total.astype(piece.dtype)
+
+
+def product_body(facts, mine, theirs, first, second, third, fourth, kept, *sent):
+    x = facts[0]
+    for half in (theirs, mine):
+        total = jnp.zeros((SHARE, CHANNELS), F32)
+        for k, piece in enumerate((first, second, third, fourth)):
+            j = lax.rem(x - k + PARTS, PARTS)
+            total = total + dot(half[at(j, OWN), :], piece[0:OWN, :], ((0,), (0,)))
+        if half is mine:
+            kept[...] = total
+        else:
+            for n, target in enumerate(sent):
+                target[...] = total[n * STRIP : (n + 1) * STRIP].astype(BF16)
+
+
+def slots(q):
+    row = lax.broadcasted_iota(jnp.int32, (SENT, 1), 0)
+    inner = lax.rem(row, SLOT)
+    wanted = jnp.where(inner // ROWS == q, row // SLOT * ROWS + lax.rem(inner, ROWS), -1)
+    return (lax.broadcasted_iota(jnp.int32, (SENT, SHARE), 1) == wanted).astype(BF16)
+
+
+def tile_at(q, g):
+    start = (FOLD * g + q) * LANES
+    return slice(start, start + LANES)
+
+
+def folded(block, q):
+    return jnp.concatenate([block[:, tile_at(q, g)] for g in range(TILES)], axis=1)
+
+
+def copies_body(row_block, copies):
+    inner = lax.rem(lax.broadcasted_iota(jnp.int32, (SENT, ROWS), 0), SLOT)
+    column = lax.broadcasted_iota(jnp.int32, (SENT, ROWS), 1)
+    total = jnp.zeros((SENT, BLOCK), F32)
+    for q in range(FOLD):
+        choose = (inner == q * ROWS + column).astype(BF16)
+        total = total + dot(choose, folded(row_block[...], q), ((1,), (0,)))
+    copies[...] = total.astype(BF16)
 
 
 def weight_body(rows, half):
-    half[...] = dot(slots(), rows[...], ((1,), (0,))).astype(BF16)
-
-
-def spread_body(kept, other, spread):
-    both = (kept[...] + other[...].astype(F32)).astype(BF16)
-    spread[...] = dot(slots(), both, ((0,), (0,))).astype(BF16)
+    for q in range(FOLD):
+        part = dot(slots(q), rows[...], ((0,), (0,))).astype(BF16)
+        for g in range(TILES):
+            half[:, tile_at(q, g)] = part[:, g * LANES : (g + 1) * LANES]
+
+
+def spread_body(kept, first, second, third, fourth, spread):
+    other = jnp.concatenate([strip[...].astype(F32) for strip in (first, second, third, fourth)], axis=0)
+    both = (kept[...] + other).astype(BF16)
+    total = jnp.zeros((SENT, BLOCK), F32)
+    for q in range(FOLD):
+        total = total + dot(slots(q), folded(both, q), ((1,), (0,)))
+    spread[...] = total.astype(BF16)
+
+
+def unfold_body(sums, rows):
+    for q in range(FOLD):
+        for g in range(TILES):
+            rows[:, tile_at(q, g)] = sums[q * ROWS : (q + 1) * ROWS, g * LANES : (g + 1) * LANES]
 
 
 def around_x(piece, shift):
@@ -258,10 +308,9 @@
     return lax.optimization_barrier((value,) + others)[0]
 
 
-def along_z(low, high):
-    up = [(i, i + 1) for i in range(AXES["z"] - 1)]
-    down = [(i + 1, i) for i in range(AXES["z"] - 1)]
-    return lax.ppermute(high, "z", up), lax.ppermute(low, "z", down)
+def between_blocks(rows):
+    ends = [(4 * z + 3, 4 * z + 4) for z in range(AXES["z"] - 1)]
+    return lax.ppermute(rows, ("z", "x"), ends + [(b, a) for a, b in ends])
 
 
 def exchange(payload, axes):
@@ -273,65 +322,77 @@
     x, y, z, core = (lax.axis_index(axis) for axis in ("x", "y", "z", "c"))
     facts = jnp.stack([x, z, length[0], language[0], core, y]).astype(jnp.int32)
 
-    pieces = [lax.dynamic_slice(glu, (0, lax.rem(x + k, PARTS) * BLOCK), (OWN, BLOCK)) for k in range(PARTS)]
-    pieces = [pieces[0]] + [around_x(pieces[k], k) for k in range(1, PARTS)]
-    later = wait_for(cot, *pieces)
-    cots = [cot] + [around_x(later, k) for k in range(1, PARTS)]
-    low = jnp.stack([piece[:TAPS] for piece in pieces])
-    high = jnp.stack([piece[OWN - TAPS :] for piece in pieces])
-    low = lax.dynamic_index_in_dim(low, x, 0, keepdims=False)
-    high = lax.dynamic_index_in_dim(high, lax.rem(x + 1, PARTS), 0, keepdims=False)
-    before, after = along_z(low, high)
+    last = x == PARTS - 1
+    rim = jnp.concatenate(
+        [
+            lax.dynamic_slice_in_dim(glu, jnp.where(last, OWN - TAPS, 0), TAPS, 0),
+            lax.dynamic_slice_in_dim(cot, jnp.where(last, OWN - HALF, 0), HALF, 0),
+        ],
+        axis=0,
+    )
+    rim = between_blocks(rim)
+    copies = small(copies_body, (SENT, BLOCK), BF16)(swap_xy(w_out))
+
+    pieces = []
+    for k in range(PARTS):
+        column = lax.rem(x + k, PARTS) * BLOCK
+        own = lax.dynamic_slice(glu, (0, column), (OWN, BLOCK))
+        piece = jnp.concatenate([own, lax.dynamic_slice(rim, (0, column), (TAPS, BLOCK))], axis=0)
+        pieces.append(around_x(piece, k) if k else piece)
+    rows = exchange(wait_for(copies, *pieces), ("z", "y"))
+    cot = wait_for(jnp.concatenate([cot, rim[TAPS:]], axis=0), *pieces)
+    cots = [cot] + [around_x(cot, k) for k in range(1, PARTS)]
     convolved, payload = call(
         conv_body,
         [((WIDE, BLOCK), F32), ((MEMBERS, 8, LANES), F32)],
-        [pltpu.VMEM((WIDE + 2 * HALF, BLOCK), F32)],
-    )(facts, *pieces, before, after, conv_weight)
-
-    slot = jnp.broadcast_to(swap_xy(w_out)[None], (32, ROWS, CHANNELS))
-    slot = jnp.pad(slot, ((0, 0), (0, SLOT - ROWS), (0, 0))).reshape(-1, CHANNELS)
-    rows = exchange(slot, ("z", "y"))
+        [pltpu.VMEM((FRAMES + 3 * TAPS, BLOCK), F32)],
+        cost=5,
+    )(facts, *pieces, conv_weight)
+
     (half,) = call(weight_body, [((SHARE, CHANNELS), BF16)], scalars=0)(wait_for(rows, payload))
-    gathered = exchange(wait_for(payload, *cots), STATS)
-    weight, back, low, high = call(
-        back_body,
-        [((BLOCK, CHANNELS), BF16), ((FRAMES, BLOCK), F32), ((HALF, BLOCK), F32), ((HALF, BLOCK), F32)],
-    )(facts, *cots, half, other_core(half))
-    back_before, back_after = along_z(low, high)
-
-    active, normed, grad, inverses, payload = call(
+    gathered = exchange(wait_for(payload, half, *cots), STATS)
+    other_half = other_core(half)
+    (back,) = call(back_body, [((WIDE + HALF, BLOCK), F32)], [pltpu.VMEM((BLOCK, CHANNELS), BF16)], cost=3)(
+        facts, *cots, half, other_half
+    )
+
+    kept, sent, normed, grad, inverses, payload = call(
         act_body,
         [
-            ((FRAMES, BLOCK), BF16),
+            ((FRAMES, SHARE), BF16),
+            ((FRAMES, SHARE), BF16),
             ((WIDE, BLOCK), F32),
             ((WIDE, BLOCK), F32),
             ((8, LANES), F32),
             ((MEMBERS, 8, LANES), F32),
         ],
-    )(facts, gathered, convolved, back, back_before, back_after, bn_gain, bn_bias)
+        [pltpu.VMEM((FRAMES, BLOCK), BF16)],
+        cost=2,
+    )(facts, gathered, convolved, back, bn_gain, bn_bias)
     sums = exchange(payload, STATS)
 
-    kept, sent = call(
-        product_body,
-        [((SHARE, CHANNELS), F32), ((SHARE, CHANNELS), BF16)],
-        [pltpu.VMEM((BLOCK, CHANNELS), F32)],
-    )(facts, active, *cots)
-    (spread,) = call(spread_body, [((32 * SLOT, CHANNELS), BF16)], scalars=0)(kept, other_core(sent))
-    spread = exchange(spread, ("z", "y")).reshape(32, SLOT, CHANNELS)
-    weight_grad = swap_xy(jnp.sum(spread.astype(F32), axis=0)[:ROWS])
-
-    output, *others = call(
-        out_body, [((OWN, CHANNELS), F32)] + [((OWN, CHANNELS), BF16)] * (PARTS - 1)
-    )(facts, active, weight)
-    for k, piece in enumerate(others):
-        output = output + around_x(piece, k + 1).astype(F32)
-    output = output.astype(BF16)
+    output, *others = call(out_body, [((OWN, CHANNELS), F32)] + [((OWN, CHANNELS), BF16)] * (PARTS - 1))(
+        facts, kept, sent, half, other_half
+    )
+    arrived = [around_x(piece, k + 1) for k, piece in enumerate(others)]
+
+    kept, *sent = call(product_body, [((SHARE, CHANNELS), F32)] + [((STRIP, CHANNELS), BF16)] * 4)(
+        facts, wait_for(kept, *others), sent, *cots
+    )
+    (spread,) = call(spread_body, [((SENT, BLOCK), BF16)], scalars=0)(kept, *[other_core(strip) for strip in sent])
+    spread = exchange(spread, ("z", "y")).reshape(32, SLOT, BLOCK)
+    spread = swap_xy(jnp.sum(spread.astype(F32), axis=0))
+    (weight_grad,) = call(unfold_body, [((ROWS, CHANNELS), F32)], scalars=0)(spread)
 
     pieces = call(
         grad_body,
         [((OWN, BLOCK), BF16)] * PARTS,
         [pltpu.VMEM((WIDE, BLOCK), F32), pltpu.VMEM((FRAMES, BLOCK), F32)],
+        cost=5,
     )(facts, gathered, sums, normed, grad, inverses, conv_weight)
+    for piece in arrived:
+        output = output + wait_for(piece, *pieces).astype(F32)
+    output = output.astype(BF16)
     pieces = [pieces[0]] + [around_x(pieces[k], k) for k in range(1, PARTS)]
     (input_grad,) = call(lanes_body, [((OWN, CHANNELS), BF16)])(facts, *pieces)
     return output[None], weight_grad, input_grad[None]

time: 151 us -> 152 us (level)
  starting transfers between devices: 74.7 us -> 64.8 us
  local copies, waits for them, and re-layouts: 10.3 us -> 18.5 us
  Pallas kernels: 22 us -> 25.6 us
    ppermute x4 -> x1, starting transfers between devices: 10.7 us -> 0.67 us  [between_blocks(): return lax.ppermute(rows, ('z', 'x'), ends + [(b, a) for a, b in ends])]
    ppermute x12, waiting for transfers between devices: 7.75 us -> 16.6 us  [around_x(): lax.ppermute(piece, 'x', [(i, (i + shift) % size) for i in range(size)])]
    unnamed x39 -> x56, local copies, waits for them, and re-layouts: 9.01 us -> 15.6 us
    all_to_all x4, waiting for transfers between devices: 18.2 us -> 13.9 us  [exchange(): return lax.all_to_all(payload, axes, 0, 0, tiled=True)]
    pallas_call x9 -> x11, Pallas kernels: 22 us -> 25.6 us  [run(): pl.pallas_call(body, out_shape=[jax.ShapeDtypeStruct(shape, kind) for sha...]
    ppermute x4 -> x1, waiting for transfers between devices: 3.13 us -> 0.01 us  [between_blocks(): return lax.ppermute(rows, ('z', 'x'), ends + [(b, a) for a, b in ends])]
    dynamic_slice x1 -> x4, local copies, waits for them, and re-layouts: 0.05 us -> 2.82 us  [the longest x1 1.09 us: on_device(): own = lax.dynamic_slice(glu, (0, column), (OWN, BLOCK))]
    ppermute x2, waiting for transfers between devices: 8.13 us -> 5.74 us  [swap_xy(): return lax.ppermute(block, ('y', 'x'), pairs)]
  transfers between devices with their start and end apart: 24 -> 24, of which waited for: 11 -> 13; matrix products, arithmetic and copies ran while one was open for 2% -> 2% of each run, Pallas kernels for 12% -> 15%
where the time goes in v3:
time: 152 us; the launch traced here: 151 us
  starting transfers between devices  64.8 us (43%)
  waiting for transfers between devices  37.3 us (25%)
  Pallas kernels  25.6 us (17%)
  local copies, waits for them, and re-layouts  18.5 us (12%)
  between operations  2.31 us (2%)
  other arithmetic  2.18 us (1%)
    all_to_all x4, starting transfers between devices, exchange(): return lax.all_to_all(payload, axes, 0, 0, tiled=True)  39.4 us
    pallas_call x11, Pallas kernels, run(): pl.pallas_call(body, out_shape=[jax.ShapeDtypeStruct(shape, kind) for sha...  25.6 us
    ppermute x12, waiting for transfers between devices, around_x(): lax.ppermute(piece, 'x', [(i, (i + shift) % size) for i in range(size)])  16.6 us
    ppermute x12, starting transfers between devices, around_x(): lax.ppermute(piece, 'x', [(i, (i + shift) % size) for i in range(size)])  16.2 us
    unnamed x56, local copies, waits for them, and re-layouts  15.6 us
    all_to_all x4, waiting for transfers between devices, exchange(): return lax.all_to_all(payload, axes, 0, 0, tiled=True)  13.9 us
    ppermute x2, starting transfers between devices, swap_xy(): return lax.ppermute(block, ('y', 'x'), pairs)  7.36 us
    ppermute x2, waiting for transfers between devices, swap_xy(): return lax.ppermute(block, ('y', 'x'), pairs)  5.74 us
  transfers between devices with their start and end apart: 24, of which 13 were waited for; matrix products, arithmetic and copies ran while one was open for 2% of the time, Pallas kernels for 15%

profile of v3, /device:TPU:16, one launch (start us, length us, event | category | flops | bytes accessed | tf_op | source)
XLA Modules:
  0.0 150.7 jit_solution(16434040258930713639)
XLA Ops:
  0.6 0.8 dynamic-slice_bitcast_fusion.5
  1.4 0.9 dynamic-slice_bitcast_fusion.3
  2.4 0.7 collective-permute-start
  3.0 4.7 %collective-permute-start.4 = (bf16[6,1536]{1,0:T(8,128)(2,1)}, bf16[6,1536]{1,0:T(8,128)(2,1)S(1)}, u32[]{:S(2)}, u32[]{:S(2)}) collective-permute-start(bf16[6,1536]{1,0:T(8,128)(2,1)} %param.12), channel_id=1, source_target_pairs={{0,0},{1,64},{2,128},{3,192},{64,1},{65,65},{66,129},{67,193},{128... | collective-permute-start | bytes 55304 | tf_op jit(solution)/shard_map/ppermute | solution.py:304
  7.8 1.1 dynamic-slice_bitcast_fusion
  9.1 6.7 %collective-permute-start.1 = (bf16[160,384]{1,0:T(8,128)(2,1)S(1)}, bf16[160,384]{1,0:T(8,128)(2,1)S(1)}, u32[]{:S(2)}, u32[]{:S(2)}) collective-permute-start(bf16[160,384]{1,0:T(8,128)(2,1)S(1)} %pad_maximum_fusion.3), channel_id=1, source_target_pairs={{0,1},{1,2},{2,3},{3,0},{4,5},{5,6},{6,7},{7,4},{8,9},{9,10},{10,1... | collective-permute-start | bytes 368648 | tf_op jit(solution)/shard_map/ppermute | solution.py:295
  15.9 1.6 %shard_map.104 = bf16[768,384]{1,0:T(8,128)(2,1)} custom-call(bf16[6,1536]{1,0:T(8,128)(2,1)S(1)} %collective-permute-done.4.row_block), custom_call_target="tpu_custom_call" | custom-call | flops 1000000000 | bytes 1000 | tf_op jit(solution)/shard_map/pallas_call | solution.py:37
  17.5 0.7 collective-permute-done.1.second
  18.2 2.6 %collective-permute-done.3.fourth = bf16[160,384]{1,0:T(8,128)(2,1)S(1)} collective-permute-done((bf16[160,384]{1,0:T(8,128)(2,1)S(1)}, bf16[160,384]{1,0:T(8,128)(2,1)S(1)}, u32[]{:S(2)}, u32[]{:S(2)}) %collective-permute-start.3) | collective-permute-done | bytes 122912 | tf_op jit(solution)/shard_map/ppermute | solution.py:295
  20.8 12.2 %all-to-all-start = ((bf16[32,24,384]{2,1,0:T(8,128)(2,1)}), bf16[32,24,384]{2,1,0:T(8,128)(2,1)S(1)}, u32[]{:S(2)}, u32[]{:S(2)}) async-start(bf16[32,24,384]{2,1,0:T(8,128)(2,1)} %bitcast.10), calls=%async_computation | async-start | bytes 1179648 | tf_op jit(solution)/shard_map/all_to_all | solution.py:317
  34.5 2.0 %collective-permute-start.7 = (bf16[144,1536]{1,0:T(8,128)(2,1)S(1)}, bf16[144,1536]{1,0:T(8,128)(2,1)S(1)}, u32[]{:S(2)}, u32[]{:S(2)}) collective-permute-start(bf16[144,1536]{1,0:T(8,128)(2,1)S(1)} %pad_maximum_fusion.first), channel_id=1, source_target_pairs={{0,3},{1,0},{2,1},{3,2},{4,7},{5,4},{6,5},{7,6},{8,11},{9,8},{10,9... | collective-permute-start | bytes 1327112 | tf_op jit(solution)/shard_map/ppermute | solution.py:295
  36.4 0.6 collective-permute-start.6
  37.0 0.4 collective-permute-start.5
  37.4 5.0 %shard_map.103 = (f32[544,384]{1,0:T(8,128)S(1)}, f32[64,8,128]{2,1,0:T(8,128)}) custom-call(s32[6]{0:T(128)S(1)} %stack.19.facts, bf16[160,384]{1,0:T(8,128)(2,1)S(1)} %pad_maximum_fusion.2.first, bf16[160,384]{1,0:T(8,128)(2,1)S(1)} %collective-permute-done.1.second, bf16[160,384]{1,0:T(8,128)(2,1)S(1)} %collective-permute-done.2.third, ...), custom_call_target="tpu_custom_call" | custom-call | flops 5000000000 | bytes 1000 | tf_op jit(solution)/shard_map/pallas_call | solution.py:37
  42.4 0.9 copy-done.25
  43.2 7.6 %all-to-all-done = bf16[32,24,384]{2,1,0:T(8,128)(2,1)S(1)} async-done(((bf16[32,24,384]{2,1,0:T(8,128)(2,1)}), bf16[32,24,384]{2,1,0:T(8,128)(2,1)S(1)}, u32[]{:S(2)}, u32[]{:S(2)}) %all-to-all-start) | async-done | bytes 589856 | tf_op jit(solution)/shard_map/all_to_all | solution.py:317
  50.8 1.3 shard_map.105.own_half
  52.2 0.8 copy-done
  52.9 4.0 %collective-permute-done.5.second = bf16[144,1536]{1,0:T(8,128)(2,1)} collective-permute-done((bf16[144,1536]{1,0:T(8,128)(2,1)S(1)}, bf16[144,1536]{1,0:T(8,128)(2,1)}, u32[]{:S(2)}, u32[]{:S(2)}) %collective-permute-start.5) | collective-permute-done | bytes 442400 | tf_op jit(solution)/shard_map/ppermute | solution.py:295
  56.9 10.2 %all-to-all-start.1 = ((f32[64,8,128]{2,1,0:T(8,128)}), f32[64,8,128]{2,1,0:T(8,128)S(1)}, u32[]{:S(2)}, u32[]{:S(2)}) async-start(f32[64,8,128]{2,1,0:T(8,128)} %get-tuple-element.36), calls=%async_computation.1 | async-start | bytes 524288 | tf_op jit(solution)/shard_map/all_to_all | solution.py:317
  67.1 1.0 copy-done.1
  68.1 2.6 %shard_map.106.back = f32[560,384]{1,0:T(8,128)S(1)} custom-call(s32[6]{0:T(128)S(1)} %stack.19.facts, bf16[144,1536]{1,0:T(8,128)(2,1)S(1)} %pad_maximum_fusion.first, bf16[144,1536]{1,0:T(8,128)(2,1)} %collective-permute-done.5.second, bf16[144,1536]{1,0:T(8,128)(2,1)S(1)} %copy-done.1, bf16[144,1536]{1,0:T(8,128)(2,1)S(1)} %collective-permute-done.7.fourth, ...), custom_call_target="tpu_custom_call" | custom-call | flops 3000000000 | bytes 1000 | tf_op jit(solution)/shard_map/pallas_call | solution.py:37
  70.7 0.9 copy-done.19
  71.7 6.4 %all-to-all-done.1.gathered = f32[64,8,128]{2,1,0:T(8,128)S(1)} async-done(((f32[64,8,128]{2,1,0:T(8,128)}), f32[64,8,128]{2,1,0:T(8,128)S(1)}, u32[]{:S(2)}, u32[]{:S(2)}) %all-to-all-start.1) | async-done | bytes 262176 | tf_op jit(solution)/shard_map/all_to_all | solution.py:317
  78.1 1.2 copy-done.20
  79.2 1.1 copy-done.26
  80.4 2.5 %shard_map.107 = (bf16[512,192]{1,0:T(8,128)(2,1)S(1)}, bf16[512,192]{1,0:T(8,128)(2,1)S(1)}, f32[544,384]{1,0:T(8,128)S(1)}, f32[544,384]{1,0:T(8,128)S(1)}, f3...) custom-call(s32[6]{0:T(128)S(1)} %stack.19.facts, f32[64,8,128]{2,1,0:T(8,128)S(1)} %all-to-all-done.1.gathered, ...), custom_call_target="tpu_custom_call" | custom-call | flops 2000000000 | bytes 1000 | tf_op jit(solution)/shard_map/pallas_call | solution.py:37
  82.9 0.7 copy-done.13
  83.6 0.7 copy-done.16
  84.3 0.9 copy-done.21
  85.2 0.9 copy-done.23
  86.1 6.9 %all-to-all-start.2 = ((f32[64,8,128]{2,1,0:T(8,128)}), f32[64,8,128]{2,1,0:T(8,128)S(1)}, u32[]{:S(2)}, u32[]{:S(2)}) async-start(f32[64,8,128]{2,1,0:T(8,128)} %get-tuple-element.42), calls=%async_computation.2 | async-start | bytes 524288 | tf_op jit(solution)/shard_map/all_to_all | solution.py:317
  93.0 0.9 copy-done.14
  94.0 0.9 copy-done.17
  94.9 1.5 shard_map.108
  96.4 0.7 copy-done.3
  97.2 0.7 copy-done.5
  97.9 0.7 copy-done.7
  98.7 2.4 %shard_map.110 = (f32[192,1536]{1,0:T(8,128)S(1)}, bf16[48,1536]{1,0:T(8,128)(2,1)S(1)}, bf16[48,1536]{1,0:T(8,128)(2,1)S(1)}, bf16[48,1536]{1,0:T(8,128)(2,1)S(1)}, bf16[48,1536]{1,0:T(8,128)(2,1)S(1)}) custom-call(s32[6]{0:T(128)S(1)} %stack.19.facts, bf16[512,192]{1,0:T(8,128)(2,1)S(1)} %copy-done.15, bf16[512,192]{1,0:T(8,128)(2,1)S(1)} %copy-done.18, ...), custom_call_target="tpu_custom_call" | custom-call | flops 1000000000 | bytes 1000 | tf_op jit(solution)/shard_map/pallas_call | solution.py:37
  101.1 0.3 collective-permute-start.12
  101.4 0.3 collective-permute-start.13
  101.7 0.2 collective-permute-start.14
  101.9 0.3 collective-permute-start.15
  102.2 0.3 collective-permute-done.12.first
  102.6 0.2 collective-permute-done.13.second
  102.8 0.3 collective-permute-done.14.third
  103.3 2.1 %shard_map.111 = bf16[768,384]{1,0:T(8,128)(2,1)} custom-call(f32[192,1536]{1,0:T(8,128)S(1)} %get-tuple-element.56.kept, bf16[48,1536]{1,0:T(8,128)(2,1)S(1)} %collective-permute-done.12.first, bf16[48,1536]{1,0:T(8,128)(2,1)S(1)} %collective-permute-done.13.second, bf16[48,1536]{1,0:T(8,128)(2,1)S(1)} %collective-permute-done.14.third, ...), custom_call_target="tpu_custom_call" | custom-call | flops 1000000000 | bytes 1000 | tf_op jit(solution)/shard_map/pallas_call | solution.py:37
  105.4 10.1 %all-to-all-start.3 = ((bf16[32,24,384]{2,1,0:T(8,128)(2,1)}), bf16[32,24,384]{2,1,0:T(8,128)(2,1)}, u32[]{:S(2)}, u32[]{:S(2)}) async-start(bf16[32,24,384]{2,1,0:T(8,128)(2,1)} %bitcast.14), calls=%async_computation.3 | async-start | bytes 1179648 | tf_op jit(solution)/shard_map/all_to_all | solution.py:317
  115.6 2.9 %collective-permute-start.10 = (bf16[128,1536]{1,0:T(8,128)(2,1)S(1)}, bf16[128,1536]{1,0:T(8,128)(2,1)S(1)}, u32[]{:S(2)}, u32[]{:S(2)}) collective-permute-start(bf16[128,1536]{1,0:T(8,128)(2,1)S(1)} %copy-done.6), channel_id=1, source_target_pairs={{0,2},{1,3},{2,0},{3,1},{4,6},{5,7},{6,4},{7,5},{8,10},{9,11},{10,... | collective-permute-start | bytes 1179656 | tf_op jit(solution)/shard_map/ppermute | solution.py:295
  118.5 0.8 collective-permute-start.11
  119.3 1.1 copy-done.22
  120.4 1.1 copy-done.24
  121.6 4.7 %shard_map.109 = (bf16[128,384]{1,0:T(8,128)(2,1)S(1)}, bf16[128,384]{1,0:T(8,128)(2,1)S(1)}, bf16[128,384]{1,0:T(8,128)(2,1)S(1)}, bf16[128,384]{1,0:T(8,128)(2,1)S(1)}) custom-call(s32[6]{0:T(128)S(1)} %stack.19.facts, f32[64,8,128]{2,1,0:T(8,128)S(1)} %all-to-all-done.1.gathered, f32[64,8,128]{2,1,0:T(8,128)S(1)} %all-to-all-done.2.sums, ...), custom_call_target="tpu_custom_call" | custom-call | flops 5000000000 | bytes 1000 | tf_op jit(solution)/shard_map/pallas_call | solution.py:37
  126.2 1.3 collective-permute-start.17
  127.6 1.4 collective-permute-start.18
  128.9 6.3 %collective-permute-done.9 = bf16[128,1536]{1,0:T(8,128)(2,1)S(1)} collective-permute-done((bf16[128,1536]{1,0:T(8,128)(2,1)S(1)}, bf16[128,1536]{1,0:T(8,128)(2,1)S(1)}, u32[]{:S(2)}, u32[]{:S(2)}) %collective-permute-start.9) | collective-permute-done | bytes 393248 | tf_op jit(solution)/shard_map/ppermute | solution.py:295
  135.3 1.8 %collective-permute-done.10 = bf16[128,1536]{1,0:T(8,128)(2,1)S(1)} collective-permute-done((bf16[128,1536]{1,0:T(8,128)(2,1)S(1)}, bf16[128,1536]{1,0:T(8,128)(2,1)S(1)}, u32[]{:S(2)}, u32[]{:S(2)}) %collective-permute-start.10) | collective-permute-done | bytes 393248 | tf_op jit(solution)/shard_map/ppermute | solution.py:295
  137.0 1.2 collective-permute-done.11
  138.2 0.9 fusion
  139.1 1.2 convert_reduce_fusion
  140.3 2.6 %collective-permute-start.16 = (f32[24,384]{1,0:T(8,128)S(1)}, f32[24,384]{1,0:T(8,128)S(1)}, u32[]{:S(2)}, u32[]{:S(2)}) collective-permute-start(f32[24,384]{1,0:T(8,128)S(1)} %convert_reduce_fusion), channel_id=1, source_target_pairs={{0,0},{1,64},{2,128},{3,192},{64,1},{65,65},{66,129},{67,193},{128... | collective-permute-start | bytes 110600 | tf_op jit(solution)/shard_map/ppermute | solution.py:304
  143.0 1.3 shard_map.113
  144.3 5.7 %collective-permute-done.16.sums = f32[24,384]{1,0:T(8,128)S(1)} collective-permute-done((f32[24,384]{1,0:T(8,128)S(1)}, f32[24,384]{1,0:T(8,128)S(1)}, u32[]{:S(2)}, u32[]{:S(2)}) %collective-permute-start.16) | collective-permute-done | bytes 36896 | tf_op jit(solution)/shard_map/ppermute | solution.py:304
  150.0 0.6 shard_map.112
  (65 shorter events, 0.9 us)
Async XLA Ops:
  2.4 6.5 %collective-permute-start = (bf16[48,1536]{1,0:T(8,128)(2,1)S(1)}, bf16[48,1536]{1,0:T(8,128)(2,1)S(1)}, u32[]{:S(2)}, u32[]{:S(2)}) collective-permute-start(bf16[48,1536]{1,0:T(8,128)(2,1)S(1)} %pad_maximum_fusion.1), channel_id=1, source_target_pairs={{3,4},{7,8},{11,12},{15,16},{19,20},{23,24},{27,28},{4,3},{8,7},{1... | collective-permute-start | bytes 442376 | tf_op jit(solution)/shard_map/ppermute | solution.py:313
  3.0 12.9 %collective-permute-start.4 = (bf16[6,1536]{1,0:T(8,128)(2,1)}, bf16[6,1536]{1,0:T(8,128)(2,1)S(1)}, u32[]{:S(2)}, u32[]{:S(2)}) collective-permute-start(bf16[6,1536]{1,0:T(8,128)(2,1)} %param.12), channel_id=1, source_target_pairs={{0,0},{1,64},{2,128},{3,192},{64,1},{65,65},{66,129},{67,193},{128... | collective-permute-start | bytes 55304 | tf_op jit(solution)/shard_map/ppermute | solution.py:304
  8.9 8.6 %collective-permute-start.2 = (bf16[160,384]{1,0:T(8,128)(2,1)S(1)}, bf16[160,384]{1,0:T(8,128)(2,1)S(1)}, u32[]{:S(2)}, u32[]{:S(2)}) collective-permute-start(bf16[160,384]{1,0:T(8,128)(2,1)S(1)} %pad_maximum_fusion.4), channel_id=1, source_target_pairs={{0,2},{1,3},{2,0},{3,1},{4,6},{5,7},{6,4},{7,5},{8,10},{9,11},{10,... | collective-permute-start | bytes 368648 | tf_op jit(solution)/shard_map/ppermute | solution.py:295
  9.1 9.2 %collective-permute-start.1 = (bf16[160,384]{1,0:T(8,128)(2,1)S(1)}, bf16[160,384]{1,0:T(8,128)(2,1)S(1)}, u32[]{:S(2)}, u32[]{:S(2)}) collective-permute-start(bf16[160,384]{1,0:T(8,128)(2,1)S(1)} %pad_maximum_fusion.3), channel_id=1, source_target_pairs={{0,1},{1,2},{2,3},{3,0},{4,5},{5,6},{6,7},{7,4},{8,9},{9,10},{10,1... | collective-permute-start | bytes 368648 | tf_op jit(solution)/shard_map/ppermute | solution.py:295
  15.8 5.0 %collective-permute-start.3 = (bf16[160,384]{1,0:T(8,128)(2,1)S(1)}, bf16[160,384]{1,0:T(8,128)(2,1)S(1)}, u32[]{:S(2)}, u32[]{:S(2)}) collective-permute-start(bf16[160,384]{1,0:T(8,128)(2,1)S(1)} %pad_maximum_fusion.5), channel_id=1, source_target_pairs={{0,3},{1,0},{2,1},{3,2},{4,7},{5,4},{6,5},{7,6},{8,11},{9,8},{10,9... | collective-permute-start | bytes 368648 | tf_op jit(solution)/shard_map/ppermute | solution.py:295
  17.5 16.9 %copy-start.27 = (bf16[1,128,1536]{2,1,0:T(8,128)(2,1)S(1)}, bf16[1,128,1536]{2,1,0:T(8,128)(2,1)}, u32[]{:S(2)}) copy-start(bf16[1,128,1536]{2,1,0:T(8,128)(2,1)} %param.13) | copy-start | bytes 1179652
  17.5 19.9 %copy-start.9 = (f32[32,1536]{1,0:T(8,128)S(1)}, f32[32,1536]{1,0:T(8,128)}, u32[]{:S(2)}) copy-start(f32[32,1536]{1,0:T(8,128)} %weights.3) | copy-start | bytes 589828
  20.8 30.0 %all-to-all-start = ((bf16[32,24,384]{2,1,0:T(8,128)(2,1)}), bf16[32,24,384]{2,1,0:T(8,128)(2,1)S(1)}, u32[]{:S(2)}, u32[]{:S(2)}) async-start(bf16[32,24,384]{2,1,0:T(8,128)(2,1)} %bitcast.10), calls=%async_computation | async-start | bytes 1179648 | tf_op jit(solution)/shard_map/all_to_all | solution.py:317
  34.5 17.7 %collective-permute-start.7 = (bf16[144,1536]{1,0:T(8,128)(2,1)S(1)}, bf16[144,1536]{1,0:T(8,128)(2,1)S(1)}, u32[]{:S(2)}, u32[]{:S(2)}) collective-permute-start(bf16[144,1536]{1,0:T(8,128)(2,1)S(1)} %pad_maximum_fusion.first), channel_id=1, source_target_pairs={{0,3},{1,0},{2,1},{3,2},{4,7},{5,4},{6,5},{7,6},{8,11},{9,8},{10,9... | collective-permute-start | bytes 1327112 | tf_op jit(solution)/shard_map/ppermute | solution.py:295
  36.4 15.7 %collective-permute-start.6 = (bf16[144,1536]{1,0:T(8,128)(2,1)S(1)}, bf16[144,1536]{1,0:T(8,128)(2,1)S(1)}, u32[]{:S(2)}, u32[]{:S(2)}) collective-permute-start(bf16[144,1536]{1,0:T(8,128)(2,1)S(1)} %pad_maximum_fusion.first), channel_id=1, source_target_pairs={{0,2},{1,3},{2,0},{3,1},{4,6},{5,7},{6,4},{7,5},{8,10},{9,11},{10,... | collective-permute-start | bytes 1327112 | tf_op jit(solution)/shard_map/ppermute | solution.py:295
  37.0 19.9 %collective-permute-start.5 = (bf16[144,1536]{1,0:T(8,128)(2,1)S(1)}, bf16[144,1536]{1,0:T(8,128)(2,1)}, u32[]{:S(2)}, u32[]{:S(2)}) collective-permute-start(bf16[144,1536]{1,0:T(8,128)(2,1)S(1)} %pad_maximum_fusion.first), channel_id=1, source_target_pairs={{0,1},{1,2},{2,3},{3,0},{4,5},{5,6},{6,7},{7,4},{8,9},{9,10},{10,1... | collective-permute-start | bytes 1327112 | tf_op jit(solution)/shard_map/ppermute | solution.py:295
  42.3 0.9 copy-start.25
  52.1 15.0 %collective-permute-start.8 = (bf16[192,1536]{1,0:T(8,128)(2,1)S(1)}, bf16[192,1536]{1,0:T(8,128)(2,1)S(1)}, u32[]{:S(2)}, u32[]{:S(2)}) collective-permute-start(bf16[192,1536]{1,0:T(8,128)(2,1)S(1)} %shard_map.105.own_half), channel_id=1, source_target_pairs={{0,32},{32,0},{1,33},{33,1},{2,34},{34,2},{3,35},{35,3},{4,36},{36... | collective-permute-start | bytes 1769480 | tf_op jit(solution)/shard_map/ppermute | solution.py:299
  52.2 0.8 copy-start
  56.9 21.1 %all-to-all-start.1 = ((f32[64,8,128]{2,1,0:T(8,128)}), f32[64,8,128]{2,1,0:T(8,128)S(1)}, u32[]{:S(2)}, u32[]{:S(2)}) async-start(f32[64,8,128]{2,1,0:T(8,128)} %get-tuple-element.36), calls=%async_computation.1 | async-start | bytes 524288 | tf_op jit(solution)/shard_map/all_to_all | solution.py:317
  67.1 1.0 copy-start.1
  68.1 9.9 %copy-start.11 = (f32[16,1536]{1,0:T(8,128)S(1)}, f32[16,1536]{1,0:T(8,128)}, u32[]{:S(2)}) copy-start(f32[16,1536]{1,0:T(8,128)} %gains.1) | copy-start | bytes 294916
  68.1 9.9 %copy-start.12 = (f32[16,1536]{1,0:T(8,128)S(1)}, f32[16,1536]{1,0:T(8,128)}, u32[]{:S(2)}) copy-start(f32[16,1536]{1,0:T(8,128)} %biases.1) | copy-start | bytes 294916
  70.7 0.9 copy-start.19
  78.1 1.2 copy-start.20
  79.2 1.1 copy-start.26
  82.9 0.7 copy-start.13
  83.5 0.7 copy-start.16
  84.3 0.9 copy-start.21
  85.2 0.9 copy-start.23
  86.1 19.3 %all-to-all-start.2 = ((f32[64,8,128]{2,1,0:T(8,128)}), f32[64,8,128]{2,1,0:T(8,128)S(1)}, u32[]{:S(2)}, u32[]{:S(2)}) async-start(f32[64,8,128]{2,1,0:T(8,128)} %get-tuple-element.42), calls=%async_computation.2 | async-start | bytes 524288 | tf_op jit(solution)/shard_map/all_to_all | solution.py:317
  93.0 1.0 copy-start.14
  94.0 0.9 copy-start.17
  94.9 3.8 %copy-start.2 = (bf16[144,1536]{1,0:T(8,128)(2,1)S(1)}, bf16[144,1536]{1,0:T(8,128)(2,1)}, u32[]{:S(2)}) copy-start(bf16[144,1536]{1,0:T(8,128)(2,1)} %copy-done) | copy-start | bytes 1327108
  94.9 3.8 %copy-start.15 = (bf16[512,192]{1,0:T(8,128)(2,1)S(1)}, bf16[512,192]{1,0:T(8,128)(2,1)}, u32[]{:S(2)}) copy-start(bf16[512,192]{1,0:T(8,128)(2,1)} %copy-done.13) | copy-start | bytes 589828
  94.9 3.8 %copy-start.18 = (bf16[512,192]{1,0:T(8,128)(2,1)S(1)}, bf16[512,192]{1,0:T(8,128)(2,1)}, u32[]{:S(2)}) copy-start(bf16[512,192]{1,0:T(8,128)(2,1)} %copy-done.16) | copy-start | bytes 589828
  96.4 0.7 copy-start.3
  97.2 0.7 copy-start.5
  97.9 0.7 copy-start.7
  101.1 1.5 collective-permute-start.12
  101.4 1.4 collective-permute-start.13
  101.7 1.4 collective-permute-start.14
  101.9 1.4 collective-permute-start.15
  103.3 16.0 %copy-start.10 = (f32[32,1536]{1,0:T(8,128)S(1)}, f32[32,1536]{1,0:T(8,128)}, u32[]{:S(2)}) copy-start(f32[32,1536]{1,0:T(8,128)} %weights.3) | copy-start | bytes 589828
  105.4 10.1 %copy-start.8 = (bf16[128,1536]{1,0:T(8,128)(2,1)S(1)}, bf16[128,1536]{1,0:T(8,128)(2,1)}, u32[]{:S(2)}) copy-start(bf16[128,1536]{1,0:T(8,128)(2,1)} %copy-done.7) | copy-start | bytes 1179652
  105.4 10.2 %copy-start.6 = (bf16[128,1536]{1,0:T(8,128)(2,1)S(1)}, bf16[128,1536]{1,0:T(8,128)(2,1)}, u32[]{:S(2)}) copy-start(bf16[128,1536]{1,0:T(8,128)(2,1)} %copy-done.5) | copy-start | bytes 1179652
  105.4 13.1 %copy-start.4 = (bf16[128,1536]{1,0:T(8,128)(2,1)S(1)}, bf16[128,1536]{1,0:T(8,128)(2,1)}, u32[]{:S(2)}) copy-start(bf16[128,1536]{1,0:T(8,128)(2,1)} %copy-done.3) | copy-start | bytes 1179652
  105.4 33.7 %all-to-all-start.3 = ((bf16[32,24,384]{2,1,0:T(8,128)(2,1)}), bf16[32,24,384]{2,1,0:T(8,128)(2,1)}, u32[]{:S(2)}, u32[]{:S(2)}) async-start(bf16[32,24,384]{2,1,0:T(8,128)(2,1)} %bitcast.14), calls=%async_computation.3 | async-start | bytes 1179648 | tf_op jit(solution)/shard_map/all_to_all | solution.py:317
  115.5 19.7 %collective-permute-start.9 = (bf16[128,1536]{1,0:T(8,128)(2,1)S(1)}, bf16[128,1536]{1,0:T(8,128)(2,1)S(1)}, u32[]{:S(2)}, u32[]{:S(2)}) collective-permute-start(bf16[128,1536]{1,0:T(8,128)(2,1)S(1)} %copy-done.8), channel_id=1, source_target_pairs={{0,1},{1,2},{2,3},{3,0},{4,5},{5,6},{6,7},{7,4},{8,9},{9,10},{10,1... | collective-permute-start | bytes 1179656 | tf_op jit(solution)/shard_map/ppermute | solution.py:295
  115.6 21.4 %collective-permute-start.10 = (bf16[128,1536]{1,0:T(8,128)(2,1)S(1)}, bf16[128,1536]{1,0:T(8,128)(2,1)S(1)}, u32[]{:S(2)}, u32[]{:S(2)}) collective-permute-start(bf16[128,1536]{1,0:T(8,128)(2,1)S(1)} %copy-done.6), channel_id=1, source_target_pairs={{0,2},{1,3},{2,0},{3,1},{4,6},{5,7},{6,4},{7,5},{8,10},{9,11},{10,... | collective-permute-start | bytes 1179656 | tf_op jit(solution)/shard_map/ppermute | solution.py:295
  118.5 19.7 %collective-permute-start.11 = (bf16[128,1536]{1,0:T(8,128)(2,1)S(1)}, bf16[128,1536]{1,0:T(8,128)(2,1)S(1)}, u32[]{:S(2)}, u32[]{:S(2)}) collective-permute-start(bf16[128,1536]{1,0:T(8,128)(2,1)S(1)} %copy-done.4), channel_id=1, source_target_pairs={{0,3},{1,0},{2,1},{3,2},{4,7},{5,4},{6,5},{7,6},{8,11},{9,8},{10,9... | collective-permute-start | bytes 1179656 | tf_op jit(solution)/shard_map/ppermute | solution.py:295
  119.3 1.2 copy-start.22
  120.4 1.1 copy-start.24
  126.2 16.7 %collective-permute-start.17 = (bf16[128,384]{1,0:T(8,128)(2,1)S(1)}, bf16[128,384]{1,0:T(8,128)(2,1)S(1)}, u32[]{:S(2)}, u32[]{:S(2)}) collective-permute-start(bf16[128,384]{1,0:T(8,128)(2,1)S(1)} %get-tuple-element.47), channel_id=1, source_target_pairs={{0,1},{1,2},{2,3},{3,0},{4,5},{5,6},{6,7},{7,4},{8,9},{9,10},{10,1... | collective-permute-start | bytes 294920 | tf_op jit(solution)/shard_map/ppermute | solution.py:295
  127.6 15.4 %collective-permute-start.18 = (bf16[128,384]{1,0:T(8,128)(2,1)S(1)}, bf16[128,384]{1,0:T(8,128)(2,1)S(1)}, u32[]{:S(2)}, u32[]{:S(2)}) collective-permute-start(bf16[128,384]{1,0:T(8,128)(2,1)S(1)} %get-tuple-element.48), channel_id=1, source_target_pairs={{0,2},{1,3},{2,0},{3,1},{4,6},{5,7},{6,4},{7,5},{8,10},{9,11},{10,... | collective-permute-start | bytes 294920 | tf_op jit(solution)/shard_map/ppermute | solution.py:295
  135.3 7.7 %collective-permute-start.19 = (bf16[128,384]{1,0:T(8,128)(2,1)S(1)}, bf16[128,384]{1,0:T(8,128)(2,1)S(1)}, u32[]{:S(2)}, u32[]{:S(2)}) collective-permute-start(bf16[128,384]{1,0:T(8,128)(2,1)S(1)} %get-tuple-element.49), channel_id=1, source_target_pairs={{0,3},{1,0},{2,1},{3,2},{4,7},{5,4},{6,5},{7,6},{8,11},{9,8},{10,9... | collective-permute-start | bytes 294920 | tf_op jit(solution)/shard_map/ppermute | solution.py:295
  140.3 9.8 %collective-permute-start.16 = (f32[24,384]{1,0:T(8,128)S(1)}, f32[24,384]{1,0:T(8,128)S(1)}, u32[]{:S(2)}, u32[]{:S(2)}) collective-permute-start(f32[24,384]{1,0:T(8,128)S(1)} %convert_reduce_fusion), channel_id=1, source_target_pairs={{0,0},{1,64},{2,128},{3,192},{64,1},{65,65},{66,129},{67,193},{128... | collective-permute-start | bytes 110600 | tf_op jit(solution)/shard_map/ppermute | solution.py:304

commit v4 on v3

--- a/solution.py
+++ b/solution.py
@@ -41,6 +41,47 @@
             out_specs=[pl.BlockSpec(memory_space=pltpu.VMEM)] * len(outs),
             scratch_shapes=list(scratch),
             compiler_params=pltpu.CompilerParams(vmem_limit_bytes=LIMIT),
+            cost_estimate=pl.CostEstimate(flops=cost * 10**9, bytes_accessed=1000, transcendentals=0),
+        )(*operands)
+
+    return run
+
+
+def staged_call(body, outs, scratch=(), scalars=1, cost=1):
+    made = [jax.ShapeDtypeStruct(shape, kind) for shape, kind in outs]
+
+    def run(*operands):
+        arrays = operands[scalars:]
+        taken, given = len(arrays), len(made)
+
+        def staged(*refs):
+            facts, refs = refs[:scalars], refs[scalars:]
+            sources, refs = refs[:taken], refs[taken:]
+            targets, refs = refs[:given], refs[given:]
+            held, refs = refs[:taken], refs[taken:]
+            results, refs = refs[:given], refs[given:]
+            own, (arrive, leave) = refs[: len(scratch)], refs[len(scratch) :]
+            copies = [pltpu.make_async_copy(s, h, arrive.at[i]) for i, (s, h) in enumerate(zip(sources, held))]
+            for copy in copies:
+                copy.start()
+            for copy in copies:
+                copy.wait()
+            body(*facts, *held, *results, *own)
+            copies = [pltpu.make_async_copy(r, t, leave.at[i]) for i, (r, t) in enumerate(zip(results, targets))]
+            for copy in copies:
+                copy.start()
+            for copy in copies:
+                copy.wait()
+
+        return pl.pallas_call(
+            staged,
+            out_shape=made,
+            in_specs=[pl.BlockSpec(memory_space=pltpu.SMEM)] * scalars + [pl.BlockSpec(memory_space=pl.ANY)] * taken,
+            out_specs=[pl.BlockSpec(memory_space=pl.ANY)] * given,
+            scratch_shapes=[pltpu.VMEM(array.shape, array.dtype) for array in (*arrays, *made)]
+            + list(scratch)
+            + [pltpu.SemaphoreType.DMA((taken,)), pltpu.SemaphoreType.DMA((given,))],
+            compiler_params=pltpu.CompilerParams(vmem_limit_bytes=5 * LIMIT),
             cost_estimate=pl.CostEstimate(flops=cost * 10**9, bytes_accessed=1000, transcendentals=0),
         )(*operands)
 
@@ -350,13 +391,13 @@
     )(facts, *pieces, conv_weight)
 
     (half,) = call(weight_body, [((SHARE, CHANNELS), BF16)], scalars=0)(wait_for(rows, payload))
-    gathered = exchange(wait_for(payload, half, *cots), STATS)
+    gathered = exchange(wait_for(payload, *cots), STATS)
     other_half = other_core(half)
     (back,) = call(back_body, [((WIDE + HALF, BLOCK), F32)], [pltpu.VMEM((BLOCK, CHANNELS), BF16)], cost=3)(
         facts, *cots, half, other_half
     )
 
-    kept, sent, normed, grad, inverses, payload = call(
+    kept, sent, normed, grad, inverses, payload = staged_call(
         act_body,
         [
             ((FRAMES, SHARE), BF16),
@@ -389,7 +430,7 @@
         [((OWN, BLOCK), BF16)] * PARTS,
         [pltpu.VMEM((WIDE, BLOCK), F32), pltpu.VMEM((FRAMES, BLOCK), F32)],
         cost=5,
-    )(facts, gathered, sums, normed, grad, inverses, conv_weight)
+    )(facts, gathered, wait_for(sums, *arrived), normed, grad, inverses, conv_weight)
     for piece in arrived:
         output = output + wait_for(piece, *pieces).astype(F32)
     output = output.astype(BF16)

time: 152 us -> 145 us (0.954)
  local copies, waits for them, and re-layouts: 18.5 us -> 9.68 us
  waiting for transfers between devices: 37.3 us -> 32.2 us
  starting transfers between devices: 64.8 us -> 68.4 us
  Pallas kernels: 25.6 us -> 29 us
    unnamed x56 -> x32, local copies, waits for them, and re-layouts: 15.6 us -> 6.77 us
    pallas_call x0 -> x1, Pallas kernels: none -> 5 us  [run(): pl.pallas_call(staged, out_shape=made, in_specs=[pl.BlockSpec(memory_spac...]
    ppermute x12, waiting for transfers between devices: 16.6 us -> 12.9 us  [around_x(): lax.ppermute(piece, 'x', [(i, (i + shift) % size) for i in range(size)])]
    ppermute x2, waiting for transfers between devices: 5.74 us -> 3.73 us  [swap_xy(): return lax.ppermute(block, ('y', 'x'), pairs)]
    ppermute x2, starting transfers between devices: 7.36 us -> 9.36 us  [swap_xy(): return lax.ppermute(block, ('y', 'x'), pairs)]
    ppermute x12, starting transfers between devices: 16.2 us -> 17.9 us  [around_x(): lax.ppermute(piece, 'x', [(i, (i + shift) % size) for i in range(size)])]
    pallas_call x11 -> x10, Pallas kernels: 25.6 us -> 24.1 us  [run(): pl.pallas_call(body, out_shape=[jax.ShapeDtypeStruct(shape, kind) for sha...]
  transfers between devices with their start and end apart: 24 -> 24, of which waited for: 13 -> 12; matrix products, arithmetic and copies ran while one was open for 2% -> 2% of each run, Pallas kernels for 15% -> 16%
where the time goes in v4:
time: 145 us; the launch traced here: 144 us
  starting transfers between devices  68.4 us (47%)
  waiting for transfers between devices  32.2 us (22%)
  Pallas kernels  29 us (20%)
  local copies, waits for them, and re-layouts  9.68 us (7%)
  between operations  2.28 us (2%)
  other arithmetic  2.23 us (2%)
    all_to_all x4, starting transfers between devices, exchange(): return lax.all_to_all(payload, axes, 0, 0, tiled=True)  39.3 us
    pallas_call x10, Pallas kernels, run(): pl.pallas_call(body, out_shape=[jax.ShapeDtypeStruct(shape, kind) for sha...  24.1 us
    ppermute x12, starting transfers between devices, around_x(): lax.ppermute(piece, 'x', [(i, (i + shift) % size) for i in range(size)])  17.9 us
    all_to_all x4, waiting for transfers between devices, exchange(): return lax.all_to_all(payload, axes, 0, 0, tiled=True)  14.5 us
    ppermute x12, waiting for transfers between devices, around_x(): lax.ppermute(piece, 'x', [(i, (i + shift) % size) for i in range(size)])  12.9 us
    ppermute x2, starting transfers between devices, swap_xy(): return lax.ppermute(block, ('y', 'x'), pairs)  9.36 us
    unnamed x32, local copies, waits for them, and re-layouts  6.77 us
    pallas_call x1, Pallas kernels, run(): pl.pallas_call(staged, out_shape=made, in_specs=[pl.BlockSpec(memory_spac...  5 us
  transfers between devices with their start and end apart: 24, of which 12 were waited for; matrix products, arithmetic and copies ran while one was open for 2% of the time, Pallas kernels for 16%

profile of v4, /device:TPU:16, one launch (start us, length us, event | category | flops | bytes accessed | tf_op | source)
XLA Modules:
  0.0 143.9 jit_solution(4482508212623578699)
XLA Ops:
  0.6 0.9 dynamic-slice_bitcast_fusion.3
  1.5 0.8 dynamic-slice_bitcast_fusion.5
  2.4 0.7 collective-permute-start
  3.0 4.7 %collective-permute-start.7 = (bf16[6,1536]{1,0:T(8,128)(2,1)}, bf16[6,1536]{1,0:T(8,128)(2,1)S(1)}, u32[]{:S(2)}, u32[]{:S(2)}) collective-permute-start(bf16[6,1536]{1,0:T(8,128)(2,1)} %param.12), channel_id=1, source_target_pairs={{0,0},{1,64},{2,128},{3,192},{64,1},{65,65},{66,129},{67,193},{128... | collective-permute-start | bytes 55304 | tf_op jit(solution)/shard_map/ppermute | solution.py:345
  7.8 1.1 dynamic-slice_bitcast_fusion
  8.9 0.0 collective-permute-done
  8.9 0.1 collective-permute-start.2
  9.1 5.9 %collective-permute-start.3 = (bf16[160,384]{1,0:T(8,128)(2,1)S(1)}, bf16[160,384]{1,0:T(8,128)(2,1)S(1)}, u32[]{:S(2)}, u32[]{:S(2)}) collective-permute-start(bf16[160,384]{1,0:T(8,128)(2,1)S(1)} %pad_maximum_fusion.5), channel_id=1, source_target_pairs={{0,3},{1,0},{2,1},{3,2},{4,7},{5,4},{6,5},{7,6},{8,11},{9,8},{10,9... | collective-permute-start | bytes 368648 | tf_op jit(solution)/shard_map/ppermute | solution.py:336
  15.0 0.9 collective-permute-start.1
  15.9 1.6 %shard_map.104 = bf16[768,384]{1,0:T(8,128)(2,1)} custom-call(bf16[6,1536]{1,0:T(8,128)(2,1)S(1)} %collective-permute-done.7.row_block), custom_call_target="tpu_custom_call" | custom-call | flops 1000000000 | bytes 1000 | tf_op jit(solution)/shard_map/pallas_call | solution.py:37
  17.5 0.0 collective-permute-done.2.third
  17.5 3.0 %collective-permute-done.3.fourth = bf16[160,384]{1,0:T(8,128)(2,1)S(1)} collective-permute-done((bf16[160,384]{1,0:T(8,128)(2,1)S(1)}, bf16[160,384]{1,0:T(8,128)(2,1)S(1)}, u32[]{:S(2)}, u32[]{:S(2)}) %collective-permute-start.3) | collective-permute-done | bytes 122912 | tf_op jit(solution)/shard_map/ppermute | solution.py:336
  20.5 0.6 collective-permute-done.1.second
  21.1 12.3 %all-to-all-start.1 = ((bf16[32,24,384]{2,1,0:T(8,128)(2,1)}), bf16[32,24,384]{2,1,0:T(8,128)(2,1)S(1)}, u32[]{:S(2)}, u32[]{:S(2)}) async-start(bf16[32,24,384]{2,1,0:T(8,128)(2,1)} %bitcast.11), calls=%async_computation.1 | async-start | bytes 1179648 | tf_op jit(solution)/shard_map/all_to_all | solution.py:358
  34.7 0.1 stack.19.facts.refs_0_
  34.9 0.1 collective-permute-start.4
  35.0 2.6 %collective-permute-start.5 = (bf16[144,1536]{1,0:T(8,128)(2,1)S(1)}, bf16[144,1536]{1,0:T(8,128)(2,1)}, u32[]{:S(2)}, u32[]{:S(2)}) collective-permute-start(bf16[144,1536]{1,0:T(8,128)(2,1)S(1)} %pad_maximum_fusion.first), channel_id=1, source_target_pairs={{0,2},{1,3},{2,0},{3,1},{4,6},{5,7},{6,4},{7,5},{8,10},{9,11},{10,... | collective-permute-start | bytes 1327112 | tf_op jit(solution)/shard_map/ppermute | solution.py:336
  37.6 1.2 collective-permute-start.6
  38.8 4.9 %shard_map.103 = (f32[544,384]{1,0:T(8,128)S(1)}, f32[64,8,128]{2,1,0:T(8,128)}) custom-call(s32[6]{0:T(128)S(1)} %stack.19.facts.refs_0_, bf16[160,384]{1,0:T(8,128)(2,1)S(1)} %pad_maximum_fusion.2.first, bf16[160,384]{1,0:T(8,128)(2,1)S(1)} %collective-permute-done.1.second, bf16[160,384]{1,0:T(8,128)(2,1)S(1)} %collective-permute-done.2.third, ...), custom_call_target="tpu_custom_call" | custom-call | flops 5000000000 | bytes 1000 | tf_op jit(solution)/shard_map/pallas_call | solution.py:37
  43.7 0.9 copy-done.13
  44.6 6.0 %all-to-all-done.1 = bf16[32,24,384]{2,1,0:T(8,128)(2,1)S(1)} async-done(((bf16[32,24,384]{2,1,0:T(8,128)(2,1)}), bf16[32,24,384]{2,1,0:T(8,128)(2,1)S(1)}, u32[]{:S(2)}, u32[]{:S(2)}) %all-to-all-start.1) | async-done | bytes 589856 | tf_op jit(solution)/shard_map/all_to_all | solution.py:358
  50.7 1.3 shard_map.105.own_half
  51.9 0.1 collective-permute-start.8
  52.0 4.0 %collective-permute-done.5.third = bf16[144,1536]{1,0:T(8,128)(2,1)} collective-permute-done((bf16[144,1536]{1,0:T(8,128)(2,1)S(1)}, bf16[144,1536]{1,0:T(8,128)(2,1)}, u32[]{:S(2)}, u32[]{:S(2)}) %collective-permute-start.5) | collective-permute-done | bytes 442400 | tf_op jit(solution)/shard_map/ppermute | solution.py:336
  56.1 0.6 collective-permute-done.6.fourth
  56.7 10.2 %all-to-all-start = ((f32[64,8,128]{2,1,0:T(8,128)}), f32[64,8,128]{2,1,0:T(8,128)S(1)}, u32[]{:S(2)}, u32[]{:S(2)}) async-start(f32[64,8,128]{2,1,0:T(8,128)} %get-tuple-element.35), calls=%async_computation | async-start | bytes 524288 | tf_op jit(solution)/shard_map/all_to_all | solution.py:358
  66.9 2.7 %shard_map.106.refs_3_ = f32[560,384]{1,0:T(8,128)S(1)} custom-call(s32[6]{0:T(128)S(1)} %stack.19.facts.refs_0_, bf16[144,1536]{1,0:T(8,128)(2,1)S(1)} %pad_maximum_fusion.first, bf16[144,1536]{1,0:T(8,128)(2,1)S(1)} %collective-permute-done.4.second, bf16[144,1536]{1,0:T(8,128)(2,1)} %collective-permute-done.5.third, ...), custom_call_target="tpu_custom_call" | custom-call | flops 3000000000 | bytes 1000 | tf_op jit(solution)/shard_map/pallas_call | solution.py:37
  69.6 0.9 copy-done.10
  70.5 7.3 %all-to-all-done.refs_1_.gathered = f32[64,8,128]{2,1,0:T(8,128)S(1)} async-done(((f32[64,8,128]{2,1,0:T(8,128)}), f32[64,8,128]{2,1,0:T(8,128)S(1)}, u32[]{:S(2)}, u32[]{:S(2)}) %all-to-all-start) | async-done | bytes 262176 | tf_op jit(solution)/shard_map/all_to_all | solution.py:358
  77.8 0.7 copy-done
  78.6 5.0 %shard_map.107 = (bf16[512,192]{1,0:T(8,128)(2,1)}, bf16[512,192]{1,0:T(8,128)(2,1)}, f32[544,384]{1,0:T(8,128)}, f32[544,384]{1,0:T(8,128)}, f32[8,128]{1,0:T(8,128)}, /*index=5*/f32[64,8,128]{2,1,0:T(8,128)}) custom-call(s32[6]{0:T(128)} %copy-done.2, f32[64,8,128]{2,1,0:T(8,128)} %copy-done, f32[544,384]{1,0:T(8,128)} %copy-done.13, ...), custom_call_target="tpu_custom_call" | custom-call | flops 2000000000 | bytes 1000 | tf_op jit(solution)/shard_map/pallas_call | solution.py:76
  83.6 6.9 %all-to-all-start.2 = ((f32[64,8,128]{2,1,0:T(8,128)}), f32[64,8,128]{2,1,0:T(8,128)S(1)}, u32[]{:S(2)}, u32[]{:S(2)}) async-start(f32[64,8,128]{2,1,0:T(8,128)} %get-tuple-element.43), calls=%async_computation.2 | async-start | bytes 524288 | tf_op jit(solution)/shard_map/all_to_all | solution.py:358
  90.5 0.9 copy-done.6
  91.5 0.9 copy-done.8
  92.4 2.3 %shard_map.108 = (f32[128,1536]{1,0:T(8,128)S(1)}, bf16[128,1536]{1,0:T(8,128)(2,1)S(1)}, bf16[128,1536]{1,0:T(8,128)(2,1)}, bf16[128,1536]{1,0:T(8,128)(2,1)}) custom-call(s32[6]{0:T(128)S(1)} %copy-done.3, bf16[512,192]{1,0:T(8,128)(2,1)S(1)} %copy-done.6, bf16[512,192]{1,0:T(8,128)(2,1)S(1)} %copy-done.8, bf16[192,1536]{1,0:T(8,128)(2,1)S(1)} %shard_map.105.own_half, ...), custom_call_target="tpu_custom_call" | custom-call | flops 1000000000 | bytes 1000 | tf_op jit(solution)/shard_map/pallas_call | solution.py:37
  94.7 2.6 %shard_map.110 = (f32[192,1536]{1,0:T(8,128)S(1)}, bf16[48,1536]{1,0:T(8,128)(2,1)S(1)}, bf16[48,1536]{1,0:T(8,128)(2,1)S(1)}, bf16[48,1536]{1,0:T(8,128)(2,1)S(1)}, bf16[48,1536]{1,0:T(8,128)(2,1)S(1)}) custom-call(s32[6]{0:T(128)S(1)} %copy-done.3, bf16[512,192]{1,0:T(8,128)(2,1)S(1)} %copy-done.7, bf16[512,192]{1,0:T(8,128)(2,1)S(1)} %copy-done.9, ...), custom_call_target="tpu_custom_call" | custom-call | flops 1000000000 | bytes 1000 | tf_op jit(solution)/shard_map/pallas_call | solution.py:37
  97.2 0.3 collective-permute-start.12
  97.6 0.3 collective-permute-start.13
  97.8 0.9 collective-permute-start.10
  98.7 2.0 %collective-permute-start.11 = (bf16[128,1536]{1,0:T(8,128)(2,1)}, bf16[128,1536]{1,0:T(8,128)(2,1)}, u32[]{:S(2)}, u32[]{:S(2)}) collective-permute-start(bf16[128,1536]{1,0:T(8,128)(2,1)} %get-tuple-element.45), channel_id=1, source_target_pairs={{0,3},{1,0},{2,1},{3,2},{4,7},{5,4},{6,5},{7,6},{8,11},{9,8},{10,9... | collective-permute-start | bytes 1179656 | tf_op jit(solution)/shard_map/ppermute | solution.py:336
  100.8 0.3 collective-permute-start.9
  101.1 0.0 collective-permute-done.13.second
  101.1 0.5 collective-permute-start.15
  101.6 0.9 collective-permute-done.14.third
  102.4 0.2 collective-permute-done.15.fourth
  102.6 2.1 %shard_map.111 = bf16[768,384]{1,0:T(8,128)(2,1)} custom-call(f32[192,1536]{1,0:T(8,128)S(1)} %get-tuple-element.58.kept, bf16[48,1536]{1,0:T(8,128)(2,1)S(1)} %collective-permute-done.12.first, bf16[48,1536]{1,0:T(8,128)(2,1)S(1)} %collective-permute-done.13.second, bf16[48,1536]{1,0:T(8,128)(2,1)S(1)} %collective-permute-done.14.third, ...), custom_call_target="tpu_custom_call" | custom-call | flops 1000000000 | bytes 1000 | tf_op jit(solution)/shard_map/pallas_call | solution.py:37
  104.8 9.9 %all-to-all-start.3 = ((bf16[32,24,384]{2,1,0:T(8,128)(2,1)}), bf16[32,24,384]{2,1,0:T(8,128)(2,1)S(1)}, u32[]{:S(2)}, u32[]{:S(2)}) async-start(bf16[32,24,384]{2,1,0:T(8,128)(2,1)} %bitcast.14), calls=%async_computation.3 | async-start | bytes 1179648 | tf_op jit(solution)/shard_map/all_to_all | solution.py:358
  114.7 0.0 collective-permute-done.10
  114.7 4.3 %collective-permute-done.11 = bf16[128,1536]{1,0:T(8,128)(2,1)} collective-permute-done((bf16[128,1536]{1,0:T(8,128)(2,1)}, bf16[128,1536]{1,0:T(8,128)(2,1)}, u32[]{:S(2)}, u32[]{:S(2)}) %collective-permute-start.11) | collective-permute-done | bytes 393248 | tf_op jit(solution)/shard_map/ppermute | solution.py:336
  119.1 0.3 collective-permute-done.9
  119.4 1.1 copy-done.11
  120.5 1.1 copy-done.12
  121.7 4.7 %shard_map.109 = (bf16[128,384]{1,0:T(8,128)(2,1)S(1)}, bf16[128,384]{1,0:T(8,128)(2,1)S(1)}, bf16[128,384]{1,0:T(8,128)(2,1)S(1)}, bf16[128,384]{1,0:T(8,128)(2,1)S(1)}) custom-call(s32[6]{0:T(128)S(1)} %copy-done.3, f32[64,8,128]{2,1,0:T(8,128)S(1)} %copy-done.1, f32[64,8,128]{2,1,0:T(8,128)S(1)} %all-to-all-done.2.sums, f32[544,384]{1,0:T(8,128)S(1)} %copy-done.11, ...), custom_call_target="tpu_custom_call" | custom-call | flops 5000000000 | bytes 1000 | tf_op jit(solution)/shard_map/pallas_call | solution.py:37
  126.3 0.3 collective-permute-start.17
  126.6 3.6 %collective-permute-start.18 = (bf16[128,384]{1,0:T(8,128)(2,1)S(1)}, bf16[128,384]{1,0:T(8,128)(2,1)S(1)}, u32[]{:S(2)}, u32[]{:S(2)}) collective-permute-start(bf16[128,384]{1,0:T(8,128)(2,1)S(1)} %get-tuple-element.52), channel_id=1, source_target_pairs={{0,2},{1,3},{2,0},{3,1},{4,6},{5,7},{6,4},{7,5},{8,10},{9,11},{10,... | collective-permute-start | bytes 294920 | tf_op jit(solution)/shard_map/ppermute | solution.py:336
  130.2 0.0 collective-permute-start.19
  130.2 2.0 %fusion = bf16[1,128,1536]{2,1,0:T(8,128)(2,1)} fusion(bf16[128,1536]{1,0:T(8,128)(2,1)} %collective-permute-done.11, bf16[128,1536]{1,0:T(8,128)(2,1)S(1)} %collective-permute-done.10, f32[128,1536]{1,0:T(8,128)S(1)} %get-tuple-element.41, bf16[128,1536]{1,0:T(8,128)(2,1)} %collective-permute-done.9), kind=kLoop, calls=%fused_computation.3 | loop fusion | flops 1376256 | bytes 2359296 | tf_op jit(solution)/shard_map/broadcast_in_dim | solution.py:439
  132.3 1.1 all-to-all-done.3
  133.4 0.1 convert_reduce_fusion
  133.5 4.7 %collective-permute-start.16 = (f32[24,384]{1,0:T(8,128)S(1)}, f32[24,384]{1,0:T(8,128)S(1)}, u32[]{:S(2)}, u32[]{:S(2)}) collective-permute-start(f32[24,384]{1,0:T(8,128)S(1)} %convert_reduce_fusion), channel_id=1, source_target_pairs={{0,0},{1,64},{2,128},{3,192},{64,1},{65,65},{66,129},{67,193},{128... | collective-permute-start | bytes 110600 | tf_op jit(solution)/shard_map/ppermute | solution.py:345
  138.2 0.0 collective-permute-done.18.third
  138.2 1.3 shard_map.113
  139.5 3.7 %collective-permute-done.16.sums = f32[24,384]{1,0:T(8,128)S(1)} collective-permute-done((f32[24,384]{1,0:T(8,128)S(1)}, f32[24,384]{1,0:T(8,128)S(1)}, u32[]{:S(2)}, u32[]{:S(2)}) %collective-permute-start.16) | collective-permute-done | bytes 36896 | tf_op jit(solution)/shard_map/ppermute | solution.py:345
  143.3 0.6 shard_map.112
  (41 shorter events, 0.2 us)
Async XLA Ops:
  2.4 6.5 %collective-permute-start = (bf16[48,1536]{1,0:T(8,128)(2,1)S(1)}, bf16[48,1536]{1,0:T(8,128)(2,1)S(1)}, u32[]{:S(2)}, u32[]{:S(2)}) collective-permute-start(bf16[48,1536]{1,0:T(8,128)(2,1)S(1)} %pad_maximum_fusion.1), channel_id=1, source_target_pairs={{3,4},{7,8},{11,12},{15,16},{19,20},{23,24},{27,28},{4,3},{8,7},{1... | collective-permute-start | bytes 442376 | tf_op jit(solution)/shard_map/ppermute | solution.py:354
  3.0 12.9 %collective-permute-start.7 = (bf16[6,1536]{1,0:T(8,128)(2,1)}, bf16[6,1536]{1,0:T(8,128)(2,1)S(1)}, u32[]{:S(2)}, u32[]{:S(2)}) collective-permute-start(bf16[6,1536]{1,0:T(8,128)(2,1)} %param.12), channel_id=1, source_target_pairs={{0,0},{1,64},{2,128},{3,192},{64,1},{65,65},{66,129},{67,193},{128... | collective-permute-start | bytes 55304 | tf_op jit(solution)/shard_map/ppermute | solution.py:345
  8.9 8.6 %collective-permute-start.2 = (bf16[160,384]{1,0:T(8,128)(2,1)S(1)}, bf16[160,384]{1,0:T(8,128)(2,1)S(1)}, u32[]{:S(2)}, u32[]{:S(2)}) collective-permute-start(bf16[160,384]{1,0:T(8,128)(2,1)S(1)} %pad_maximum_fusion.4), channel_id=1, source_target_pairs={{0,2},{1,3},{2,0},{3,1},{4,6},{5,7},{6,4},{7,5},{8,10},{9,11},{10,... | collective-permute-start | bytes 368648 | tf_op jit(solution)/shard_map/ppermute | solution.py:336
  9.1 11.5 %collective-permute-start.3 = (bf16[160,384]{1,0:T(8,128)(2,1)S(1)}, bf16[160,384]{1,0:T(8,128)(2,1)S(1)}, u32[]{:S(2)}, u32[]{:S(2)}) collective-permute-start(bf16[160,384]{1,0:T(8,128)(2,1)S(1)} %pad_maximum_fusion.5), channel_id=1, source_target_pairs={{0,3},{1,0},{2,1},{3,2},{4,7},{5,4},{6,5},{7,6},{8,11},{9,8},{10,9... | collective-permute-start | bytes 368648 | tf_op jit(solution)/shard_map/ppermute | solution.py:336
  15.0 6.2 %collective-permute-start.1 = (bf16[160,384]{1,0:T(8,128)(2,1)S(1)}, bf16[160,384]{1,0:T(8,128)(2,1)S(1)}, u32[]{:S(2)}, u32[]{:S(2)}) collective-permute-start(bf16[160,384]{1,0:T(8,128)(2,1)S(1)} %pad_maximum_fusion.3), channel_id=1, source_target_pairs={{0,1},{1,2},{2,3},{3,0},{4,5},{5,6},{6,7},{7,4},{8,9},{9,10},{10,1... | collective-permute-start | bytes 368648 | tf_op jit(solution)/shard_map/ppermute | solution.py:336
  17.5 17.4 %copy-start.15 = (bf16[1,128,1536]{2,1,0:T(8,128)(2,1)S(1)}, bf16[1,128,1536]{2,1,0:T(8,128)(2,1)}, u32[]{:S(2)}) copy-start(bf16[1,128,1536]{2,1,0:T(8,128)(2,1)} %param.13) | copy-start | bytes 1179652
  17.5 21.3 %copy-start.4 = (f32[32,1536]{1,0:T(8,128)S(1)}, f32[32,1536]{1,0:T(8,128)}, u32[]{:S(2)}) copy-start(f32[32,1536]{1,0:T(8,128)} %weights.3) | copy-start | bytes 589828
  21.1 29.5 %all-to-all-start.1 = ((bf16[32,24,384]{2,1,0:T(8,128)(2,1)}), bf16[32,24,384]{2,1,0:T(8,128)(2,1)S(1)}, u32[]{:S(2)}, u32[]{:S(2)}) async-start(bf16[32,24,384]{2,1,0:T(8,128)(2,1)} %bitcast.11), calls=%async_computation.1 | async-start | bytes 1179648 | tf_op jit(solution)/shard_map/all_to_all | solution.py:358
  34.8 32.1 %copy-start.2 = (s32[6]{0:T(128)}, s32[6]{0:T(128)S(1)}, u32[]{:S(2)}) copy-start(s32[6]{0:T(128)S(1)} %stack.19.facts.refs_0_) | copy-start | bytes 76
  34.9 17.2 %collective-permute-start.4 = (bf16[144,1536]{1,0:T(8,128)(2,1)S(1)}, bf16[144,1536]{1,0:T(8,128)(2,1)S(1)}, u32[]{:S(2)}, u32[]{:S(2)}) collective-permute-start(bf16[144,1536]{1,0:T(8,128)(2,1)S(1)} %pad_maximum_fusion.first), channel_id=1, source_target_pairs={{0,1},{1,2},{2,3},{3,0},{4,5},{5,6},{6,7},{7,4},{8,9},{9,10},{10,1... | collective-permute-start | bytes 1327112 | tf_op jit(solution)/shard_map/ppermute | solution.py:336
  35.0 21.1 %collective-permute-start.5 = (bf16[144,1536]{1,0:T(8,128)(2,1)S(1)}, bf16[144,1536]{1,0:T(8,128)(2,1)}, u32[]{:S(2)}, u32[]{:S(2)}) collective-permute-start(bf16[144,1536]{1,0:T(8,128)(2,1)S(1)} %pad_maximum_fusion.first), channel_id=1, source_target_pairs={{0,2},{1,3},{2,0},{3,1},{4,6},{5,7},{6,4},{7,5},{8,10},{9,11},{10,... | collective-permute-start | bytes 1327112 | tf_op jit(solution)/shard_map/ppermute | solution.py:336
  37.6 19.1 %collective-permute-start.6 = (bf16[144,1536]{1,0:T(8,128)(2,1)S(1)}, bf16[144,1536]{1,0:T(8,128)(2,1)}, u32[]{:S(2)}, u32[]{:S(2)}) collective-permute-start(bf16[144,1536]{1,0:T(8,128)(2,1)S(1)} %pad_maximum_fusion.first), channel_id=1, source_target_pairs={{0,3},{1,0},{2,1},{3,2},{4,7},{5,4},{6,5},{7,6},{8,11},{9,8},{10,9... | collective-permute-start | bytes 1327112 | tf_op jit(solution)/shard_map/ppermute | solution.py:336
  43.7 0.9 copy-start.13
  51.9 15.0 %collective-permute-start.8 = (bf16[192,1536]{1,0:T(8,128)(2,1)S(1)}, bf16[192,1536]{1,0:T(8,128)(2,1)S(1)}, u32[]{:S(2)}, u32[]{:S(2)}) collective-permute-start(bf16[192,1536]{1,0:T(8,128)(2,1)S(1)} %shard_map.105.own_half), channel_id=1, source_target_pairs={{0,32},{32,0},{1,33},{33,1},{2,34},{34,2},{3,35},{35,3},{4,36},{36... | collective-permute-start | bytes 1769480 | tf_op jit(solution)/shard_map/ppermute | solution.py:340
  56.7 21.1 %all-to-all-start = ((f32[64,8,128]{2,1,0:T(8,128)}), f32[64,8,128]{2,1,0:T(8,128)S(1)}, u32[]{:S(2)}, u32[]{:S(2)}) async-start(f32[64,8,128]{2,1,0:T(8,128)} %get-tuple-element.35), calls=%async_computation | async-start | bytes 524288 | tf_op jit(solution)/shard_map/all_to_all | solution.py:358
  69.6 0.9 copy-start.10
  77.8 0.7 copy-start
  78.6 11.9 %copy-start.3 = (s32[6]{0:T(128)S(1)}, s32[6]{0:T(128)}, u32[]{:S(2)}) copy-start(s32[6]{0:T(128)} %copy-done.2) | copy-start | bytes 76
  83.6 21.2 %all-to-all-start.2 = ((f32[64,8,128]{2,1,0:T(8,128)}), f32[64,8,128]{2,1,0:T(8,128)S(1)}, u32[]{:S(2)}, u32[]{:S(2)}) async-start(f32[64,8,128]{2,1,0:T(8,128)} %get-tuple-element.43), calls=%async_computation.2 | async-start | bytes 524288 | tf_op jit(solution)/shard_map/all_to_all | solution.py:358
  90.5 1.0 copy-start.6
  91.5 0.9 copy-start.8
  92.4 2.3 %copy-start.7 = (bf16[512,192]{1,0:T(8,128)(2,1)S(1)}, bf16[512,192]{1,0:T(8,128)(2,1)}, u32[]{:S(2)}) copy-start(bf16[512,192]{1,0:T(8,128)(2,1)} %get-tuple-element.57.mine) | copy-start | bytes 589828
  92.4 2.3 %copy-start.9 = (bf16[512,192]{1,0:T(8,128)(2,1)S(1)}, bf16[512,192]{1,0:T(8,128)(2,1)}, u32[]{:S(2)}) copy-start(bf16[512,192]{1,0:T(8,128)(2,1)} %get-tuple-element.40.theirs) | copy-start | bytes 589828
  97.2 3.8 %collective-permute-start.12 = (bf16[48,1536]{1,0:T(8,128)(2,1)S(1)}, bf16[48,1536]{1,0:T(8,128)(2,1)S(1)}, u32[]{:S(2)}, u32[]{:S(2)}) collective-permute-start(bf16[48,1536]{1,0:T(8,128)(2,1)S(1)} %get-tuple-element.59), channel_id=1, source_target_pairs={{0,32},{32,0},{1,33},{33,1},{2,34},{34,2},{3,35},{35,3},{4,36},{36... | collective-permute-start | bytes 442376 | tf_op jit(solution)/shard_map/ppermute | solution.py:340
  97.6 3.5 %collective-permute-start.13 = (bf16[48,1536]{1,0:T(8,128)(2,1)S(1)}, bf16[48,1536]{1,0:T(8,128)(2,1)S(1)}, u32[]{:S(2)}, u32[]{:S(2)}) collective-permute-start(bf16[48,1536]{1,0:T(8,128)(2,1)S(1)} %get-tuple-element.60), channel_id=1, source_target_pairs={{0,32},{32,0},{1,33},{33,1},{2,34},{34,2},{3,35},{35,3},{4,36},{36... | collective-permute-start | bytes 442376 | tf_op jit(solution)/shard_map/ppermute | solution.py:340
  97.8 16.9 %collective-permute-start.10 = (bf16[128,1536]{1,0:T(8,128)(2,1)}, bf16[128,1536]{1,0:T(8,128)(2,1)S(1)}, u32[]{:S(2)}, u32[]{:S(2)}) collective-permute-start(bf16[128,1536]{1,0:T(8,128)(2,1)} %get-tuple-element.44), channel_id=1, source_target_pairs={{0,2},{1,3},{2,0},{3,1},{4,6},{5,7},{6,4},{7,5},{8,10},{9,11},{10,... | collective-permute-start | bytes 1179656 | tf_op jit(solution)/shard_map/ppermute | solution.py:336
  98.7 20.3 %collective-permute-start.11 = (bf16[128,1536]{1,0:T(8,128)(2,1)}, bf16[128,1536]{1,0:T(8,128)(2,1)}, u32[]{:S(2)}, u32[]{:S(2)}) collective-permute-start(bf16[128,1536]{1,0:T(8,128)(2,1)} %get-tuple-element.45), channel_id=1, source_target_pairs={{0,3},{1,0},{2,1},{3,2},{4,7},{5,4},{6,5},{7,6},{8,11},{9,8},{10,9... | collective-permute-start | bytes 1179656 | tf_op jit(solution)/shard_map/ppermute | solution.py:336
  100.8 18.6 %collective-permute-start.9 = (bf16[128,1536]{1,0:T(8,128)(2,1)S(1)}, bf16[128,1536]{1,0:T(8,128)(2,1)}, u32[]{:S(2)}, u32[]{:S(2)}) collective-permute-start(bf16[128,1536]{1,0:T(8,128)(2,1)S(1)} %get-tuple-element.42), channel_id=1, source_target_pairs={{0,1},{1,2},{2,3},{3,0},{4,5},{5,6},{6,7},{7,4},{8,9},{9,10},{10,1... | collective-permute-start | bytes 1179656 | tf_op jit(solution)/shard_map/ppermute | solution.py:336
  101.1 1.4 collective-permute-start.14
  101.1 1.6 %collective-permute-start.15 = (bf16[48,1536]{1,0:T(8,128)(2,1)S(1)}, bf16[48,1536]{1,0:T(8,128)(2,1)S(1)}, u32[]{:S(2)}, u32[]{:S(2)}) collective-permute-start(bf16[48,1536]{1,0:T(8,128)(2,1)S(1)} %get-tuple-element.62), channel_id=1, source_target_pairs={{0,32},{32,0},{1,33},{33,1},{2,34},{34,2},{3,35},{35,3},{4,36},{36... | collective-permute-start | bytes 442376 | tf_op jit(solution)/shard_map/ppermute | solution.py:340
  104.8 14.6 %copy-start.1 = (f32[64,8,128]{2,1,0:T(8,128)S(1)}, f32[64,8,128]{2,1,0:T(8,128)}, u32[]{:S(2)}) copy-start(f32[64,8,128]{2,1,0:T(8,128)} %copy-done) | copy-start | bytes 786436
  104.8 14.6 %copy-start.5 = (f32[32,1536]{1,0:T(8,128)S(1)}, f32[32,1536]{1,0:T(8,128)}, u32[]{:S(2)}) copy-start(f32[32,1536]{1,0:T(8,128)} %weights.3) | copy-start | bytes 589828
  104.8 14.6 %copy-start.14 = (f32[8,128]{1,0:T(8,128)S(1)}, f32[8,128]{1,0:T(8,128)}, u32[]{:S(2)}) copy-start(f32[8,128]{1,0:T(8,128)} %get-tuple-element.49.inverses) | copy-start | bytes 12292
  104.8 28.6 %all-to-all-start.3 = ((bf16[32,24,384]{2,1,0:T(8,128)(2,1)}), bf16[32,24,384]{2,1,0:T(8,128)(2,1)S(1)}, u32[]{:S(2)}, u32[]{:S(2)}) async-start(bf16[32,24,384]{2,1,0:T(8,128)(2,1)} %bitcast.14), calls=%async_computation.3 | async-start | bytes 1179648 | tf_op jit(solution)/shard_map/all_to_all | solution.py:358
  119.4 1.2 copy-start.11
  120.5 1.1 copy-start.12
  126.3 11.8 %collective-permute-start.17 = (bf16[128,384]{1,0:T(8,128)(2,1)S(1)}, bf16[128,384]{1,0:T(8,128)(2,1)S(1)}, u32[]{:S(2)}, u32[]{:S(2)}) collective-permute-start(bf16[128,384]{1,0:T(8,128)(2,1)S(1)} %get-tuple-element.51), channel_id=1, source_target_pairs={{0,1},{1,2},{2,3},{3,0},{4,5},{5,6},{6,7},{7,4},{8,9},{9,10},{10,1... | collective-permute-start | bytes 294920 | tf_op jit(solution)/shard_map/ppermute | solution.py:336
  126.6 11.6 %collective-permute-start.18 = (bf16[128,384]{1,0:T(8,128)(2,1)S(1)}, bf16[128,384]{1,0:T(8,128)(2,1)S(1)}, u32[]{:S(2)}, u32[]{:S(2)}) collective-permute-start(bf16[128,384]{1,0:T(8,128)(2,1)S(1)} %get-tuple-element.52), channel_id=1, source_target_pairs={{0,2},{1,3},{2,0},{3,1},{4,6},{5,7},{6,4},{7,5},{8,10},{9,11},{10,... | collective-permute-start | bytes 294920 | tf_op jit(solution)/shard_map/ppermute | solution.py:336
  130.2 8.0 %collective-permute-start.19 = (bf16[128,384]{1,0:T(8,128)(2,1)S(1)}, bf16[128,384]{1,0:T(8,128)(2,1)S(1)}, u32[]{:S(2)}, u32[]{:S(2)}) collective-permute-start(bf16[128,384]{1,0:T(8,128)(2,1)S(1)} %get-tuple-element.53), channel_id=1, source_target_pairs={{0,3},{1,0},{2,1},{3,2},{4,7},{5,4},{6,5},{7,6},{8,11},{9,8},{10,9... | collective-permute-start | bytes 294920 | tf_op jit(solution)/shard_map/ppermute | solution.py:336
  133.5 9.8 %collective-permute-start.16 = (f32[24,384]{1,0:T(8,128)S(1)}, f32[24,384]{1,0:T(8,128)S(1)}, u32[]{:S(2)}, u32[]{:S(2)}) collective-permute-start(f32[24,384]{1,0:T(8,128)S(1)} %convert_reduce_fusion), channel_id=1, source_target_pairs={{0,0},{1,64},{2,128},{3,192},{64,1},{65,65},{66,129},{67,193},{128... | collective-permute-start | bytes 110600 | tf_op jit(solution)/shard_map/ppermute | solution.py:345

commit v5 on v4

--- a/solution.py
+++ b/solution.py
@@ -412,7 +412,7 @@
     )(facts, gathered, convolved, back, bn_gain, bn_bias)
     sums = exchange(payload, STATS)
 
-    output, *others = call(out_body, [((OWN, CHANNELS), F32)] + [((OWN, CHANNELS), BF16)] * (PARTS - 1))(
+    output, *others = call(out_body, [((OWN, CHANNELS), F32)] + [((OWN, CHANNELS), BF16)] * (PARTS - 1), cost=1)(
         facts, kept, sent, half, other_half
     )
     arrived = [around_x(piece, k + 1) for k, piece in enumerate(others)]
@@ -429,13 +429,13 @@
         grad_body,
         [((OWN, BLOCK), BF16)] * PARTS,
         [pltpu.VMEM((WIDE, BLOCK), F32), pltpu.VMEM((FRAMES, BLOCK), F32)],
-        cost=5,
+        cost=12,
     )(facts, gathered, wait_for(sums, *arrived), normed, grad, inverses, conv_weight)
-    for piece in arrived:
-        output = output + wait_for(piece, *pieces).astype(F32)
-    output = output.astype(BF16)
     pieces = [pieces[0]] + [around_x(pieces[k], k) for k in range(1, PARTS)]
     (input_grad,) = call(lanes_body, [((OWN, CHANNELS), BF16)])(facts, *pieces)
+    for piece in arrived:
+        output = output + wait_for(piece, input_grad).astype(F32)
+    output = output.astype(BF16)
     return output[None], weight_grad, input_grad[None]
 
 

time: 145 us -> 148 us (1.021)
    ppermute x12, waiting for transfers between devices: 12.9 us -> 15.1 us  [around_x(): lax.ppermute(piece, 'x', [(i, (i + shift) % size) for i in range(size)])]
    all_to_all x4, waiting for transfers between devices: 14.5 us -> 13 us  [exchange(): return lax.all_to_all(payload, axes, 0, 0, tiled=True)]
    unnamed x32 -> x30, local copies, waits for them, and re-layouts: 6.77 us -> 6.75 us
  transfers between devices with their start and end apart: 24 -> 24, of which waited for: 12 -> 15; matrix products, arithmetic and copies ran while one was open for 2% -> 2% of each run, Pallas kernels for 16% -> 16%
where the time goes in v5:
time: 148 us; the launch traced here: 146 us
  starting transfers between devices  69 us (47%)
  waiting for transfers between devices  33.3 us (22%)
  Pallas kernels  29.1 us (20%)
  local copies, waits for them, and re-layouts  9.66 us (7%)
  other arithmetic  2.34 us (2%)
  between operations  2.25 us (2%)
    all_to_all x4, starting transfers between devices, exchange(): return lax.all_to_all(payload, axes, 0, 0, tiled=True)  39.3 us
    pallas_call x10, Pallas kernels, run(): pl.pallas_call(body, out_shape=[jax.ShapeDtypeStruct(shape, kind) for sha...  24 us
    ppermute x12, starting transfers between devices, around_x(): lax.ppermute(piece, 'x', [(i, (i + shift) % size) for i in range(size)])  18.9 us
    ppermute x12, waiting for transfers between devices, around_x(): lax.ppermute(piece, 'x', [(i, (i + shift) % size) for i in range(size)])  15.1 us
    all_to_all x4, waiting for transfers between devices, exchange(): return lax.all_to_all(payload, axes, 0, 0, tiled=True)  13 us
    ppermute x2, starting transfers between devices, swap_xy(): return lax.ppermute(block, ('y', 'x'), pairs)  9.06 us
    unnamed x30, local copies, waits for them, and re-layouts  6.75 us
    pallas_call x1, Pallas kernels, run(): pl.pallas_call(staged, out_shape=made, in_specs=[pl.BlockSpec(memory_spac...  5.02 us
  transfers between devices with their start and end apart: 24, of which 15 were waited for; matrix products, arithmetic and copies ran while one was open for 2% of the time, Pallas kernels for 16%

profile of v5, /device:TPU:16, one launch (start us, length us, event | category | flops | bytes accessed | tf_op | source)
XLA Modules:
  0.0 145.7 jit_solution(6403430310078972171)
XLA Ops:
  0.6 0.8 dynamic-slice_bitcast_fusion.5
  1.4 0.9 dynamic-slice_bitcast_fusion.3
  2.4 0.7 collective-permute-start
  3.0 4.7 %collective-permute-start.7 = (bf16[6,1536]{1,0:T(8,128)(2,1)}, bf16[6,1536]{1,0:T(8,128)(2,1)S(1)}, u32[]{:S(2)}, u32[]{:S(2)}) collective-permute-start(bf16[6,1536]{1,0:T(8,128)(2,1)} %param.12), channel_id=1, source_target_pairs={{0,0},{1,64},{2,128},{3,192},{64,1},{65,65},{66,129},{67,193},{128... | collective-permute-start | bytes 55304 | tf_op jit(solution)/shard_map/ppermute | solution.py:345
  7.8 1.1 dynamic-slice_bitcast_fusion
  8.9 0.0 collective-permute-done
  8.9 0.1 collective-permute-start.1
  9.1 7.3 %collective-permute-start.2 = (bf16[160,384]{1,0:T(8,128)(2,1)S(1)}, bf16[160,384]{1,0:T(8,128)(2,1)S(1)}, u32[]{:S(2)}, u32[]{:S(2)}) collective-permute-start(bf16[160,384]{1,0:T(8,128)(2,1)S(1)} %pad_maximum_fusion.4), channel_id=1, source_target_pairs={{0,2},{1,3},{2,0},{3,1},{4,6},{5,7},{6,4},{7,5},{8,10},{9,11},{10,... | collective-permute-start | bytes 368648 | tf_op jit(solution)/shard_map/ppermute | solution.py:336
  16.4 0.1 collective-permute-start.3
  16.5 1.6 %shard_map.104 = bf16[768,384]{1,0:T(8,128)(2,1)} custom-call(bf16[6,1536]{1,0:T(8,128)(2,1)S(1)} %collective-permute-done.7.row_block), custom_call_target="tpu_custom_call" | custom-call | flops 1000000000 | bytes 1000 | tf_op jit(solution)/shard_map/pallas_call | solution.py:37
  18.1 0.9 collective-permute-done.1.second
  19.0 2.1 %collective-permute-done.2.third = bf16[160,384]{1,0:T(8,128)(2,1)S(1)} collective-permute-done((bf16[160,384]{1,0:T(8,128)(2,1)S(1)}, bf16[160,384]{1,0:T(8,128)(2,1)S(1)}, u32[]{:S(2)}, u32[]{:S(2)}) %collective-permute-start.2) | collective-permute-done | bytes 122912 | tf_op jit(solution)/shard_map/ppermute | solution.py:336
  21.1 0.3 collective-permute-done.3.fourth
  21.4 12.3 %all-to-all-start.1 = ((bf16[32,24,384]{2,1,0:T(8,128)(2,1)}), bf16[32,24,384]{2,1,0:T(8,128)(2,1)S(1)}, u32[]{:S(2)}, u32[]{:S(2)}) async-start(bf16[32,24,384]{2,1,0:T(8,128)(2,1)} %bitcast.11), calls=%async_computation.1 | async-start | bytes 1179648 | tf_op jit(solution)/shard_map/all_to_all | solution.py:358
  34.9 0.1 stack.19.facts.refs_0_
  35.1 0.6 collective-permute-start.4
  35.6 3.4 %collective-permute-start.5 = (bf16[144,1536]{1,0:T(8,128)(2,1)S(1)}, bf16[144,1536]{1,0:T(8,128)(2,1)}, u32[]{:S(2)}, u32[]{:S(2)}) collective-permute-start(bf16[144,1536]{1,0:T(8,128)(2,1)S(1)} %pad_maximum_fusion.first), channel_id=1, source_target_pairs={{0,2},{1,3},{2,0},{3,1},{4,6},{5,7},{6,4},{7,5},{8,10},{9,11},{10,... | collective-permute-start | bytes 1327112 | tf_op jit(solution)/shard_map/ppermute | solution.py:336
  39.1 0.0 collective-permute-start.6
  39.1 4.9 %shard_map.103 = (f32[544,384]{1,0:T(8,128)S(1)}, f32[64,8,128]{2,1,0:T(8,128)}) custom-call(s32[6]{0:T(128)S(1)} %stack.19.facts.refs_0_, bf16[160,384]{1,0:T(8,128)(2,1)S(1)} %pad_maximum_fusion.2.first, bf16[160,384]{1,0:T(8,128)(2,1)S(1)} %collective-permute-done.1.second, bf16[160,384]{1,0:T(8,128)(2,1)S(1)} %collective-permute-done.2.third, ...), custom_call_target="tpu_custom_call" | custom-call | flops 5000000000 | bytes 1000 | tf_op jit(solution)/shard_map/pallas_call | solution.py:37
  44.0 0.9 copy-done.12
  44.9 4.9 %all-to-all-done.1 = bf16[32,24,384]{2,1,0:T(8,128)(2,1)S(1)} async-done(((bf16[32,24,384]{2,1,0:T(8,128)(2,1)}), bf16[32,24,384]{2,1,0:T(8,128)(2,1)S(1)}, u32[]{:S(2)}, u32[]{:S(2)}) %all-to-all-start.1) | async-done | bytes 589856 | tf_op jit(solution)/shard_map/all_to_all | solution.py:358
  49.8 1.3 shard_map.105.own_half
  51.1 0.1 collective-permute-start.8
  51.2 6.0 %collective-permute-done.5.third = bf16[144,1536]{1,0:T(8,128)(2,1)} collective-permute-done((bf16[144,1536]{1,0:T(8,128)(2,1)S(1)}, bf16[144,1536]{1,0:T(8,128)(2,1)}, u32[]{:S(2)}, u32[]{:S(2)}) %collective-permute-start.5) | collective-permute-done | bytes 442400 | tf_op jit(solution)/shard_map/ppermute | solution.py:336
  57.2 10.2 %all-to-all-start = ((f32[64,8,128]{2,1,0:T(8,128)}), f32[64,8,128]{2,1,0:T(8,128)S(1)}, u32[]{:S(2)}, u32[]{:S(2)}) async-start(f32[64,8,128]{2,1,0:T(8,128)} %get-tuple-element.35), calls=%async_computation | async-start | bytes 524288 | tf_op jit(solution)/shard_map/all_to_all | solution.py:358
  67.4 2.7 %shard_map.106.refs_3_ = f32[560,384]{1,0:T(8,128)S(1)} custom-call(s32[6]{0:T(128)S(1)} %stack.19.facts.refs_0_, bf16[144,1536]{1,0:T(8,128)(2,1)S(1)} %pad_maximum_fusion.first, bf16[144,1536]{1,0:T(8,128)(2,1)S(1)} %collective-permute-done.4.second, bf16[144,1536]{1,0:T(8,128)(2,1)} %collective-permute-done.5.third, ...), custom_call_target="tpu_custom_call" | custom-call | flops 3000000000 | bytes 1000 | tf_op jit(solution)/shard_map/pallas_call | solution.py:37
  70.1 0.9 copy-done.9
  71.1 7.3 %all-to-all-done.refs_1_.gathered = f32[64,8,128]{2,1,0:T(8,128)S(1)} async-done(((f32[64,8,128]{2,1,0:T(8,128)}), f32[64,8,128]{2,1,0:T(8,128)S(1)}, u32[]{:S(2)}, u32[]{:S(2)}) %all-to-all-start) | async-done | bytes 262176 | tf_op jit(solution)/shard_map/all_to_all | solution.py:358
  78.4 0.7 copy-done
  79.1 5.0 %shard_map.107 = (bf16[512,192]{1,0:T(8,128)(2,1)}, bf16[512,192]{1,0:T(8,128)(2,1)}, f32[544,384]{1,0:T(8,128)}, f32[544,384]{1,0:T(8,128)}, f32[8,128]{1,0:T(8,128)}, /*index=5*/f32[64,8,128]{2,1,0:T(8,128)}) custom-call(s32[6]{0:T(128)} %copy-done.2, f32[64,8,128]{2,1,0:T(8,128)} %copy-done, f32[544,384]{1,0:T(8,128)} %copy-done.12, ...), custom_call_target="tpu_custom_call" | custom-call | flops 2000000000 | bytes 1000 | tf_op jit(solution)/shard_map/pallas_call | solution.py:76
  84.1 6.9 %all-to-all-start.2 = ((f32[64,8,128]{2,1,0:T(8,128)}), f32[64,8,128]{2,1,0:T(8,128)S(1)}, u32[]{:S(2)}, u32[]{:S(2)}) async-start(f32[64,8,128]{2,1,0:T(8,128)} %get-tuple-element.43), calls=%async_computation.2 | async-start | bytes 524288 | tf_op jit(solution)/shard_map/all_to_all | solution.py:358
  91.0 0.0 copy-start.6
  91.0 0.9 copy-done.6
  92.0 0.9 copy-done.7
  92.9 2.3 %shard_map.108 = (f32[128,1536]{1,0:T(8,128)S(1)}, bf16[128,1536]{1,0:T(8,128)(2,1)}, bf16[128,1536]{1,0:T(8,128)(2,1)S(1)}, bf16[128,1536]{1,0:T(8,128)(2,1)}) custom-call(s32[6]{0:T(128)S(1)} %copy-done.3, bf16[512,192]{1,0:T(8,128)(2,1)S(1)} %copy-done.6, bf16[512,192]{1,0:T(8,128)(2,1)S(1)} %copy-done.7, bf16[192,1536]{1,0:T(8,128)(2,1)S(1)} %shard_map.105.own_half, ...), custom_call_target="tpu_custom_call" | custom-call | flops 1000000000 | bytes 1000 | tf_op jit(solution)/shard_map/pallas_call | solution.py:37
  95.2 2.2 %collective-permute-start.11 = (bf16[128,1536]{1,0:T(8,128)(2,1)}, bf16[128,1536]{1,0:T(8,128)(2,1)}, u32[]{:S(2)}, u32[]{:S(2)}) collective-permute-start(bf16[128,1536]{1,0:T(8,128)(2,1)} %get-tuple-element.45), channel_id=1, source_target_pairs={{0,3},{1,0},{2,1},{3,2},{4,7},{5,4},{6,5},{7,6},{8,11},{9,8},{10,9... | collective-permute-start | bytes 1179656 | tf_op jit(solution)/shard_map/ppermute | solution.py:336
  97.3 1.5 %collective-permute-start.10 = (bf16[128,1536]{1,0:T(8,128)(2,1)S(1)}, bf16[128,1536]{1,0:T(8,128)(2,1)}, u32[]{:S(2)}, u32[]{:S(2)}) collective-permute-start(bf16[128,1536]{1,0:T(8,128)(2,1)S(1)} %get-tuple-element.44), channel_id=1, source_target_pairs={{0,2},{1,3},{2,0},{3,1},{4,6},{5,7},{6,4},{7,5},{8,10},{9,11},{10,... | collective-permute-start | bytes 1179656 | tf_op jit(solution)/shard_map/ppermute | solution.py:336
  98.8 2.6 %shard_map.111 = (f32[192,1536]{1,0:T(8,128)S(1)}, bf16[48,1536]{1,0:T(8,128)(2,1)S(1)}, bf16[48,1536]{1,0:T(8,128)(2,1)S(1)}, bf16[48,1536]{1,0:T(8,128)(2,1)S(1)}, bf16[48,1536]{1,0:T(8,128)(2,1)S(1)}) custom-call(s32[6]{0:T(128)S(1)} %copy-done.3, bf16[512,192]{1,0:T(8,128)(2,1)S(1)} %copy-done.6, bf16[512,192]{1,0:T(8,128)(2,1)S(1)} %copy-done.8, ...), custom_call_target="tpu_custom_call" | custom-call | flops 1000000000 | bytes 1000 | tf_op jit(solution)/shard_map/pallas_call | solution.py:37
  101.4 0.1 collective-permute-start.15
  101.5 0.5 collective-permute-start.16
  102.0 0.9 collective-permute-done.15.first
  102.8 0.1 collective-permute-start.17
  103.0 0.1 collective-permute-done.16.second
  103.0 0.3 collective-permute-start.18
  103.3 0.9 collective-permute-done.17.third
  104.2 0.2 collective-permute-done.18.fourth
  104.4 2.1 %shard_map.112 = bf16[768,384]{1,0:T(8,128)(2,1)} custom-call(f32[192,1536]{1,0:T(8,128)S(1)} %get-tuple-element.58.kept, bf16[48,1536]{1,0:T(8,128)(2,1)S(1)} %collective-permute-done.15.first, bf16[48,1536]{1,0:T(8,128)(2,1)S(1)} %collective-permute-done.16.second, bf16[48,1536]{1,0:T(8,128)(2,1)S(1)} %collective-permute-done.17.third, ...), custom_call_target="tpu_custom_call" | custom-call | flops 1000000000 | bytes 1000 | tf_op jit(solution)/shard_map/pallas_call | solution.py:37
  106.6 10.0 %all-to-all-start.3 = ((bf16[32,24,384]{2,1,0:T(8,128)(2,1)}), bf16[32,24,384]{2,1,0:T(8,128)(2,1)S(1)}, u32[]{:S(2)}, u32[]{:S(2)}) async-start(bf16[32,24,384]{2,1,0:T(8,128)(2,1)} %bitcast.14), calls=%async_computation.3 | async-start | bytes 1179648 | tf_op jit(solution)/shard_map/all_to_all | solution.py:358
  116.5 1.7 %collective-permute-done.9 = bf16[128,1536]{1,0:T(8,128)(2,1)} collective-permute-done((bf16[128,1536]{1,0:T(8,128)(2,1)}, bf16[128,1536]{1,0:T(8,128)(2,1)}, u32[]{:S(2)}, u32[]{:S(2)}) %collective-permute-start.9) | collective-permute-done | bytes 393248 | tf_op jit(solution)/shard_map/ppermute | solution.py:336
  118.3 1.1 copy-done.10
  119.4 1.1 copy-done.11
  120.6 4.7 %shard_map.109 = (bf16[128,384]{1,0:T(8,128)(2,1)S(1)}, bf16[128,384]{1,0:T(8,128)(2,1)S(1)}, bf16[128,384]{1,0:T(8,128)(2,1)S(1)}, bf16[128,384]{1,0:T(8,128)(2,1)S(1)}) custom-call(s32[6]{0:T(128)S(1)} %copy-done.3, f32[64,8,128]{2,1,0:T(8,128)S(1)} %copy-done.1, f32[64,8,128]{2,1,0:T(8,128)S(1)} %all-to-all-done.2.sums, f32[544,384]{1,0:T(8,128)S(1)} %copy-done.10, ...), custom_call_target="tpu_custom_call" | custom-call | flops 12000000000 | bytes 1000 | tf_op jit(solution)/shard_map/pallas_call | solution.py:37
  125.3 1.0 collective-permute-start.12
  126.2 0.9 collective-permute-start.13
  127.1 1.9 %collective-permute-start.14 = (bf16[128,384]{1,0:T(8,128)(2,1)S(1)}, bf16[128,384]{1,0:T(8,128)(2,1)S(1)}, u32[]{:S(2)}, u32[]{:S(2)}) collective-permute-start(bf16[128,384]{1,0:T(8,128)(2,1)S(1)} %get-tuple-element.53), channel_id=1, source_target_pairs={{0,3},{1,0},{2,1},{3,2},{4,7},{5,4},{6,5},{7,6},{8,11},{9,8},{10,9... | collective-permute-start | bytes 294920 | tf_op jit(solution)/shard_map/ppermute | solution.py:336
  129.0 3.9 %collective-permute-done.12.second = bf16[128,384]{1,0:T(8,128)(2,1)S(1)} collective-permute-done((bf16[128,384]{1,0:T(8,128)(2,1)S(1)}, bf16[128,384]{1,0:T(8,128)(2,1)S(1)}, u32[]{:S(2)}, u32[]{:S(2)}) %collective-permute-start.12) | collective-permute-done | bytes 98336 | tf_op jit(solution)/shard_map/ppermute | solution.py:336
  133.0 0.1 collective-permute-done.14.fourth
  133.1 1.3 shard_map.110
  134.4 0.8 all-to-all-done.3
  135.2 0.1 convert_reduce_fusion
  135.3 4.4 %collective-permute-start.19 = (f32[24,384]{1,0:T(8,128)S(1)}, f32[24,384]{1,0:T(8,128)S(1)}, u32[]{:S(2)}, u32[]{:S(2)}) collective-permute-start(f32[24,384]{1,0:T(8,128)S(1)} %convert_reduce_fusion), channel_id=1, source_target_pairs={{0,0},{1,64},{2,128},{3,192},{64,1},{65,65},{66,129},{67,193},{128... | collective-permute-start | bytes 110600 | tf_op jit(solution)/shard_map/ppermute | solution.py:345
  139.7 2.2 %fusion = bf16[1,128,1536]{2,1,0:T(8,128)(2,1)} fusion(bf16[128,1536]{1,0:T(8,128)(2,1)} %collective-permute-done.11, bf16[128,1536]{1,0:T(8,128)(2,1)} %collective-permute-done.10, f32[128,1536]{1,0:T(8,128)S(1)} %get-tuple-element.41, bf16[128,1536]{1,0:T(8,128)(2,1)} %collective-permute-done.9), kind=kLoop, calls=%fused_computation.3 | loop fusion | flops 1376256 | bytes 2359296 | tf_op jit(solution)/shard_map/broadcast_in_dim | solution.py:439
  141.8 3.2 %collective-permute-done.19.sums = f32[24,384]{1,0:T(8,128)S(1)} collective-permute-done((f32[24,384]{1,0:T(8,128)S(1)}, f32[24,384]{1,0:T(8,128)S(1)}, u32[]{:S(2)}, u32[]{:S(2)}) %collective-permute-start.19) | collective-permute-done | bytes 36896 | tf_op jit(solution)/shard_map/ppermute | solution.py:345
  145.1 0.6 shard_map.113
  (39 shorter events, 0.2 us)
Async XLA Ops:
  2.4 6.5 %collective-permute-start = (bf16[48,1536]{1,0:T(8,128)(2,1)S(1)}, bf16[48,1536]{1,0:T(8,128)(2,1)S(1)}, u32[]{:S(2)}, u32[]{:S(2)}) collective-permute-start(bf16[48,1536]{1,0:T(8,128)(2,1)S(1)} %pad_maximum_fusion.1), channel_id=1, source_target_pairs={{3,4},{7,8},{11,12},{15,16},{19,20},{23,24},{27,28},{4,3},{8,7},{1... | collective-permute-start | bytes 442376 | tf_op jit(solution)/shard_map/ppermute | solution.py:354
  3.0 13.5 %collective-permute-start.7 = (bf16[6,1536]{1,0:T(8,128)(2,1)}, bf16[6,1536]{1,0:T(8,128)(2,1)S(1)}, u32[]{:S(2)}, u32[]{:S(2)}) collective-permute-start(bf16[6,1536]{1,0:T(8,128)(2,1)} %param.12), channel_id=1, source_target_pairs={{0,0},{1,64},{2,128},{3,192},{64,1},{65,65},{66,129},{67,193},{128... | collective-permute-start | bytes 55304 | tf_op jit(solution)/shard_map/ppermute | solution.py:345
  8.9 10.0 %collective-permute-start.1 = (bf16[160,384]{1,0:T(8,128)(2,1)S(1)}, bf16[160,384]{1,0:T(8,128)(2,1)S(1)}, u32[]{:S(2)}, u32[]{:S(2)}) collective-permute-start(bf16[160,384]{1,0:T(8,128)(2,1)S(1)} %pad_maximum_fusion.3), channel_id=1, source_target_pairs={{0,1},{1,2},{2,3},{3,0},{4,5},{5,6},{6,7},{7,4},{8,9},{9,10},{10,1... | collective-permute-start | bytes 368648 | tf_op jit(solution)/shard_map/ppermute | solution.py:336
  9.1 12.0 %collective-permute-start.2 = (bf16[160,384]{1,0:T(8,128)(2,1)S(1)}, bf16[160,384]{1,0:T(8,128)(2,1)S(1)}, u32[]{:S(2)}, u32[]{:S(2)}) collective-permute-start(bf16[160,384]{1,0:T(8,128)(2,1)S(1)} %pad_maximum_fusion.4), channel_id=1, source_target_pairs={{0,2},{1,3},{2,0},{3,1},{4,6},{5,7},{6,4},{7,5},{8,10},{9,11},{10,... | collective-permute-start | bytes 368648 | tf_op jit(solution)/shard_map/ppermute | solution.py:336
  16.4 5.0 %collective-permute-start.3 = (bf16[160,384]{1,0:T(8,128)(2,1)S(1)}, bf16[160,384]{1,0:T(8,128)(2,1)S(1)}, u32[]{:S(2)}, u32[]{:S(2)}) collective-permute-start(bf16[160,384]{1,0:T(8,128)(2,1)S(1)} %pad_maximum_fusion.5), channel_id=1, source_target_pairs={{0,3},{1,0},{2,1},{3,2},{4,7},{5,4},{6,5},{7,6},{8,11},{9,8},{10,9... | collective-permute-start | bytes 368648 | tf_op jit(solution)/shard_map/ppermute | solution.py:336
  18.1 17.0 %copy-start.14 = (bf16[1,128,1536]{2,1,0:T(8,128)(2,1)S(1)}, bf16[1,128,1536]{2,1,0:T(8,128)(2,1)}, u32[]{:S(2)}) copy-start(bf16[1,128,1536]{2,1,0:T(8,128)(2,1)} %param.13) | copy-start | bytes 1179652
  18.1 21.0 %copy-start.4 = (f32[32,1536]{1,0:T(8,128)S(1)}, f32[32,1536]{1,0:T(8,128)}, u32[]{:S(2)}) copy-start(f32[32,1536]{1,0:T(8,128)} %weights.3) | copy-start | bytes 589828
  21.4 28.5 %all-to-all-start.1 = ((bf16[32,24,384]{2,1,0:T(8,128)(2,1)}), bf16[32,24,384]{2,1,0:T(8,128)(2,1)S(1)}, u32[]{:S(2)}, u32[]{:S(2)}) async-start(bf16[32,24,384]{2,1,0:T(8,128)(2,1)} %bitcast.11), calls=%async_computation.1 | async-start | bytes 1179648 | tf_op jit(solution)/shard_map/all_to_all | solution.py:358
  35.0 32.4 %copy-start.2 = (s32[6]{0:T(128)}, s32[6]{0:T(128)S(1)}, u32[]{:S(2)}) copy-start(s32[6]{0:T(128)S(1)} %stack.19.facts.refs_0_) | copy-start | bytes 76
  35.1 16.1 %collective-permute-start.4 = (bf16[144,1536]{1,0:T(8,128)(2,1)S(1)}, bf16[144,1536]{1,0:T(8,128)(2,1)S(1)}, u32[]{:S(2)}, u32[]{:S(2)}) collective-permute-start(bf16[144,1536]{1,0:T(8,128)(2,1)S(1)} %pad_maximum_fusion.first), channel_id=1, source_target_pairs={{0,1},{1,2},{2,3},{3,0},{4,5},{5,6},{6,7},{7,4},{8,9},{9,10},{10,1... | collective-permute-start | bytes 1327112 | tf_op jit(solution)/shard_map/ppermute | solution.py:336
  35.6 21.6 %collective-permute-start.5 = (bf16[144,1536]{1,0:T(8,128)(2,1)S(1)}, bf16[144,1536]{1,0:T(8,128)(2,1)}, u32[]{:S(2)}, u32[]{:S(2)}) collective-permute-start(bf16[144,1536]{1,0:T(8,128)(2,1)S(1)} %pad_maximum_fusion.first), channel_id=1, source_target_pairs={{0,2},{1,3},{2,0},{3,1},{4,6},{5,7},{6,4},{7,5},{8,10},{9,11},{10,... | collective-permute-start | bytes 1327112 | tf_op jit(solution)/shard_map/ppermute | solution.py:336
  39.1 18.1 %collective-permute-start.6 = (bf16[144,1536]{1,0:T(8,128)(2,1)S(1)}, bf16[144,1536]{1,0:T(8,128)(2,1)}, u32[]{:S(2)}, u32[]{:S(2)}) collective-permute-start(bf16[144,1536]{1,0:T(8,128)(2,1)S(1)} %pad_maximum_fusion.first), channel_id=1, source_target_pairs={{0,3},{1,0},{2,1},{3,2},{4,7},{5,4},{6,5},{7,6},{8,11},{9,8},{10,9... | collective-permute-start | bytes 1327112 | tf_op jit(solution)/shard_map/ppermute | solution.py:336
  44.0 0.9 copy-start.12
  51.1 16.3 %collective-permute-start.8 = (bf16[192,1536]{1,0:T(8,128)(2,1)S(1)}, bf16[192,1536]{1,0:T(8,128)(2,1)S(1)}, u32[]{:S(2)}, u32[]{:S(2)}) collective-permute-start(bf16[192,1536]{1,0:T(8,128)(2,1)S(1)} %shard_map.105.own_half), channel_id=1, source_target_pairs={{0,32},{32,0},{1,33},{33,1},{2,34},{34,2},{3,35},{35,3},{4,36},{36... | collective-permute-start | bytes 1769480 | tf_op jit(solution)/shard_map/ppermute | solution.py:340
  57.2 21.1 %all-to-all-start = ((f32[64,8,128]{2,1,0:T(8,128)}), f32[64,8,128]{2,1,0:T(8,128)S(1)}, u32[]{:S(2)}, u32[]{:S(2)}) async-start(f32[64,8,128]{2,1,0:T(8,128)} %get-tuple-element.35), calls=%async_computation | async-start | bytes 524288 | tf_op jit(solution)/shard_map/all_to_all | solution.py:358
  70.1 0.9 copy-start.9
  78.4 0.7 copy-start
  79.0 12.0 %copy-start.3 = (s32[6]{0:T(128)S(1)}, s32[6]{0:T(128)}, u32[]{:S(2)}) copy-start(s32[6]{0:T(128)} %copy-done.2) | copy-start | bytes 76
  84.1 22.5 %all-to-all-start.2 = ((f32[64,8,128]{2,1,0:T(8,128)}), f32[64,8,128]{2,1,0:T(8,128)S(1)}, u32[]{:S(2)}, u32[]{:S(2)}) async-start(f32[64,8,128]{2,1,0:T(8,128)} %get-tuple-element.43), calls=%async_computation.2 | async-start | bytes 524288 | tf_op jit(solution)/shard_map/all_to_all | solution.py:358
  91.0 1.0 copy-start.6
  92.0 0.9 copy-start.7
  92.9 5.9 %copy-start.8 = (bf16[512,192]{1,0:T(8,128)(2,1)S(1)}, bf16[512,192]{1,0:T(8,128)(2,1)}, u32[]{:S(2)}) copy-start(bf16[512,192]{1,0:T(8,128)(2,1)} %get-tuple-element.40.theirs) | copy-start | bytes 589828
  95.2 21.3 %collective-permute-start.11 = (bf16[128,1536]{1,0:T(8,128)(2,1)}, bf16[128,1536]{1,0:T(8,128)(2,1)}, u32[]{:S(2)}, u32[]{:S(2)}) collective-permute-start(bf16[128,1536]{1,0:T(8,128)(2,1)} %get-tuple-element.45), channel_id=1, source_target_pairs={{0,3},{1,0},{2,1},{3,2},{4,7},{5,4},{6,5},{7,6},{8,11},{9,8},{10,9... | collective-permute-start | bytes 1179656 | tf_op jit(solution)/shard_map/ppermute | solution.py:336
  97.3 20.9 %collective-permute-start.9 = (bf16[128,1536]{1,0:T(8,128)(2,1)}, bf16[128,1536]{1,0:T(8,128)(2,1)}, u32[]{:S(2)}, u32[]{:S(2)}) collective-permute-start(bf16[128,1536]{1,0:T(8,128)(2,1)} %get-tuple-element.42), channel_id=1, source_target_pairs={{0,1},{1,2},{2,3},{3,0},{4,5},{5,6},{6,7},{7,4},{8,9},{9,10},{10,1... | collective-permute-start | bytes 1179656 | tf_op jit(solution)/shard_map/ppermute | solution.py:336
  97.3 20.9 %collective-permute-start.10 = (bf16[128,1536]{1,0:T(8,128)(2,1)S(1)}, bf16[128,1536]{1,0:T(8,128)(2,1)}, u32[]{:S(2)}, u32[]{:S(2)}) collective-permute-start(bf16[128,1536]{1,0:T(8,128)(2,1)S(1)} %get-tuple-element.44), channel_id=1, source_target_pairs={{0,2},{1,3},{2,0},{3,1},{4,6},{5,7},{6,4},{7,5},{8,10},{9,11},{10,... | collective-permute-start | bytes 1179656 | tf_op jit(solution)/shard_map/ppermute | solution.py:336
  101.4 1.5 %collective-permute-start.15 = (bf16[48,1536]{1,0:T(8,128)(2,1)S(1)}, bf16[48,1536]{1,0:T(8,128)(2,1)S(1)}, u32[]{:S(2)}, u32[]{:S(2)}) collective-permute-start(bf16[48,1536]{1,0:T(8,128)(2,1)S(1)} %get-tuple-element.59), channel_id=1, source_target_pairs={{0,32},{32,0},{1,33},{33,1},{2,34},{34,2},{3,35},{35,3},{4,36},{36... | collective-permute-start | bytes 442376 | tf_op jit(solution)/shard_map/ppermute | solution.py:340
  101.5 1.6 %collective-permute-start.16 = (bf16[48,1536]{1,0:T(8,128)(2,1)S(1)}, bf16[48,1536]{1,0:T(8,128)(2,1)S(1)}, u32[]{:S(2)}, u32[]{:S(2)}) collective-permute-start(bf16[48,1536]{1,0:T(8,128)(2,1)S(1)} %get-tuple-element.60), channel_id=1, source_target_pairs={{0,32},{32,0},{1,33},{33,1},{2,34},{34,2},{3,35},{35,3},{4,36},{36... | collective-permute-start | bytes 442376 | tf_op jit(solution)/shard_map/ppermute | solution.py:340
  102.8 1.4 collective-permute-start.17
  103.0 1.4 collective-permute-start.18
  106.5 11.7 %copy-start.1 = (f32[64,8,128]{2,1,0:T(8,128)S(1)}, f32[64,8,128]{2,1,0:T(8,128)}, u32[]{:S(2)}) copy-start(f32[64,8,128]{2,1,0:T(8,128)} %copy-done) | copy-start | bytes 786436
  106.5 11.7 %copy-start.5 = (f32[32,1536]{1,0:T(8,128)S(1)}, f32[32,1536]{1,0:T(8,128)}, u32[]{:S(2)}) copy-start(f32[32,1536]{1,0:T(8,128)} %weights.3) | copy-start | bytes 589828
  106.5 11.7 %copy-start.13 = (f32[8,128]{1,0:T(8,128)S(1)}, f32[8,128]{1,0:T(8,128)}, u32[]{:S(2)}) copy-start(f32[8,128]{1,0:T(8,128)} %get-tuple-element.49.inverses) | copy-start | bytes 12292
  106.6 28.7 %all-to-all-start.3 = ((bf16[32,24,384]{2,1,0:T(8,128)(2,1)}), bf16[32,24,384]{2,1,0:T(8,128)(2,1)S(1)}, u32[]{:S(2)}, u32[]{:S(2)}) async-start(bf16[32,24,384]{2,1,0:T(8,128)(2,1)} %bitcast.14), calls=%async_computation.3 | async-start | bytes 1179648 | tf_op jit(solution)/shard_map/all_to_all | solution.py:358
  118.3 1.2 copy-start.10
  119.4 1.1 copy-start.11
  125.3 7.7 %collective-permute-start.12 = (bf16[128,384]{1,0:T(8,128)(2,1)S(1)}, bf16[128,384]{1,0:T(8,128)(2,1)S(1)}, u32[]{:S(2)}, u32[]{:S(2)}) collective-permute-start(bf16[128,384]{1,0:T(8,128)(2,1)S(1)} %get-tuple-element.51), channel_id=1, source_target_pairs={{0,1},{1,2},{2,3},{3,0},{4,5},{5,6},{6,7},{7,4},{8,9},{9,10},{10,1... | collective-permute-start | bytes 294920 | tf_op jit(solution)/shard_map/ppermute | solution.py:336
  126.2 6.7 %collective-permute-start.13 = (bf16[128,384]{1,0:T(8,128)(2,1)S(1)}, bf16[128,384]{1,0:T(8,128)(2,1)S(1)}, u32[]{:S(2)}, u32[]{:S(2)}) collective-permute-start(bf16[128,384]{1,0:T(8,128)(2,1)S(1)} %get-tuple-element.52), channel_id=1, source_target_pairs={{0,2},{1,3},{2,0},{3,1},{4,6},{5,7},{6,4},{7,5},{8,10},{9,11},{10,... | collective-permute-start | bytes 294920 | tf_op jit(solution)/shard_map/ppermute | solution.py:336
  127.1 6.0 %collective-permute-start.14 = (bf16[128,384]{1,0:T(8,128)(2,1)S(1)}, bf16[128,384]{1,0:T(8,128)(2,1)S(1)}, u32[]{:S(2)}, u32[]{:S(2)}) collective-permute-start(bf16[128,384]{1,0:T(8,128)(2,1)S(1)} %get-tuple-element.53), channel_id=1, source_target_pairs={{0,3},{1,0},{2,1},{3,2},{4,7},{5,4},{6,5},{7,6},{8,11},{9,8},{10,9... | collective-permute-start | bytes 294920 | tf_op jit(solution)/shard_map/ppermute | solution.py:336
  135.3 9.8 %collective-permute-start.19 = (f32[24,384]{1,0:T(8,128)S(1)}, f32[24,384]{1,0:T(8,128)S(1)}, u32[]{:S(2)}, u32[]{:S(2)}) collective-permute-start(f32[24,384]{1,0:T(8,128)S(1)} %convert_reduce_fusion), channel_id=1, source_target_pairs={{0,0},{1,64},{2,128},{3,192},{64,1},{65,65},{66,129},{67,193},{128... | collective-permute-start | bytes 110600 | tf_op jit(solution)/shard_map/ppermute | solution.py:345

commit v6 on v4

--- a/solution.py
+++ b/solution.py
@@ -372,23 +372,25 @@
         axis=0,
     )
     rim = between_blocks(rim)
-    copies = small(copies_body, (SENT, BLOCK), BF16)(swap_xy(w_out))
-
-    pieces = []
+    swapped = swap_xy(w_out)
+
+    pieces, slices = [], []
     for k in range(PARTS):
         column = lax.rem(x + k, PARTS) * BLOCK
         own = lax.dynamic_slice(glu, (0, column), (OWN, BLOCK))
         piece = jnp.concatenate([own, lax.dynamic_slice(rim, (0, column), (TAPS, BLOCK))], axis=0)
+        slices.append(piece)
         pieces.append(around_x(piece, k) if k else piece)
+    copies = small(copies_body, (SENT, BLOCK), BF16)(wait_for(swapped, *slices))
     rows = exchange(wait_for(copies, *pieces), ("z", "y"))
-    cot = wait_for(jnp.concatenate([cot, rim[TAPS:]], axis=0), *pieces)
+    cot = wait_for(jnp.concatenate([cot, rim[TAPS:]], axis=0), copies, *pieces)
     cots = [cot] + [around_x(cot, k) for k in range(1, PARTS)]
     convolved, payload = call(
         conv_body,
         [((WIDE, BLOCK), F32), ((MEMBERS, 8, LANES), F32)],
         [pltpu.VMEM((FRAMES + 3 * TAPS, BLOCK), F32)],
-        cost=5,
-    )(facts, *pieces, conv_weight)
+        cost=20,
+    )(facts, wait_for(pieces[0], cots[1]), *pieces[1:], conv_weight)
 
     (half,) = call(weight_body, [((SHARE, CHANNELS), BF16)], scalars=0)(wait_for(rows, payload))
     gathered = exchange(wait_for(payload, *cots), STATS)

time: 145 us -> 143 us (0.986)
  starting transfers between devices: 68.4 us -> 66.4 us
    all_to_all x4, starting transfers between devices: 39.3 us -> 35 us  [exchange(): return lax.all_to_all(payload, axes, 0, 0, tiled=True)]
    ppermute x12, starting transfers between devices: 17.9 us -> 21.1 us  [around_x(): lax.ppermute(piece, 'x', [(i, (i + shift) % size) for i in range(size)])]
    ppermute x12, waiting for transfers between devices: 12.9 us -> 10.5 us  [around_x(): lax.ppermute(piece, 'x', [(i, (i + shift) % size) for i in range(size)])]
  transfers between devices with their start and end apart: 24 -> 24, of which waited for: 12 -> 12; matrix products, arithmetic and copies ran while one was open for 2% -> 2% of each run, Pallas kernels for 16% -> 17%
where the time goes in v6:
time: 143 us; the launch traced here: 142 us
  starting transfers between devices  66.4 us (46%)
  waiting for transfers between devices  31.9 us (22%)
  Pallas kernels  29.1 us (20%)
  local copies, waits for them, and re-layouts  9.75 us (7%)
  between operations  2.3 us (2%)
  other arithmetic  2.23 us (2%)
    all_to_all x4, starting transfers between devices, exchange(): return lax.all_to_all(payload, axes, 0, 0, tiled=True)  35 us
    pallas_call x10, Pallas kernels, run(): pl.pallas_call(body, out_shape=[jax.ShapeDtypeStruct(shape, kind) for sha...  24.1 us
    ppermute x12, starting transfers between devices, around_x(): lax.ppermute(piece, 'x', [(i, (i + shift) % size) for i in range(size)])  21.1 us
    all_to_all x4, waiting for transfers between devices, exchange(): return lax.all_to_all(payload, axes, 0, 0, tiled=True)  15.6 us
    ppermute x12, waiting for transfers between devices, around_x(): lax.ppermute(piece, 'x', [(i, (i + shift) % size) for i in range(size)])  10.5 us
    ppermute x2, starting transfers between devices, swap_xy(): return lax.ppermute(block, ('y', 'x'), pairs)  8.46 us
    unnamed x32, local copies, waits for them, and re-layouts  6.77 us
    pallas_call x1, Pallas kernels, run(): pl.pallas_call(staged, out_shape=made, in_specs=[pl.BlockSpec(memory_spac...  5 us
  transfers between devices with their start and end apart: 24, of which 12 were waited for; matrix products, arithmetic and copies ran while one was open for 2% of the time, Pallas kernels for 17%

profile of v6, /device:TPU:16, one launch (start us, length us, event | category | flops | bytes accessed | tf_op | source)
XLA Modules:
  0.0 141.6 jit_solution(16698748875624167306)
XLA Ops:
  0.6 0.9 dynamic-slice_bitcast_fusion.3
  1.6 0.9 dynamic-slice_bitcast_fusion.5
  2.4 0.7 collective-permute-start
  3.1 4.7 %collective-permute-start.1 = (bf16[6,1536]{1,0:T(8,128)(2,1)}, bf16[6,1536]{1,0:T(8,128)(2,1)S(1)}, u32[]{:S(2)}, u32[]{:S(2)}) collective-permute-start(bf16[6,1536]{1,0:T(8,128)(2,1)} %param.12), channel_id=1, source_target_pairs={{0,0},{1,64},{2,128},{3,192},{64,1},{65,65},{66,129},{67,193},{128... | collective-permute-start | bytes 55304 | tf_op jit(solution)/shard_map/ppermute | solution.py:345
  7.9 1.1 dynamic-slice_bitcast_fusion
  9.0 0.1 collective-permute-start.2
  9.2 7.3 %collective-permute-start.3 = (bf16[160,384]{1,0:T(8,128)(2,1)S(1)}, bf16[160,384]{1,0:T(8,128)(2,1)S(1)}, u32[]{:S(2)}, u32[]{:S(2)}) collective-permute-start(bf16[160,384]{1,0:T(8,128)(2,1)S(1)} %pad_maximum_fusion.4), channel_id=1, source_target_pairs={{0,2},{1,3},{2,0},{3,1},{4,6},{5,7},{6,4},{7,5},{8,10},{9,11},{10,... | collective-permute-start | bytes 368648 | tf_op jit(solution)/shard_map/ppermute | solution.py:336
  16.5 0.1 collective-permute-start.4
  16.7 0.0 collective-permute-done.1.row_block
  16.7 1.6 %shard_map.103 = bf16[768,384]{1,0:T(8,128)(2,1)} custom-call(bf16[6,1536]{1,0:T(8,128)(2,1)S(1)} %collective-permute-done.1.row_block), custom_call_target="tpu_custom_call" | custom-call | flops 1000000000 | bytes 1000 | tf_op jit(solution)/shard_map/pallas_call | solution.py:37
  18.2 0.8 collective-permute-done.2.second
  19.1 2.1 %collective-permute-done.3.third = bf16[160,384]{1,0:T(8,128)(2,1)S(1)} collective-permute-done((bf16[160,384]{1,0:T(8,128)(2,1)S(1)}, bf16[160,384]{1,0:T(8,128)(2,1)S(1)}, u32[]{:S(2)}, u32[]{:S(2)}) %collective-permute-start.3) | collective-permute-done | bytes 122912 | tf_op jit(solution)/shard_map/ppermute | solution.py:336
  21.2 0.3 collective-permute-done.4.fourth
  21.4 0.0 collective-permute-start.5
  22.7 0.1 stack.19.facts.refs_0_
  22.8 3.4 %collective-permute-start.6 = (bf16[144,1536]{1,0:T(8,128)(2,1)S(1)}, bf16[144,1536]{1,0:T(8,128)(2,1)}, u32[]{:S(2)}, u32[]{:S(2)}) collective-permute-start(bf16[144,1536]{1,0:T(8,128)(2,1)S(1)} %pad_maximum_fusion.first), channel_id=1, source_target_pairs={{0,2},{1,3},{2,0},{3,1},{4,6},{5,7},{6,4},{7,5},{8,10},{9,11},{10,... | collective-permute-start | bytes 1327112 | tf_op jit(solution)/shard_map/ppermute | solution.py:336
  26.2 0.7 collective-permute-start.7
  26.9 12.1 %all-to-all-start.1 = ((bf16[32,24,384]{2,1,0:T(8,128)(2,1)}), bf16[32,24,384]{2,1,0:T(8,128)(2,1)S(1)}, u32[]{:S(2)}, u32[]{:S(2)}) async-start(bf16[32,24,384]{2,1,0:T(8,128)(2,1)} %bitcast.11), calls=%async_computation.1 | async-start | bytes 1179648 | tf_op jit(solution)/shard_map/all_to_all | solution.py:358
  39.0 3.9 %collective-permute-done.5.second = bf16[144,1536]{1,0:T(8,128)(2,1)S(1)} collective-permute-done((bf16[144,1536]{1,0:T(8,128)(2,1)S(1)}, bf16[144,1536]{1,0:T(8,128)(2,1)S(1)}, u32[]{:S(2)}, u32[]{:S(2)}) %collective-permute-start.5) | collective-permute-done | bytes 442400 | tf_op jit(solution)/shard_map/ppermute | solution.py:336
  42.9 4.9 %shard_map.104 = (f32[544,384]{1,0:T(8,128)S(1)}, f32[64,8,128]{2,1,0:T(8,128)}) custom-call(s32[6]{0:T(128)S(1)} %stack.19.facts.refs_0_, bf16[160,384]{1,0:T(8,128)(2,1)S(1)} %pad_maximum_fusion.2.first, bf16[160,384]{1,0:T(8,128)(2,1)S(1)} %collective-permute-done.2.second, bf16[160,384]{1,0:T(8,128)(2,1)S(1)} %collective-permute-done.3.third, ...), custom_call_target="tpu_custom_call" | custom-call | flops 20000000000 | bytes 1000 | tf_op jit(solution)/shard_map/pallas_call | solution.py:37
  47.9 0.9 copy-done.13
  48.8 7.2 %all-to-all-done.1 = bf16[32,24,384]{2,1,0:T(8,128)(2,1)S(1)} async-done(((bf16[32,24,384]{2,1,0:T(8,128)(2,1)}), bf16[32,24,384]{2,1,0:T(8,128)(2,1)S(1)}, u32[]{:S(2)}, u32[]{:S(2)}) %all-to-all-start.1) | async-done | bytes 589856 | tf_op jit(solution)/shard_map/all_to_all | solution.py:358
  56.0 1.3 shard_map.105.own_half
  57.2 0.1 collective-permute-start.8
  57.3 0.0 collective-permute-done.7.fourth
  57.4 6.0 %all-to-all-start = ((f32[64,8,128]{2,1,0:T(8,128)}), f32[64,8,128]{2,1,0:T(8,128)S(1)}, u32[]{:S(2)}, u32[]{:S(2)}) async-start(f32[64,8,128]{2,1,0:T(8,128)} %get-tuple-element.39), calls=%async_computation | async-start | bytes 524288 | tf_op jit(solution)/shard_map/all_to_all | solution.py:358
  63.4 2.7 %shard_map.106.refs_3_ = f32[560,384]{1,0:T(8,128)S(1)} custom-call(s32[6]{0:T(128)S(1)} %stack.19.facts.refs_0_, bf16[144,1536]{1,0:T(8,128)(2,1)S(1)} %pad_maximum_fusion.first, bf16[144,1536]{1,0:T(8,128)(2,1)S(1)} %collective-permute-done.5.second, bf16[144,1536]{1,0:T(8,128)(2,1)} %collective-permute-done.6.third, ...), custom_call_target="tpu_custom_call" | custom-call | flops 3000000000 | bytes 1000 | tf_op jit(solution)/shard_map/pallas_call | solution.py:37
  66.1 0.9 copy-done.10
  67.0 7.3 %all-to-all-done.refs_1_.gathered = f32[64,8,128]{2,1,0:T(8,128)S(1)} async-done(((f32[64,8,128]{2,1,0:T(8,128)}), f32[64,8,128]{2,1,0:T(8,128)S(1)}, u32[]{:S(2)}, u32[]{:S(2)}) %all-to-all-start) | async-done | bytes 262176 | tf_op jit(solution)/shard_map/all_to_all | solution.py:358
  74.4 0.7 copy-done
  75.1 5.0 %shard_map.107 = (bf16[512,192]{1,0:T(8,128)(2,1)}, bf16[512,192]{1,0:T(8,128)(2,1)}, f32[544,384]{1,0:T(8,128)}, f32[544,384]{1,0:T(8,128)}, f32[8,128]{1,0:T(8,128)}, /*index=5*/f32[64,8,128]{2,1,0:T(8,128)}) custom-call(s32[6]{0:T(128)} %copy-done.2, f32[64,8,128]{2,1,0:T(8,128)} %copy-done, f32[544,384]{1,0:T(8,128)} %copy-done.13, ...), custom_call_target="tpu_custom_call" | custom-call | flops 2000000000 | bytes 1000 | tf_op jit(solution)/shard_map/pallas_call | solution.py:76
  80.1 6.9 %all-to-all-start.2 = ((f32[64,8,128]{2,1,0:T(8,128)}), f32[64,8,128]{2,1,0:T(8,128)S(1)}, u32[]{:S(2)}, u32[]{:S(2)}) async-start(f32[64,8,128]{2,1,0:T(8,128)} %get-tuple-element.47), calls=%async_computation.2 | async-start | bytes 524288 | tf_op jit(solution)/shard_map/all_to_all | solution.py:358
  87.0 0.9 copy-done.6
  88.0 0.9 copy-done.8
  88.9 2.3 %shard_map.108 = (f32[128,1536]{1,0:T(8,128)S(1)}, bf16[128,1536]{1,0:T(8,128)(2,1)S(1)}, bf16[128,1536]{1,0:T(8,128)(2,1)}, bf16[128,1536]{1,0:T(8,128)(2,1)}) custom-call(s32[6]{0:T(128)S(1)} %copy-done.3, bf16[512,192]{1,0:T(8,128)(2,1)S(1)} %copy-done.6, bf16[512,192]{1,0:T(8,128)(2,1)S(1)} %copy-done.8, bf16[192,1536]{1,0:T(8,128)(2,1)S(1)} %shard_map.105.own_half, ...), custom_call_target="tpu_custom_call" | custom-call | flops 1000000000 | bytes 1000 | tf_op jit(solution)/shard_map/pallas_call | solution.py:37
  91.2 2.6 %shard_map.110 = (f32[192,1536]{1,0:T(8,128)S(1)}, bf16[48,1536]{1,0:T(8,128)(2,1)S(1)}, bf16[48,1536]{1,0:T(8,128)(2,1)S(1)}, bf16[48,1536]{1,0:T(8,128)(2,1)S(1)}, bf16[48,1536]{1,0:T(8,128)(2,1)S(1)}) custom-call(s32[6]{0:T(128)S(1)} %copy-done.3, bf16[512,192]{1,0:T(8,128)(2,1)S(1)} %copy-done.7, bf16[512,192]{1,0:T(8,128)(2,1)S(1)} %copy-done.9, ...), custom_call_target="tpu_custom_call" | custom-call | flops 1000000000 | bytes 1000 | tf_op jit(solution)/shard_map/pallas_call | solution.py:37
  93.8 0.3 collective-permute-start.12
  94.1 0.3 collective-permute-start.13
  94.4 1.5 %collective-permute-start.10 = (bf16[128,1536]{1,0:T(8,128)(2,1)}, bf16[128,1536]{1,0:T(8,128)(2,1)S(1)}, u32[]{:S(2)}, u32[]{:S(2)}) collective-permute-start(bf16[128,1536]{1,0:T(8,128)(2,1)} %get-tuple-element.48), channel_id=1, source_target_pairs={{0,2},{1,3},{2,0},{3,1},{4,6},{5,7},{6,4},{7,5},{8,10},{9,11},{10,... | collective-permute-start | bytes 1179656 | tf_op jit(solution)/shard_map/ppermute | solution.py:336
  95.8 3.0 %collective-permute-start.11 = (bf16[128,1536]{1,0:T(8,128)(2,1)}, bf16[128,1536]{1,0:T(8,128)(2,1)}, u32[]{:S(2)}, u32[]{:S(2)}) collective-permute-start(bf16[128,1536]{1,0:T(8,128)(2,1)} %get-tuple-element.49), channel_id=1, source_target_pairs={{0,3},{1,0},{2,1},{3,2},{4,7},{5,4},{6,5},{7,6},{8,11},{9,8},{10,9... | collective-permute-start | bytes 1179656 | tf_op jit(solution)/shard_map/ppermute | solution.py:336
  98.8 0.0 collective-permute-done.13.second
  98.8 0.5 collective-permute-start.15
  99.3 0.9 collective-permute-done.14.third
  100.2 0.2 collective-permute-done.15.fourth
  100.4 2.1 %shard_map.111 = bf16[768,384]{1,0:T(8,128)(2,1)} custom-call(f32[192,1536]{1,0:T(8,128)S(1)} %get-tuple-element.62.kept, bf16[48,1536]{1,0:T(8,128)(2,1)S(1)} %collective-permute-done.12.first, bf16[48,1536]{1,0:T(8,128)(2,1)S(1)} %collective-permute-done.13.second, bf16[48,1536]{1,0:T(8,128)(2,1)S(1)} %collective-permute-done.14.third, ...), custom_call_target="tpu_custom_call" | custom-call | flops 1000000000 | bytes 1000 | tf_op jit(solution)/shard_map/pallas_call | solution.py:37
  102.5 0.0 all-to-all-done.2.sums
  102.5 9.9 %all-to-all-start.3 = ((bf16[32,24,384]{2,1,0:T(8,128)(2,1)}), bf16[32,24,384]{2,1,0:T(8,128)(2,1)S(1)}, u32[]{:S(2)}, u32[]{:S(2)}) async-start(bf16[32,24,384]{2,1,0:T(8,128)(2,1)} %bitcast.14), calls=%async_computation.3 | async-start | bytes 1179648 | tf_op jit(solution)/shard_map/all_to_all | solution.py:358
  112.4 0.0 collective-permute-done.10
  112.5 1.9 %collective-permute-done.11 = bf16[128,1536]{1,0:T(8,128)(2,1)} collective-permute-done((bf16[128,1536]{1,0:T(8,128)(2,1)}, bf16[128,1536]{1,0:T(8,128)(2,1)}, u32[]{:S(2)}, u32[]{:S(2)}) %collective-permute-start.11) | collective-permute-done | bytes 393248 | tf_op jit(solution)/shard_map/ppermute | solution.py:336
  114.4 1.5 %collective-permute-done.9 = bf16[128,1536]{1,0:T(8,128)(2,1)} collective-permute-done((bf16[128,1536]{1,0:T(8,128)(2,1)S(1)}, bf16[128,1536]{1,0:T(8,128)(2,1)}, u32[]{:S(2)}, u32[]{:S(2)}) %collective-permute-start.9) | collective-permute-done | bytes 393248 | tf_op jit(solution)/shard_map/ppermute | solution.py:336
  115.9 1.1 copy-done.11
  117.0 1.1 copy-done.12
  118.2 4.7 %shard_map.109 = (bf16[128,384]{1,0:T(8,128)(2,1)S(1)}, bf16[128,384]{1,0:T(8,128)(2,1)S(1)}, bf16[128,384]{1,0:T(8,128)(2,1)S(1)}, bf16[128,384]{1,0:T(8,128)(2,1)S(1)}) custom-call(s32[6]{0:T(128)S(1)} %copy-done.3, f32[64,8,128]{2,1,0:T(8,128)S(1)} %copy-done.1, f32[64,8,128]{2,1,0:T(8,128)S(1)} %all-to-all-done.2.sums, f32[544,384]{1,0:T(8,128)S(1)} %copy-done.11, ...), custom_call_target="tpu_custom_call" | custom-call | flops 5000000000 | bytes 1000 | tf_op jit(solution)/shard_map/pallas_call | solution.py:37
  122.8 0.3 collective-permute-start.17
  123.2 2.4 %collective-permute-start.18 = (bf16[128,384]{1,0:T(8,128)(2,1)S(1)}, bf16[128,384]{1,0:T(8,128)(2,1)S(1)}, u32[]{:S(2)}, u32[]{:S(2)}) collective-permute-start(bf16[128,384]{1,0:T(8,128)(2,1)S(1)} %get-tuple-element.56), channel_id=1, source_target_pairs={{0,2},{1,3},{2,0},{3,1},{4,6},{5,7},{6,4},{7,5},{8,10},{9,11},{10,... | collective-permute-start | bytes 294920 | tf_op jit(solution)/shard_map/ppermute | solution.py:336
  125.6 2.4 %collective-permute-start.19 = (bf16[128,384]{1,0:T(8,128)(2,1)S(1)}, bf16[128,384]{1,0:T(8,128)(2,1)S(1)}, u32[]{:S(2)}, u32[]{:S(2)}) collective-permute-start(bf16[128,384]{1,0:T(8,128)(2,1)S(1)} %get-tuple-element.57), channel_id=1, source_target_pairs={{0,3},{1,0},{2,1},{3,2},{4,7},{5,4},{6,5},{7,6},{8,11},{9,8},{10,9... | collective-permute-start | bytes 294920 | tf_op jit(solution)/shard_map/ppermute | solution.py:336
  127.9 2.0 %fusion = bf16[1,128,1536]{2,1,0:T(8,128)(2,1)} fusion(bf16[128,1536]{1,0:T(8,128)(2,1)} %collective-permute-done.11, bf16[128,1536]{1,0:T(8,128)(2,1)S(1)} %collective-permute-done.10, f32[128,1536]{1,0:T(8,128)S(1)} %get-tuple-element.45, bf16[128,1536]{1,0:T(8,128)(2,1)} %collective-permute-done.9), kind=kLoop, calls=%fused_computation.3 | loop fusion | flops 1376256 | bytes 2359296 | tf_op jit(solution)/shard_map/broadcast_in_dim | solution.py:441
  130.0 1.2 all-to-all-done.3
  131.1 0.1 convert_reduce_fusion
  131.2 3.8 %collective-permute-start.16 = (f32[24,384]{1,0:T(8,128)S(1)}, f32[24,384]{1,0:T(8,128)S(1)}, u32[]{:S(2)}, u32[]{:S(2)}) collective-permute-start(f32[24,384]{1,0:T(8,128)S(1)} %convert_reduce_fusion), channel_id=1, source_target_pairs={{0,0},{1,64},{2,128},{3,192},{64,1},{65,65},{66,129},{67,193},{128... | collective-permute-start | bytes 110600 | tf_op jit(solution)/shard_map/ppermute | solution.py:345
  135.0 0.0 collective-permute-done.17.second
  135.0 1.3 shard_map.113
  136.4 4.6 %collective-permute-done.16.sums = f32[24,384]{1,0:T(8,128)S(1)} collective-permute-done((f32[24,384]{1,0:T(8,128)S(1)}, f32[24,384]{1,0:T(8,128)S(1)}, u32[]{:S(2)}, u32[]{:S(2)}) %collective-permute-start.16) | collective-permute-done | bytes 36896 | tf_op jit(solution)/shard_map/ppermute | solution.py:345
  141.0 0.6 shard_map.112
  (41 shorter events, 0.2 us)
Async XLA Ops:
  1.5 15.0 %copy-start.15 = (bf16[1,128,1536]{2,1,0:T(8,128)(2,1)S(1)}, bf16[1,128,1536]{2,1,0:T(8,128)(2,1)}, u32[]{:S(2)}) copy-start(bf16[1,128,1536]{2,1,0:T(8,128)(2,1)} %param.13) | copy-start | bytes 1179652
  2.4 6.5 %collective-permute-start = (bf16[48,1536]{1,0:T(8,128)(2,1)S(1)}, bf16[48,1536]{1,0:T(8,128)(2,1)S(1)}, u32[]{:S(2)}, u32[]{:S(2)}) collective-permute-start(bf16[48,1536]{1,0:T(8,128)(2,1)S(1)} %pad_maximum_fusion.1), channel_id=1, source_target_pairs={{3,4},{7,8},{11,12},{15,16},{19,20},{23,24},{27,28},{4,3},{8,7},{1... | collective-permute-start | bytes 442376 | tf_op jit(solution)/shard_map/ppermute | solution.py:354
  3.1 13.5 %collective-permute-start.1 = (bf16[6,1536]{1,0:T(8,128)(2,1)}, bf16[6,1536]{1,0:T(8,128)(2,1)S(1)}, u32[]{:S(2)}, u32[]{:S(2)}) collective-permute-start(bf16[6,1536]{1,0:T(8,128)(2,1)} %param.12), channel_id=1, source_target_pairs={{0,0},{1,64},{2,128},{3,192},{64,1},{65,65},{66,129},{67,193},{128... | collective-permute-start | bytes 55304 | tf_op jit(solution)/shard_map/ppermute | solution.py:345
  9.0 10.0 %collective-permute-start.2 = (bf16[160,384]{1,0:T(8,128)(2,1)S(1)}, bf16[160,384]{1,0:T(8,128)(2,1)S(1)}, u32[]{:S(2)}, u32[]{:S(2)}) collective-permute-start(bf16[160,384]{1,0:T(8,128)(2,1)S(1)} %pad_maximum_fusion.3), channel_id=1, source_target_pairs={{0,1},{1,2},{2,3},{3,0},{4,5},{5,6},{6,7},{7,4},{8,9},{9,10},{10,1... | collective-permute-start | bytes 368648 | tf_op jit(solution)/shard_map/ppermute | solution.py:336
  9.2 12.0 %collective-permute-start.3 = (bf16[160,384]{1,0:T(8,128)(2,1)S(1)}, bf16[160,384]{1,0:T(8,128)(2,1)S(1)}, u32[]{:S(2)}, u32[]{:S(2)}) collective-permute-start(bf16[160,384]{1,0:T(8,128)(2,1)S(1)} %pad_maximum_fusion.4), channel_id=1, source_target_pairs={{0,2},{1,3},{2,0},{3,1},{4,6},{5,7},{6,4},{7,5},{8,10},{9,11},{10,... | collective-permute-start | bytes 368648 | tf_op jit(solution)/shard_map/ppermute | solution.py:336
  16.5 5.0 %collective-permute-start.4 = (bf16[160,384]{1,0:T(8,128)(2,1)S(1)}, bf16[160,384]{1,0:T(8,128)(2,1)S(1)}, u32[]{:S(2)}, u32[]{:S(2)}) collective-permute-start(bf16[160,384]{1,0:T(8,128)(2,1)S(1)} %pad_maximum_fusion.5), channel_id=1, source_target_pairs={{0,3},{1,0},{2,1},{3,2},{4,7},{5,4},{6,5},{7,6},{8,11},{9,8},{10,9... | collective-permute-start | bytes 368648 | tf_op jit(solution)/shard_map/ppermute | solution.py:336
  18.2 24.7 %copy-start.4 = (f32[32,1536]{1,0:T(8,128)S(1)}, f32[32,1536]{1,0:T(8,128)}, u32[]{:S(2)}) copy-start(f32[32,1536]{1,0:T(8,128)} %weights.3) | copy-start | bytes 589828
  21.4 21.5 %collective-permute-start.5 = (bf16[144,1536]{1,0:T(8,128)(2,1)S(1)}, bf16[144,1536]{1,0:T(8,128)(2,1)S(1)}, u32[]{:S(2)}, u32[]{:S(2)}) collective-permute-start(bf16[144,1536]{1,0:T(8,128)(2,1)S(1)} %pad_maximum_fusion.first), channel_id=1, source_target_pairs={{0,1},{1,2},{2,3},{3,0},{4,5},{5,6},{6,7},{7,4},{8,9},{9,10},{10,1... | collective-permute-start | bytes 1327112 | tf_op jit(solution)/shard_map/ppermute | solution.py:336
  22.8 40.6 %copy-start.2 = (s32[6]{0:T(128)}, s32[6]{0:T(128)S(1)}, u32[]{:S(2)}) copy-start(s32[6]{0:T(128)S(1)} %stack.19.facts.refs_0_) | copy-start | bytes 76
  22.8 34.5 %collective-permute-start.6 = (bf16[144,1536]{1,0:T(8,128)(2,1)S(1)}, bf16[144,1536]{1,0:T(8,128)(2,1)}, u32[]{:S(2)}, u32[]{:S(2)}) collective-permute-start(bf16[144,1536]{1,0:T(8,128)(2,1)S(1)} %pad_maximum_fusion.first), channel_id=1, source_target_pairs={{0,2},{1,3},{2,0},{3,1},{4,6},{5,7},{6,4},{7,5},{8,10},{9,11},{10,... | collective-permute-start | bytes 1327112 | tf_op jit(solution)/shard_map/ppermute | solution.py:336
  26.2 31.1 %collective-permute-start.7 = (bf16[144,1536]{1,0:T(8,128)(2,1)S(1)}, bf16[144,1536]{1,0:T(8,128)(2,1)}, u32[]{:S(2)}, u32[]{:S(2)}) collective-permute-start(bf16[144,1536]{1,0:T(8,128)(2,1)S(1)} %pad_maximum_fusion.first), channel_id=1, source_target_pairs={{0,3},{1,0},{2,1},{3,2},{4,7},{5,4},{6,5},{7,6},{8,11},{9,8},{10,9... | collective-permute-start | bytes 1327112 | tf_op jit(solution)/shard_map/ppermute | solution.py:336
  26.9 29.0 %all-to-all-start.1 = ((bf16[32,24,384]{2,1,0:T(8,128)(2,1)}), bf16[32,24,384]{2,1,0:T(8,128)(2,1)S(1)}, u32[]{:S(2)}, u32[]{:S(2)}) async-start(bf16[32,24,384]{2,1,0:T(8,128)(2,1)} %bitcast.11), calls=%async_computation.1 | async-start | bytes 1179648 | tf_op jit(solution)/shard_map/all_to_all | solution.py:358
  47.9 0.9 copy-start.13
  57.2 6.2 %collective-permute-start.8 = (bf16[192,1536]{1,0:T(8,128)(2,1)S(1)}, bf16[192,1536]{1,0:T(8,128)(2,1)S(1)}, u32[]{:S(2)}, u32[]{:S(2)}) collective-permute-start(bf16[192,1536]{1,0:T(8,128)(2,1)S(1)} %shard_map.105.own_half), channel_id=1, source_target_pairs={{0,32},{32,0},{1,33},{33,1},{2,34},{34,2},{3,35},{35,3},{4,36},{36... | collective-permute-start | bytes 1769480 | tf_op jit(solution)/shard_map/ppermute | solution.py:340
  57.4 17.0 %all-to-all-start = ((f32[64,8,128]{2,1,0:T(8,128)}), f32[64,8,128]{2,1,0:T(8,128)S(1)}, u32[]{:S(2)}, u32[]{:S(2)}) async-start(f32[64,8,128]{2,1,0:T(8,128)} %get-tuple-element.39), calls=%async_computation | async-start | bytes 524288 | tf_op jit(solution)/shard_map/all_to_all | solution.py:358
  66.1 0.9 copy-start.10
  74.4 0.7 copy-start
  75.1 11.9 %copy-start.3 = (s32[6]{0:T(128)S(1)}, s32[6]{0:T(128)}, u32[]{:S(2)}) copy-start(s32[6]{0:T(128)} %copy-done.2) | copy-start | bytes 76
  80.1 22.4 %all-to-all-start.2 = ((f32[64,8,128]{2,1,0:T(8,128)}), f32[64,8,128]{2,1,0:T(8,128)S(1)}, u32[]{:S(2)}, u32[]{:S(2)}) async-start(f32[64,8,128]{2,1,0:T(8,128)} %get-tuple-element.47), calls=%async_computation.2 | async-start | bytes 524288 | tf_op jit(solution)/shard_map/all_to_all | solution.py:358
  87.0 1.0 copy-start.6
  88.0 0.9 copy-start.8
  88.9 2.3 %copy-start.7 = (bf16[512,192]{1,0:T(8,128)(2,1)S(1)}, bf16[512,192]{1,0:T(8,128)(2,1)}, u32[]{:S(2)}) copy-start(bf16[512,192]{1,0:T(8,128)(2,1)} %get-tuple-element.61.mine) | copy-start | bytes 589828
  88.9 2.3 %copy-start.9 = (bf16[512,192]{1,0:T(8,128)(2,1)S(1)}, bf16[512,192]{1,0:T(8,128)(2,1)}, u32[]{:S(2)}) copy-start(bf16[512,192]{1,0:T(8,128)(2,1)} %get-tuple-element.44.theirs) | copy-start | bytes 589828
  93.8 5.0 %collective-permute-start.12 = (bf16[48,1536]{1,0:T(8,128)(2,1)S(1)}, bf16[48,1536]{1,0:T(8,128)(2,1)S(1)}, u32[]{:S(2)}, u32[]{:S(2)}) collective-permute-start(bf16[48,1536]{1,0:T(8,128)(2,1)S(1)} %get-tuple-element.63), channel_id=1, source_target_pairs={{0,32},{32,0},{1,33},{33,1},{2,34},{34,2},{3,35},{35,3},{4,36},{36... | collective-permute-start | bytes 442376 | tf_op jit(solution)/shard_map/ppermute | solution.py:340
  94.1 4.7 %collective-permute-start.13 = (bf16[48,1536]{1,0:T(8,128)(2,1)S(1)}, bf16[48,1536]{1,0:T(8,128)(2,1)S(1)}, u32[]{:S(2)}, u32[]{:S(2)}) collective-permute-start(bf16[48,1536]{1,0:T(8,128)(2,1)S(1)} %get-tuple-element.64), channel_id=1, source_target_pairs={{0,32},{32,0},{1,33},{33,1},{2,34},{34,2},{3,35},{35,3},{4,36},{36... | collective-permute-start | bytes 442376 | tf_op jit(solution)/shard_map/ppermute | solution.py:340
  94.4 18.1 %collective-permute-start.10 = (bf16[128,1536]{1,0:T(8,128)(2,1)}, bf16[128,1536]{1,0:T(8,128)(2,1)S(1)}, u32[]{:S(2)}, u32[]{:S(2)}) collective-permute-start(bf16[128,1536]{1,0:T(8,128)(2,1)} %get-tuple-element.48), channel_id=1, source_target_pairs={{0,2},{1,3},{2,0},{3,1},{4,6},{5,7},{6,4},{7,5},{8,10},{9,11},{10,... | collective-permute-start | bytes 1179656 | tf_op jit(solution)/shard_map/ppermute | solution.py:336
  95.8 18.6 %collective-permute-start.11 = (bf16[128,1536]{1,0:T(8,128)(2,1)}, bf16[128,1536]{1,0:T(8,128)(2,1)}, u32[]{:S(2)}, u32[]{:S(2)}) collective-permute-start(bf16[128,1536]{1,0:T(8,128)(2,1)} %get-tuple-element.49), channel_id=1, source_target_pairs={{0,3},{1,0},{2,1},{3,2},{4,7},{5,4},{6,5},{7,6},{8,11},{9,8},{10,9... | collective-permute-start | bytes 1179656 | tf_op jit(solution)/shard_map/ppermute | solution.py:336
  98.8 17.1 %collective-permute-start.9 = (bf16[128,1536]{1,0:T(8,128)(2,1)S(1)}, bf16[128,1536]{1,0:T(8,128)(2,1)}, u32[]{:S(2)}, u32[]{:S(2)}) collective-permute-start(bf16[128,1536]{1,0:T(8,128)(2,1)S(1)} %get-tuple-element.46), channel_id=1, source_target_pairs={{0,1},{1,2},{2,3},{3,0},{4,5},{5,6},{6,7},{7,4},{8,9},{9,10},{10,1... | collective-permute-start | bytes 1179656 | tf_op jit(solution)/shard_map/ppermute | solution.py:336
  98.8 1.4 collective-permute-start.14
  98.8 1.6 %collective-permute-start.15 = (bf16[48,1536]{1,0:T(8,128)(2,1)S(1)}, bf16[48,1536]{1,0:T(8,128)(2,1)S(1)}, u32[]{:S(2)}, u32[]{:S(2)}) collective-permute-start(bf16[48,1536]{1,0:T(8,128)(2,1)S(1)} %get-tuple-element.66), channel_id=1, source_target_pairs={{0,32},{32,0},{1,33},{33,1},{2,34},{34,2},{3,35},{35,3},{4,36},{36... | collective-permute-start | bytes 442376 | tf_op jit(solution)/shard_map/ppermute | solution.py:340
  102.5 13.4 %copy-start.1 = (f32[64,8,128]{2,1,0:T(8,128)S(1)}, f32[64,8,128]{2,1,0:T(8,128)}, u32[]{:S(2)}) copy-start(f32[64,8,128]{2,1,0:T(8,128)} %copy-done) | copy-start | bytes 786436
  102.5 13.4 %copy-start.5 = (f32[32,1536]{1,0:T(8,128)S(1)}, f32[32,1536]{1,0:T(8,128)}, u32[]{:S(2)}) copy-start(f32[32,1536]{1,0:T(8,128)} %weights.3) | copy-start | bytes 589828
  102.5 13.4 %copy-start.14 = (f32[8,128]{1,0:T(8,128)S(1)}, f32[8,128]{1,0:T(8,128)}, u32[]{:S(2)}) copy-start(f32[8,128]{1,0:T(8,128)} %get-tuple-element.53.inverses) | copy-start | bytes 12292
  102.5 28.6 %all-to-all-start.3 = ((bf16[32,24,384]{2,1,0:T(8,128)(2,1)}), bf16[32,24,384]{2,1,0:T(8,128)(2,1)S(1)}, u32[]{:S(2)}, u32[]{:S(2)}) async-start(bf16[32,24,384]{2,1,0:T(8,128)(2,1)} %bitcast.14), calls=%async_computation.3 | async-start | bytes 1179648 | tf_op jit(solution)/shard_map/all_to_all | solution.py:358
  115.9 1.2 copy-start.11
  117.0 1.1 copy-start.12
  122.8 12.2 %collective-permute-start.17 = (bf16[128,384]{1,0:T(8,128)(2,1)S(1)}, bf16[128,384]{1,0:T(8,128)(2,1)S(1)}, u32[]{:S(2)}, u32[]{:S(2)}) collective-permute-start(bf16[128,384]{1,0:T(8,128)(2,1)S(1)} %get-tuple-element.55), channel_id=1, source_target_pairs={{0,1},{1,2},{2,3},{3,0},{4,5},{5,6},{6,7},{7,4},{8,9},{9,10},{10,1... | collective-permute-start | bytes 294920 | tf_op jit(solution)/shard_map/ppermute | solution.py:336
  123.2 11.9 %collective-permute-start.18 = (bf16[128,384]{1,0:T(8,128)(2,1)S(1)}, bf16[128,384]{1,0:T(8,128)(2,1)S(1)}, u32[]{:S(2)}, u32[]{:S(2)}) collective-permute-start(bf16[128,384]{1,0:T(8,128)(2,1)S(1)} %get-tuple-element.56), channel_id=1, source_target_pairs={{0,2},{1,3},{2,0},{3,1},{4,6},{5,7},{6,4},{7,5},{8,10},{9,11},{10,... | collective-permute-start | bytes 294920 | tf_op jit(solution)/shard_map/ppermute | solution.py:336
  125.6 9.5 %collective-permute-start.19 = (bf16[128,384]{1,0:T(8,128)(2,1)S(1)}, bf16[128,384]{1,0:T(8,128)(2,1)S(1)}, u32[]{:S(2)}, u32[]{:S(2)}) collective-permute-start(bf16[128,384]{1,0:T(8,128)(2,1)S(1)} %get-tuple-element.57), channel_id=1, source_target_pairs={{0,3},{1,0},{2,1},{3,2},{4,7},{5,4},{6,5},{7,6},{8,11},{9,8},{10,9... | collective-permute-start | bytes 294920 | tf_op jit(solution)/shard_map/ppermute | solution.py:336
  131.2 9.8 %collective-permute-start.16 = (f32[24,384]{1,0:T(8,128)S(1)}, f32[24,384]{1,0:T(8,128)S(1)}, u32[]{:S(2)}, u32[]{:S(2)}) collective-permute-start(f32[24,384]{1,0:T(8,128)S(1)} %convert_reduce_fusion), channel_id=1, source_target_pairs={{0,0},{1,64},{2,128},{3,192},{64,1},{65,65},{66,129},{67,193},{128... | collective-permute-start | bytes 110600 | tf_op jit(solution)/shard_map/ppermute | solution.py:345
